TPU v7x, 128 devices: a whole 4x4x4 slice. The times are simulated.
128 devices in a mesh: frame: 8 (over z, y_hi), spatial: 4 (over x), dp: 4 (over y_lo, core).
Axes of the slice: x: 4, y: 4 (y_hi: 2, y_lo: 2; y = y_hi * 2 + y_lo), z: 4, core: 2. Of those that a mesh axis runs over, the one named last changes fastest.
Arguments:
- tokens: bfloat16 [4, 8, 48, 80, 3072], P('dp', 'frame', 'spatial'), may hold values from -6 to 6
- xz_weight: bfloat16 [3072, 3072], P(('spatial', 'dp')), may hold values from -0.109375 to 0.109375
- state_weight: bfloat16 [3072, 256], P(('spatial', 'dp')), may hold values from -0.109375 to 0.109375
- step_weight: bfloat16 [3072, 24], P(('spatial', 'dp')), may hold values from -0.109375 to 0.109375
- step_bias: float32 [24], replicated, may hold values from -1 to 1
- decay_rate: float32 [2, 24], replicated, may hold values from 0 to 1, as said below
- skip: float32 [2, 24], replicated, may hold values from 0.5 to 1.5
- norm_gain: float32 [1536], replicated, may hold values from 0.5 to 1.5
Outputs:
- mixed: bfloat16 [4, 8, 48, 80, 1536], P('dp', 'frame', 'spatial')
Inputs may be any that keep to these rules, and one draw needn't show every extreme that they name: `decay_rate`: positive decay rates, one per direction and head.
All inputs are finite; a program needn't handle non-finite values.
Results may differ from a plain program's by a relative error of at most 0.0013.
Values may be sent and summed in bfloat16 or wider, within the bound.
A program may use at most 256 MiB of HBM per device.

v0:
```python
import jax
import jax.numpy as jnp
from jax import lax
from jax.sharding import PartitionSpec as P

HIGHEST = lax.Precision.HIGHEST


def prefix(x, axis, combine, identity, reverse):
    count, position = (lax.axis_size(axis), lax.axis_index(axis))
    everything = jax.tree.map(lambda part: lax.all_gather(part, axis), x)
    start = jax.tree.map(
        lambda part, zero: jnp.broadcast_to(jnp.asarray(zero, part.dtype), part.shape), x, identity
    )

    def step(k, before):
        at = count - 1 - k if reverse else k
        reached = at > position if reverse else at < position
        new = combine(before, jax.tree.map(lambda part: part[at], everything))
        return jax.tree.map(lambda a, b: jnp.where(reached, a, b), new, before)

    return lax.fori_loop(0, count, step, start)


def block_number(length):
    number = 1
    while length // number > 512 and length % (number * 2) == 0:
        number = number * 2
    return number


def block_step(memory, pieces, decay_rate, heads):
    value_rows, key_rows, query_rows, step_rows = pieces
    length = value_rows.shape[0]
    head_size = value_rows.shape[1] // heads
    running = jnp.cumsum(-step_rows * decay_rate[None, :], axis=0)
    across = running.T
    positions = jnp.arange(length)
    causal = positions[:, None] >= positions[None, :]
    between = across[:, :, None] - across[:, None, :]
    decays = jnp.exp(jnp.where(causal[None, :, :], between, -jnp.inf))
    scores = jnp.dot(query_rows, key_rows.T, precision=HIGHEST, preferred_element_type=jnp.float32)
    scaled = value_rows.reshape(length, heads, head_size) * step_rows[:, :, None]
    within = jnp.einsum("hts,shp->thp", decays * scores[None, :, :], scaled, precision=HIGHEST)
    carried = (
        jnp.einsum("tn,hpn->thp", query_rows, memory, precision=HIGHEST)
        * jnp.exp(running)[:, :, None]
    )
    final_log = running[-1]
    weighted = scaled * jnp.exp(final_log[None, :] - running)[:, :, None]
    new_memory = jnp.exp(final_log)[:, None, None] * memory + jnp.einsum(
        "shp,sn->hpn", weighted, key_rows, precision=HIGHEST
    )
    return (new_memory, (within + carried).reshape(length, -1))


def run_sequence(value_rows, key_rows, query_rows, step_rows, decay_rate, memory, heads):
    length = value_rows.shape[0]
    number = block_number(length)
    size = length // number
    pieces_out = []
    for index in range(number):
        lower = index * size
        pieces = (
            value_rows[lower : lower + size],
            key_rows[lower : lower + size],
            query_rows[lower : lower + size],
            step_rows[lower : lower + size],
        )
        memory, block_out = block_step(memory, pieces, decay_rate, heads)
        pieces_out.append(block_out)
    return (jnp.concatenate(pieces_out, axis=0), memory)


def combine_states(earlier, later):
    return (earlier[0] + later[0], jnp.exp(later[0])[..., None, None] * earlier[1] + later[1])


def local_pass(value_rows, key_rows, query_rows, step_rows, rates, heads):

    def one_video(pieces):
        video_values, video_keys, video_queries, video_steps = pieces
        head_size = video_values.shape[1] // heads
        empty_state = jnp.zeros((heads, head_size, video_keys.shape[1]), jnp.float32)
        outputs, memory = run_sequence(
            video_values, video_keys, video_queries, video_steps, rates, empty_state, heads
        )
        logs_all = -video_steps * rates[None, :]
        return (outputs, memory, jnp.sum(logs_all, axis=0), jnp.cumsum(logs_all, axis=0))

    return lax.map(one_video, (value_rows, key_rows, query_rows, step_rows))


def correction(query_rows, incoming, running):
    added = (
        jnp.einsum("vtn,vhpn->vthp", query_rows, incoming, precision=HIGHEST)
        * jnp.exp(running)[..., None]
    )
    return added.reshape(added.shape[0], added.shape[1], -1)


def local(tokens, xz_weight, state_weight, step_weight, step_bias, decay_rate, skip, norm_gain):
    videos, frame_count, row_part, col_total, width = tokens.shape
    flattened = tokens.reshape(-1, width)
    inner = xz_weight.shape[1] // 2
    state_size = state_weight.shape[1] // 2
    heads = step_weight.shape[1]
    head_size = inner // heads
    pieces = (
        lax.all_gather(xz_weight, ("spatial", "dp"), axis=0, tiled=True),
        lax.all_gather(state_weight, ("spatial", "dp"), axis=0, tiled=True),
        lax.all_gather(step_weight, ("spatial", "dp"), axis=0, tiled=True),
    )
    projected, state_rows, raw_steps = tuple(
        (jnp.dot(flattened, piece, preferred_element_type=jnp.float32) for piece in pieces)
    )
    gate_rows = projected[:, :inner]
    value_rows = projected[:, inner:]
    key_rows = state_rows[:, :state_size]
    query_rows = state_rows[:, state_size:]
    step_rows = jax.nn.softplus(raw_steps + step_bias)
    grid = (videos, frame_count, row_part, col_total)

    def per_video(source):
        return source.reshape(videos, -1, source.shape[-1])

    def reorder(source):
        turned = jnp.swapaxes(source, 2, 3)
        return turned.reshape(turned.shape[0], -1, turned.shape[-1])[:, ::-1]

    outputs, memory, totals, running = local_pass(
        per_video(value_rows),
        per_video(key_rows),
        per_video(query_rows),
        per_video(step_rows),
        decay_rate[0],
        heads,
    )
    identity = (jnp.zeros_like(totals), jnp.zeros_like(memory))
    incoming = prefix((totals, memory), ("frame", "spatial"), combine_states, identity, False)[1]
    forward_out = outputs + correction(per_video(query_rows), incoming, running)

    def shaped(source):
        return source.reshape(grid + (source.shape[-1],))

    pieces = (
        lax.all_to_all(shaped(value_rows), "spatial", split_axis=3, concat_axis=2, tiled=True),
        lax.all_to_all(shaped(key_rows), "spatial", split_axis=3, concat_axis=2, tiled=True),
        lax.all_to_all(shaped(query_rows), "spatial", split_axis=3, concat_axis=2, tiled=True),
        lax.all_to_all(shaped(step_rows), "spatial", split_axis=3, concat_axis=2, tiled=True),
    )
    ordered = tuple((reorder(piece) for piece in pieces))
    outputs, memory, totals, running = local_pass(
        ordered[0], ordered[1], ordered[2], ordered[3], decay_rate[1], heads
    )
    outputs, memory, totals, running, queries_ordered = (
        outputs,
        memory,
        totals,
        running,
        ordered[2],
    )
    identity = (jnp.zeros_like(totals), jnp.zeros_like(memory))
    incoming = prefix((totals, memory), ("frame", "spatial"), combine_states, identity, True)[1]
    result = outputs + correction(queries_ordered, incoming, running)
    column_part = col_total // lax.axis_size("spatial")
    restored = result[:, ::-1].reshape(videos, frame_count, column_part, -1, inner)
    restored = jnp.swapaxes(restored, 2, 3)
    returned = lax.all_to_all(restored, "spatial", split_axis=2, concat_axis=3, tiled=True)
    backward_out = returned.reshape(videos, -1, inner)
    value_flat = per_video(value_rows)
    forward_out = forward_out + jnp.repeat(skip[0], head_size)[None, None, :] * value_flat
    backward_out = backward_out + jnp.repeat(skip[1], head_size)[None, None, :] * value_flat
    combined = forward_out + backward_out
    gated = (combined * per_video(jax.nn.silu(gate_rows))).reshape(videos, -1, heads, head_size)
    inverse_rms = lax.rsqrt(jnp.mean(gated * gated, axis=-1, keepdims=True) + 1e-05)
    normed = (gated * inverse_rms).reshape(videos, -1, inner) * norm_gain
    return normed.astype(jnp.bfloat16).reshape(grid + (inner,))


def solution(mesh):
    in_specs = (
        P("dp", "frame", "spatial", None, None),
        P(("spatial", "dp"), None),
        P(("spatial", "dp"), None),
        P(("spatial", "dp"), None),
        P(),
        P(),
        P(),
        P(),
    )
    out_specs = P("dp", "frame", "spatial", None, None)
    return jax.shard_map(local, mesh=mesh, in_specs=in_specs, out_specs=out_specs, check_vma=False)
```

profile of v0, /device:TPU:2, one launch (start us, length us, event | category | flops | bytes accessed | tf_op | source)
XLA Modules:
  0.0 976.3 jit_solution(5417760531652360970)
XLA Ops:
  8.0 18.5 %all-gather.4 = bf16[16,192,24]{1,2,0:T(8,128)(2,1)S(1)} all-gather(bf16[1,192,24]{1,2,0:T(8,128)(2,1)} %bitcast.351), channel_id=1, replica_groups=mesh['frame'=8,'spatial'=4,'dp'=4] {'spatial','dp'}, dimensions={0}, use_global_device_ids=true | all-gather | bytes 156672 | tf_op jit(solution)/shard_map/all_gather | solution.py:112
  56.5 96.4 %all-gather.10.cloned.1.call-done = bf16[3072,3072]{1,0:T(8,128)(2,1)} async-done(((bf16[192,3072]{1,0:T(8,128)(2,1)}), bf16[3072,3072]{1,0:T(8,128)(2,1)}) %all-gather.10.cloned.1.call-update) | async-done | bytes 18874384 | tf_op jit(solution)/shard_map/all_gather | solution.py:110
  152.9 23.3 %fusion.122 = f32[960,3072]{1,0:T(8,128)S(1)} fusion(bf16[960,3072]{1,0:T(8,128)(2,1)} %bitcast.312, bf16[3072,3072]{1,0:T(8,128)(2,1)} %all-gather.10.cloned.1.call-done), kind=kOutput, calls=%fused_computation.197 | convolution fusion | flops 18119393280 | bytes 36569088 | tf_op jit(solution)/shard_map/dot_general | solution.py:115
  180.7 8.0 copy.197
  219.1 42.5 %all-to-all-done = f32[1,1,12,80,1536]{4,1,2,0,3:T(1,128)} async-done(((f32[1,1,12,80,1536]{4,1,2,0,3:T(1,128)}), f32[1,1,12,80,1536]{4,1,2,0,3:T(1,128)}, u32[]{:S(2)}, u32[]{:S(2)}) %all-to-all-start) | async-done | bytes 5898272 | tf_op jit(solution)/shard_map/all_to_all | solution.py:147
  274.1 21.0 %slice.236 = f32[1,480,1536]{2,1,0:T(8,128)S(1)} reverse(f32[1,480,1536]{2,1,0:T(8,128)} %get-tuple-element.411), dimensions={1} | reverse | bytes 5898240 | tf_op jit(solution)/shard_map/while/body/eval_jaxpr/slice | solution.py:65
  305.0 21.0 %slice.251 = f32[1,480,1536]{2,1,0:T(8,128)S(1)} reverse(f32[1,480,1536]{2,1,0:T(8,128)} %get-tuple-element.412), dimensions={1} | reverse | bytes 5898240 | tf_op jit(solution)/shard_map/while/body/eval_jaxpr/slice | solution.py:65
  332.3 14.3 %copy.226 = f32[1,480,1536]{1,2,0:T(8,128)} copy(f32[1,480,1536]{2,1,0:T(8,128)} %multiply_multiply_fusion) | data formatting | bytes 5898240 | tf_op jit(solution)/shard_map/while/body/eval_jaxpr/mul | solution.py:50
  385.4 6.8 reduce-window.46
  398.6 93.0 %all-reduce.8 = (f32[768]{0:T(1024)S(1)}, f32[768]{0:T(1024)S(1)}) all-reduce(f32[768]{0:T(1024)S(1)} %dynamic-update-slice, f32[768]{0:T(1024)S(1)} %dynamic-update-slice.1), channel_id=2, replica_groups=mesh['frame'=8,'spatial'=4,'dp'=4] {'frame','spatial'}, use_global_device_ids=true, to_apply=%add.6 | all-reduce | flops 1536 | bytes 12288
  493.0 6.7 reduce-window.56
  502.5 10.0 %all-to-all-start.2 = ((f32[1,1,12,80,128]{4,1,2,0,3:T(1,128)}), f32[1,1,12,80,128]{4,1,2,0,3:T(1,128)S(1)}, u32[]{:S(2)}, u32[]{:S(2)}) async-start(f32[1,1,12,80,128]{4,1,2,0,3:T(1,128)} %copy.208), calls=%async_computation.2 | async-start | bytes 983040 | tf_op jit(solution)/shard_map/all_to_all | solution.py:149
  531.4 27.7 %fusion.17 = f32[24,64,480]{2,1,0:T(8,128)S(1)} fusion(f32[480,480]{1,0:T(8,128)} %fusion.95, f32[24,480]{1,0:T(8,128)} %get-tuple-element.429, pred[480,480]{1,0:T(8,128)(4,1)} %iota_compare_fusion, f32[480,24,64]{0,2,1:T(8,128)} %bitcast.299, f32[480,24]{0,1:T(8,128)} %get-tuple-element.421), kind=kOutput, calls=%fused_computation.21 | convolution fusion | flops 4264058880 | bytes 7142400 | tf_op jit(solution)/shard_map/while/body/eval_jaxpr/hts,shp->thp/dot_general | solution.py:44
  567.0 27.9 %fusion.12 = f32[24,64,480]{2,1,0:T(8,128)S(1)} fusion(f32[480,480]{1,0:T(8,128)} %fusion.90, f32[24,480]{1,0:T(8,128)} %get-tuple-element.432, pred[480,480]{1,0:T(8,128)(4,1)S(1)} %copy-done.17, f32[480,24,64]{0,2,1:T(8,128)} %bitcast.308, f32[480,24]{0,1:T(8,128)S(1)} %get-tuple-element.422), kind=kOutput, calls=%fused_computation.16 | convolution fusion | flops 4264058880 | bytes 7142400 | tf_op jit(solution)/shard_map/while/body/eval_jaxpr/hts,shp->thp/dot_general | solution.py:44
  610.4 27.7 %fusion.7 = f32[24,64,480]{2,1,0:T(8,128)S(1)} fusion(f32[480,480]{1,0:T(8,128)} %fusion.82, f32[24,480]{1,0:T(8,128)} %get-tuple-element.435, pred[480,480]{1,0:T(8,128)(4,1)S(1)} %copy-done.17, f32[480,24,64]{0,2,1:T(8,128)} %bitcast.316, f32[480,24]{0,1:T(8,128)S(1)} %bitcast.346), kind=kOutput, calls=%fused_computation.11 | convolution fusion | flops 4264058880 | bytes 7142400 | tf_op jit(solution)/shard_map/while/body/eval_jaxpr/hts,shp->thp/dot_general | solution.py:44
  646.2 27.6 %fusion.2 = f32[24,64,480]{2,1,0:T(8,128)S(1)} fusion(f32[480,480]{1,0:T(8,128)} %fusion.78, f32[24,480]{1,0:T(8,128)S(1)} %copy-done.26, pred[480,480]{1,0:T(8,128)(4,1)S(1)} %copy-done.17, f32[480,24,64]{0,2,1:T(8,128)} %bitcast.315, f32[480,24]{0,1:T(8,128)S(1)} %bitcast.344), kind=kOutput, calls=%fused_computation.6 | convolution fusion | flops 4264058880 | bytes 7142400 | tf_op jit(solution)/shard_map/while/body/eval_jaxpr/hts,shp->thp/dot_general | solution.py:44
  681.9 63.4 %while.21 = (s32[]{:T(128)}, f32[1,24,64,128]{3,2,1,0:T(8,128)S(1)}, s32[]{:T(128)}, f32[32,1,24]{2,1,0:T(1,128)}, f32[32,1,24,64,128]{4,3,2,1,0:T(8,128)}, /*index=5*/s32[]{:T(128)}, s32[]{:T(128)}, s32[]{:T(128)}, s32[]{:T(128)}) while((s32[]{:T(128)}, f32[1,24,64,128]{3,2,1,0:T(8,128)S(1)}, s32[]{:T(128)}, ...), condition=%wide.region_15.16_spmd.clone, body=%wide.region_14.15_spmd.clone.sunk | while | flops 786440 | bytes 2359759 | solution.py:22
  745.2 6.9 broadcast_multiply_fusion
  752.2 6.6 copy.231
  758.8 8.2 maximum_add_fusion.1
  767.0 48.0 %rev.13 = f32[1,960,1536]{2,1,0:T(8,128)} reverse(f32[1,960,1536]{2,1,0:T(8,128)} %maximum_add_fusion.1), dimensions={1} | reverse | bytes 11796480 | tf_op jit(solution)/shard_map/rev | solution.py:167
  815.0 8.1 copy.232
  823.1 7.0 all-to-all-start.4
  830.1 63.1 %while.20 = (s32[]{:T(128)}, f32[1,24,64,128]{3,2,1,0:T(8,128)S(1)}, s32[]{:T(128)}, f32[32,1,24]{2,1,0:T(1,128)}, f32[32,1,24,64,128]{4,3,2,1,0:T(8,128)}, /*index=5*/s32[]{:T(128)}, s32[]{:T(128)}) while((s32[]{:T(128)}, f32[1,24,64,128]{3,2,1,0:T(8,128)S(1)}, s32[]{:T(128)}, f32[32,1,24]{2,1,0:T(1,128)}, ...), condition=%wide.region_6.7_spmd.clone, body=%wide.region_5.6_spmd.clone.sunk | while | flops 786436 | bytes 2359697 | solution.py:22
  893.2 6.9 broadcast_multiply_fusion.1
  900.1 6.5 copy.196
  906.6 6.5 copy.233
  913.1 7.2 reshape.461
  920.3 14.8 %fusion.114 = (f32[960,1536]{1,0:T(8,128)}, f32[960,1536]{1,0:T(8,128)}) fusion(f32[960,3072]{1,0:T(8,128)} %copy-done, f32[960,1536]{1,0:T(8,128)} %reshape.461, f32[1536]{0:T(1024)S(1)} %mul.557, f32[1536]{0:T(1024)S(1)} %mul.516, f32[960,1536]{1,0:T(8,128)} %copy.196, f32[480,1536]{1,0:T(8,128)} %copy.191, f32[480,1536]{1,0:T(8,128)S(1)} %copy-done.8), kind=kLoop, calls=%fused_computation.190 | loop fusion | flops 19169280 | bytes 41299968 | tf_op jit(solution)/shard_map/mul | solution.py:176
  935.1 6.5 copy.234
  951.8 10.0 %mul.566 = f32[1,1,12,80,1536]{4,3,2,1,0:T(8,128)} reshape(f32[960,24,64]{2,1,0:T(8,128)} %mul.565) | data formatting | bytes 11796480 | tf_op jit(solution)/shard_map/mul | solution.py:177
  961.8 7.5 multiply_convert_fusion
  (364 shorter events, 336.1 us)
Async XLA Ops:
  6.5 37.7 %all-gather.12.cloned.1.call-start = ((), (), s32[]{:S(2)}) async-start(), calls=%async_computation.6 | async-start | bytes 1671168 | tf_op jit(solution)/shard_map/all_gather | solution.py:111
  7.3 145.6 %all-gather.10.cloned.1.call-start = ((), (), s32[]{:S(2)}) async-start(), calls=%async_computation.5 | async-start | bytes 20054016 | tf_op jit(solution)/shard_map/all_gather | solution.py:110
  27.5 172.0 %copy-start.29 = (f32[24]{0:T(128)}, f32[24]{0:T(128)S(1)}, u32[]{:S(2)}) copy-start(f32[24]{0:T(128)S(1)} %get-tuple-element.442) | copy-start | bytes 292
  27.5 328.4 %copy-start.27 = (f32[24]{0:T(128)}, f32[24]{0:T(128)S(1)}, u32[]{:S(2)}) copy-start(f32[24]{0:T(128)S(1)} %get-tuple-element.441) | copy-start | bytes 292
  37.2 15.0 %all-to-all-start.1 = ((f32[4,1,5760]{2,1,0:T(1,128)}), f32[4,1,5760]{2,1,0:T(1,128)S(1)}, u32[]{:S(2)}, u32[]{:S(2)}) async-start(f32[4,1,5760]{2,1,0:T(1,128)} %reshape.496), calls=%async_computation.1 | async-start | bytes 184320 | tf_op jit(solution)/shard_map/all_to_all | solution.py:150
  52.2 136.4 %all-to-all-start.3 = ((f32[1,1,12,80,128]{4,1,2,0,3:T(1,128)}), f32[1,1,12,80,128]{4,1,2,0,3:T(1,128)S(1)}, u32[]{:S(2)}, u32[]{:S(2)}) async-start(f32[1,1,12,80,128]{4,1,2,0,3:T(1,128)} %copy.212), calls=%async_computation.3 | async-start | bytes 983040 | tf_op jit(solution)/shard_map/all_to_all | solution.py:148
  189.4 72.1 %all-to-all-start = ((f32[1,1,12,80,1536]{4,1,2,0,3:T(1,128)}), f32[1,1,12,80,1536]{4,1,2,0,3:T(1,128)}, u32[]{:S(2)}, u32[]{:S(2)}) async-start(f32[1,1,12,80,1536]{4,1,2,0,3:T(1,128)} %copy.197), calls=%async_computation | async-start | bytes 11796480 | tf_op jit(solution)/shard_map/all_to_all | solution.py:147
  195.1 486.7 %all-gather.16.cloned.1.call-start = ((), (), s32[]{:S(2)}) async-start(), calls=%async_computation.8 | async-start | bytes 25952256 | tf_op jit(solution)/shard_map/all_gather | solution.py:11
  200.3 12.8 %copy-start.22 = (f32[1,480,24]{1,2,0:T(8,128)}, f32[1,480,24]{1,2,0:T(8,128)S(1)}, u32[]{:S(2)}) copy-start(f32[1,480,24]{1,2,0:T(8,128)S(1)} %get-tuple-element.444) | copy-start | bytes 138244
  295.2 9.8 %copy-start.1 = (f32[1,480,1536]{2,1,0:T(8,128)}, f32[1,480,1536]{2,1,0:T(8,128)S(1)}, u32[]{:S(2)}) copy-start(f32[1,480,1536]{2,1,0:T(8,128)S(1)} %slice.236) | copy-start | bytes 8847364
  326.0 20.6 %copy-start.2 = (f32[1,480,1536]{2,1,0:T(8,128)}, f32[1,480,1536]{2,1,0:T(8,128)S(1)}, u32[]{:S(2)}) copy-start(f32[1,480,1536]{2,1,0:T(8,128)S(1)} %slice.251) | copy-start | bytes 8847364
  346.6 5.7 copy-start.4
  346.6 9.3 copy-start.16
  355.9 474.2 %all-gather.14.cloned.1.call-start = ((), (), s32[]{:S(2)}) async-start(), calls=%async_computation.7 | async-start | bytes 25952256 | tf_op jit(solution)/shard_map/all_gather | solution.py:11
  369.7 14.3 %copy-start.3 = (f32[480,1536]{0,1:T(8,128)}, f32[480,1536]{0,1:T(8,128)S(1)}, u32[]{:S(2)}) copy-start(f32[480,1536]{0,1:T(8,128)S(1)} %copy.183) | copy-start | bytes 8847364
  374.4 4.9 copy-start.5
  374.4 9.7 copy-start.30
  384.0 128.5 %copy-start.7 = (f32[960,256]{1,0:T(8,128)S(1)}, f32[960,256]{1,0:T(8,128)}, u32[]{:S(2)}) copy-start(f32[960,256]{1,0:T(8,128)} %copy-done.6) | copy-start | bytes 2949124
  502.5 16.5 %all-to-all-start.2 = ((f32[1,1,12,80,128]{4,1,2,0,3:T(1,128)}), f32[1,1,12,80,128]{4,1,2,0,3:T(1,128)S(1)}, u32[]{:S(2)}, u32[]{:S(2)}) async-start(f32[1,1,12,80,128]{4,1,2,0,3:T(1,128)} %copy.208), calls=%async_computation.2 | async-start | bytes 983040 | tf_op jit(solution)/shard_map/all_to_all | solution.py:149
  531.4 27.7 %copy-start.21 = (f32[480,24]{0,1:T(8,128)S(1)}, f32[480,24]{0,1:T(8,128)}, u32[]{:S(2)}) copy-start(f32[480,24]{0,1:T(8,128)} %get-tuple-element.427) | copy-start | bytes 138244
  559.1 7.9 copy-start.17
  567.0 27.9 %copy-start.12 = (f32[24,64,128]{2,1,0:T(8,128)S(1)}, f32[24,64,128]{2,1,0:T(8,128)}, u32[]{:S(2)}) copy-start(f32[24,64,128]{2,1,0:T(8,128)} %copy-done.11) | copy-start | bytes 2359300
  567.0 27.9 %copy-start.20 = (f32[480,24]{0,1:T(8,128)S(1)}, f32[480,24]{0,1:T(8,128)}, u32[]{:S(2)}) copy-start(f32[480,24]{0,1:T(8,128)} %get-tuple-element.430) | copy-start | bytes 138244
  603.0 7.5 copy-start.25
  610.4 27.7 %copy-start.19 = (f32[480,24]{0,1:T(8,128)S(1)}, f32[480,24]{0,1:T(8,128)}, u32[]{:S(2)}) copy-start(f32[480,24]{0,1:T(8,128)} %get-tuple-element.433) | copy-start | bytes 138244
  638.2 8.0 copy-start.23
  646.2 27.7 %copy-start.10 = (f32[24,64,128]{2,1,0:T(8,128)S(1)}, f32[24,64,128]{2,1,0:T(8,128)}, u32[]{:S(2)}) copy-start(f32[24,64,128]{2,1,0:T(8,128)} %copy-done.9) | copy-start | bytes 2359300
  646.2 27.7 %copy-start.18 = (f32[480,24]{0,1:T(8,128)S(1)}, f32[480,24]{0,1:T(8,128)}, u32[]{:S(2)}) copy-start(f32[480,24]{0,1:T(8,128)} %get-tuple-element.436) | copy-start | bytes 138244
  681.9 63.4 %copy-start.13 = (f32[1,960,128]{2,1,0:T(8,128)S(1)}, f32[1,960,128]{2,1,0:T(8,128)}, u32[]{:S(2)}) copy-start(f32[1,960,128]{2,1,0:T(8,128)} %rev.11) | copy-start | bytes 1474564
  823.1 83.5 %all-to-all-start.4 = ((f32[1,1,48,20,1536]{4,1,3,0,2:T(1,128)}), f32[1,1,48,20,1536]{4,1,3,0,2:T(1,128)}, u32[]{:S(2)}, u32[]{:S(2)}) async-start(f32[1,1,48,20,1536]{4,1,3,0,2:T(1,128)} %copy.232), calls=%async_computation.4 | async-start | bytes 11796480 | tf_op jit(solution)/shard_map/all_to_all | solution.py:169
  913.1 7.2 copy-start.8
  951.8 10.0 %copy-start.28 = (f32[1536]{0:T(1024)S(1)}, f32[1536]{0:T(1024)}, u32[]{:S(2)}) copy-start(f32[1536]{0:T(1024)} %param.19) | copy-start | bytes 18436
  (8 other events, 15.8 us)
Sparse Core Ops, SparseCore 0:
  9.1 35.1 all-gather.11
  46.0 106.9 all-gather.9
  356.0 208.7 all-gather.15
  567.7 205.9 all-gather.13
where the time goes:
time: 996 us; the launch traced here: 976 us
  local copies, waits for them, and re-layouts  309 us (31%)
  matrix products  202 us (20%)
  other arithmetic  159 us (16%)
  waiting for transfers between devices  144 us (14%)
  blocking collectives  112 us (11%)
  starting transfers between devices  33.3 us (3%)
  between operations  15.1 us (2%)
    dot_general x4, matrix products, block_step(): jnp.einsum('hts,shp->thp', decays * scores[None, :, :], scaled, precision...  111 us
    all_gather x1, waiting for transfers between devices, local(): lax.all_gather(xz_weight, ('spatial', 'dp'), axis=0, tiled=True)  96.4 us
    unnamed x1, blocking collectives  93 us
    select_n x64, other arithmetic, step(): return jax.tree.map(lambda a, b: jnp.where(reached, a, b), new, before)  83.5 us
    slice x8, local copies, waits for them, and re-layouts, run_sequence(): value_rows[lower:lower + size]  65.5 us
    rev x1, local copies, waits for them, and re-layouts, local(): result[:, ::-1].reshape(videos, frame_count, column_part, -1, inner)  48 us
    all_to_all x1, waiting for transfers between devices, local(): lax.all_to_all(shaped(value_rows), 'spatial', split_axis=3, concat_axis=2...  42.5 us
    exp x64, local copies, waits for them, and re-layouts, combine_states(): jnp.exp(later[0])[..., None, None] * earlier[1] + later[1]  41.1 us
  transfers between devices with their start and end apart: 9, of which 4 were waited for; matrix products, arithmetic and copies ran while one was open for 52% of the time, Pallas kernels for 0%

commit v1 on v0

v1 whole, which is shorter than its diff:
```python
import functools

import jax
import jax.numpy as jnp
from jax import lax
from jax.experimental import pallas as pl
from jax.experimental.pallas import tpu as pltpu
from jax.sharding import PartitionSpec as P

F32 = jnp.float32
BF16 = jnp.bfloat16
LANES = 128
GROUP = 4
VMEM_BYTES = 56 * 1024 * 1024


def split(value):
    high = value.astype(BF16)
    return high, (value - high.astype(F32)).astype(BF16)


def dot(a, b):
    return lax.dot_general(a, b, (((1,), (0,)), ((), ())), preferred_element_type=F32)


def rows_iota(shape):
    return lax.broadcasted_iota(jnp.int32, shape, 0)


def lanes_iota(shape):
    return lax.broadcasted_iota(jnp.int32, shape, 1)


def spread(columns, pair, head_size):
    first, second = columns[:, 2 * pair : 2 * pair + 1], columns[:, 2 * pair + 1 : 2 * pair + 2]
    shape = (columns.shape[0], LANES)
    return jnp.where(lanes_iota(shape) < head_size, first, second)


def params(semantics=("arbitrary",)):
    return pltpu.CompilerParams(vmem_limit_bytes=VMEM_BYTES, dimension_semantics=semantics)


def regroup_kernel(inner, state_columns, source_ref, bias_ref, mid_ref, steps_ref):
    step_lanes = pl.ds(inner + state_columns, LANES)
    raw = source_ref[:, step_lanes] + bias_ref[...]
    steps = jnp.maximum(raw, 0.0) + jnp.log1p(jnp.exp(-jnp.abs(raw)))
    steps_ref[...] = steps
    col_total = source_ref.shape[0] // 2
    wide = inner + state_columns

    def move(lower, upper, at, lanes):
        low = rows_iota(lower.shape) < GROUP
        mid_ref[2 * at, :, lanes] = jnp.where(low, lower, pltpu.roll(upper, GROUP, 0))
        mid_ref[2 * at + 1, :, lanes] = jnp.where(low, pltpu.roll(lower, GROUP, 0), upper)

    for at in range(col_total // 8):
        lower, upper = pl.ds(8 * at, 8), pl.ds(col_total + 8 * at, 8)
        move(source_ref[lower, :wide], source_ref[upper, :wide], at, pl.ds(0, wide))
        move(
            steps[8 * at : 8 * at + 8],
            steps[col_total + 8 * at : col_total + 8 * at + 8],
            at,
            step_lanes,
        )


def regroup(projected, bias, row_part, col_total, inner, state_columns):
    width = projected.shape[1]
    tokens = row_part * col_total
    groups = col_total // GROUP
    block = 2 * col_total
    return pl.pallas_call(
        functools.partial(regroup_kernel, inner, state_columns),
        grid=(row_part // 2,),
        in_specs=[
            pl.BlockSpec((block, width), lambda m: (m, 0)),
            pl.BlockSpec((1, LANES), lambda m: (0, 0)),
        ],
        out_specs=[
            pl.BlockSpec((groups, 2 * GROUP, width), lambda m: (0, m, 0)),
            pl.BlockSpec((block, LANES), lambda m: (m, 0)),
        ],
        out_shape=[
            jax.ShapeDtypeStruct((groups, row_part * GROUP, width), F32),
            jax.ShapeDtypeStruct((tokens, LANES), F32),
        ],
        compiler_params=params(),
    )(projected, bias)


def earlier_mask(size, column_rows):
    shape = (size, size)
    t, s = rows_iota(shape), lanes_iota(shape)
    if column_rows:

        def place(index):
            return size - 1 - (lax.rem(index, GROUP) * column_rows + index // GROUP)

        t, s = place(t), place(s)
    return s <= t


def running_logs(steps, rate, earlier):
    logs = -steps * rate
    high, rest = split(logs)
    middle = logs - high.astype(F32)
    middle, low = split(middle)
    before = jnp.where(earlier, 1.0, 0.0).astype(BF16)
    running = dot(before, high) + dot(before, middle) + dot(before, low)
    return running, jnp.sum(logs, axis=0, keepdims=True)


def advance(memory, keys_t, weighted, decay):
    keys_high, keys_low = keys_t
    high, low = split(weighted)
    both = dot(keys_high, jnp.concatenate([high, low], axis=1))
    added = both[:, :LANES] + both[:, LANES:] + dot(keys_low, high)
    return memory * decay + added


def state_kernel(
    column_rows, head_size, values_ref, keys_ref, steps_ref, rate_ref, memory_ref, decay_ref
):
    size = values_ref.shape[0] * values_ref.shape[1]
    pairs = values_ref.shape[2] // LANES

    @pl.when(pl.program_id(0) == 0)
    def _():
        memory_ref[...] = jnp.zeros_like(memory_ref)
        decay_ref[...] = jnp.ones_like(decay_ref)

    steps = steps_ref[...].reshape(size, LANES)
    keys_t = split(jnp.transpose(keys_ref[...].reshape(size, LANES)))
    running, total = running_logs(steps, rate_ref[...], earlier_mask(size, column_rows))
    coefficient = steps * jnp.exp(jnp.minimum(total - running, 0.0))
    decay = jnp.exp(total)
    for pair in range(pairs):
        lanes = pl.ds(pair * LANES, LANES)
        weighted = values_ref[:, :, lanes].reshape(size, LANES) * spread(coefficient, pair, head_size)
        pair_decay = spread(decay, pair, head_size)
        memory_ref[:, lanes] = advance(memory_ref[:, lanes], keys_t, weighted, pair_decay)
        decay_ref[pl.ds(pair, 1), :] = decay_ref[pl.ds(pair, 1), :] * pair_decay


def output_kernel(
    column_rows,
    head_size,
    values_ref,
    keys_ref,
    queries_ref,
    steps_ref,
    rate_ref,
    skip_ref,
    entering_ref,
    out_ref,
    memory_ref,
):
    size = values_ref.shape[0] * values_ref.shape[1]
    pairs = values_ref.shape[2] // LANES

    @pl.when(pl.program_id(0) == 0)
    def _():
        memory_ref[...] = entering_ref[...]

    steps = steps_ref[...].reshape(size, LANES)
    keys = keys_ref[...].reshape(size, LANES)
    keys_t = split(jnp.transpose(keys))
    queries_high, queries_low = split(queries_ref[...].reshape(size, LANES))
    earlier = earlier_mask(size, column_rows)
    running, total = running_logs(steps, rate_ref[...], earlier)
    across = jnp.transpose(running)
    scores = dot(queries_high, keys_t[0]) + dot(queries_high, keys_t[1]) + dot(queries_low, keys_t[0])
    scores = jnp.where(earlier, scores, 0.0)
    arrived = jnp.exp(running)
    leaving = jnp.exp(jnp.minimum(total - running, 0.0))
    decay = jnp.exp(total)
    first_half = lanes_iota((size, LANES)) < head_size
    for pair in range(pairs):
        lanes = pl.ds(pair * LANES, LANES)
        values = values_ref[:, :, lanes].reshape(size, LANES)
        scaled = values * spread(steps, pair, head_size)
        high, low = split(scaled)
        both = jnp.concatenate([high, low], axis=1)
        halves = []
        for head in (2 * pair, 2 * pair + 1):
            between = jnp.minimum(running[:, head : head + 1] - across[head : head + 1, :], 0.0)
            kernel_high, kernel_low = split(jnp.exp(between) * scores)
            part = dot(kernel_high, both)
            halves.append(part[:, :LANES] + part[:, LANES:] + dot(kernel_low, high))
        memory = memory_ref[:, lanes]
        memory_high, memory_low = split(memory)
        part = dot(queries_high, jnp.concatenate([memory_high, memory_low], axis=1))
        carried = part[:, :LANES] + part[:, LANES:] + dot(queries_low, memory_high)
        result = jnp.where(first_half, halves[0], halves[1])
        result = result + carried * spread(arrived, pair, head_size)
        if skip_ref is not None:
            result = result + values * skip_ref[:, lanes]
        out_ref[:, :, lanes] = result.reshape(out_ref.shape[0], out_ref.shape[1], LANES)
        weighted = scaled * spread(leaving, pair, head_size)
        memory_ref[:, lanes] = advance(memory, keys_t, weighted, spread(decay, pair, head_size))


def plain_output_kernel(column_rows, head_size, values_ref, keys_ref, queries_ref, steps_ref, rate_ref, *rest):
    output_kernel(
        column_rows, head_size, values_ref, keys_ref, queries_ref, steps_ref, rate_ref, None, *rest
    )


def chunk_specs(source, steps, inner, size, backward):
    pieces, length = source.shape[0], source.shape[1]
    part = size // pieces
    count = length // part

    def spec(lane_count, lane_block):
        def index(j):
            return (0, count - 1 - j if backward else j, lane_block)

        return pl.BlockSpec((pieces, part, lane_count), index)

    first = inner // LANES
    step_spec = spec(LANES, first + 2 if steps is None else 0)
    return count, spec(inner, 0), spec(LANES, first), spec(LANES, first + 1), step_spec


def whole(shape):
    return pl.BlockSpec(shape, lambda j: (0,) * len(shape))


def local_state(source, steps, rate, inner, size, column_rows, head_size):
    count, values, keys, _, step_spec = chunk_specs(source, steps, inner, size, column_rows > 0)
    pad = 16
    return pl.pallas_call(
        functools.partial(state_kernel, column_rows, head_size),
        grid=(count,),
        in_specs=[values, keys, step_spec, whole((1, LANES))],
        out_specs=[whole((LANES, inner)), whole((pad, LANES))],
        out_shape=[
            jax.ShapeDtypeStruct((LANES, inner), F32),
            jax.ShapeDtypeStruct((pad, LANES), F32),
        ],
        compiler_params=params(),
    )(source, source, source if steps is None else steps, rate)


def local_output(source, steps, rate, skip, entering, inner, size, column_rows, head_size):
    count, values, keys, queries, step_spec = chunk_specs(
        source, steps, inner, size, column_rows > 0
    )
    body = plain_output_kernel if skip is None else output_kernel
    skip_specs = [] if skip is None else [whole((1, inner))]
    skip_args = [] if skip is None else [skip]
    return pl.pallas_call(
        functools.partial(body, column_rows, head_size),
        grid=(count,),
        in_specs=[values, keys, queries, step_spec, whole((1, LANES))]
        + skip_specs
        + [whole((LANES, inner))],
        out_specs=values,
        out_shape=jax.ShapeDtypeStruct(source.shape[:2] + (inner,), F32),
        scratch_shapes=[pltpu.VMEM((LANES, inner), F32)],
        compiler_params=params(),
    )(source, source, source, source if steps is None else steps, rate, *skip_args, entering)


def prefix_kernel(reverse, rows, pairs, source_ref, out_ref):
    count = source_ref.shape[0]
    entering = jnp.zeros((rows, LANES), F32)
    for k in range(count):
        at = count - 1 - k if reverse else k
        out_ref[at] = entering
        decay = source_ref[at, pl.ds(rows, pairs), :]
        decay = jnp.concatenate([decay] * (rows // pairs), axis=0)
        entering = entering * decay + source_ref[at, pl.ds(0, rows), :]


def entering_state(memory, decay, axes, reverse):
    count = 1
    for axis in axes:
        count = count * lax.axis_size(axis)
    pairs = memory.shape[1] // LANES
    rows = memory.shape[0] * pairs // count
    sent = jnp.concatenate(
        [
            memory.reshape(count, rows, LANES),
            jnp.broadcast_to(decay[None], (count,) + decay.shape),
        ],
        axis=1,
    )
    received = lax.all_to_all(sent, axes, 0, 0, tiled=True)
    found = pl.pallas_call(
        functools.partial(prefix_kernel, reverse, rows, pairs),
        out_shape=jax.ShapeDtypeStruct((count, rows, LANES), F32),
        compiler_params=pltpu.CompilerParams(vmem_limit_bytes=VMEM_BYTES),
    )(received)
    returned = lax.all_to_all(found, axes, 0, 0, tiled=True)
    return returned.reshape(memory.shape)


def finish_kernel(head_size, forward_ref, backward_ref, gate_ref, gain_ref, out_ref, moved_ref):
    col_total = forward_ref.shape[0] // 2
    for at in range(col_total // 8):
        even, odd = backward_ref[2 * at], backward_ref[2 * at + 1]
        low = rows_iota(even.shape) < GROUP
        moved_ref[pl.ds(8 * at, 8), :] = jnp.where(low, even, pltpu.roll(odd, GROUP, 0))
        moved_ref[pl.ds(col_total + 8 * at, 8), :] = jnp.where(low, pltpu.roll(even, GROUP, 0), odd)
    wide = 2 * LANES
    same = rows_iota((wide, wide)) // head_size == lanes_iota((wide, wide)) // head_size
    ones = jnp.where(same, 1.0, 0.0).astype(BF16)
    for block in range(forward_ref.shape[1] // wide):
        lanes = pl.ds(block * wide, wide)
        gate = gate_ref[:, lanes]
        combined = forward_ref[:, lanes] + moved_ref[:, lanes]
        gated = combined * (gate / (1.0 + jnp.exp(-gate)))
        high, low = split(gated * gated)
        mean = (dot(high, ones) + dot(low, ones)) * (1.0 / head_size)
        normed = gated * lax.rsqrt(mean + 1e-5) * gain_ref[:, lanes]
        out_ref[:, lanes] = normed.astype(out_ref.dtype)


def finish(forward, backward, gate, gain, row_part, col_total, head_size):
    tokens, inner = forward.shape
    groups = col_total // GROUP
    block = 2 * col_total
    flat = pl.BlockSpec((block, inner), lambda m: (m, 0))
    return pl.pallas_call(
        functools.partial(finish_kernel, head_size),
        grid=(row_part // 2,),
        in_specs=[
            flat,
            pl.BlockSpec((groups, 2 * GROUP, inner), lambda m: (0, m, 0)),
            flat,
            pl.BlockSpec((1, inner), lambda m: (0, 0)),
        ],
        out_specs=flat,
        out_shape=jax.ShapeDtypeStruct((tokens, inner), BF16),
        scratch_shapes=[pltpu.VMEM((block, inner), F32)],
        compiler_params=params(),
    )(forward, backward, gate, gain)


def pad_lanes(source):
    return jnp.pad(source, ((0, 0), (0, LANES - source.shape[1])))


def local(tokens, xz_weight, state_weight, step_weight, step_bias, decay_rate, skip, norm_gain):
    videos, frame_count, row_part, col_total, width = tokens.shape
    flattened = tokens.reshape(-1, width)
    inner = xz_weight.shape[1] // 2
    state_columns = state_weight.shape[1]
    heads = step_weight.shape[1]
    head_size = inner // heads
    spatial = lax.axis_size("spatial")
    column_rows = row_part * spatial
    size = column_rows * GROUP

    first_part = jnp.concatenate([xz_weight[:, inner:], state_weight, pad_lanes(step_weight)], axis=1)
    first_weight = lax.all_gather(first_part, ("spatial", "dp"), axis=0, tiled=True)
    gate_weight = lax.all_gather(xz_weight[:, :inner], ("spatial", "dp"), axis=0, tiled=True)
    projected = jnp.dot(flattened, first_weight, preferred_element_type=F32)
    gate_rows = jnp.dot(flattened, gate_weight, preferred_element_type=F32)
    rates = pad_lanes(decay_rate)
    skips = jnp.repeat(skip[0] + skip[1], head_size)[None]

    mid, steps = regroup(
        projected, pad_lanes(step_bias[None]), row_part, col_total, inner, state_columns
    )
    full = projected.shape[1]
    columns = lax.all_to_all(
        mid.reshape(spatial, -1, full), "spatial", 0, 0, tiled=True
    )
    source = projected[None]
    steps = steps[None]
    axes = ("frame", "spatial")

    memory, decay = local_state(source, steps, rates[0:1], inner, size, 0, head_size)
    entering = entering_state(memory, decay, axes, False)
    forward = local_output(source, steps, rates[0:1], skips, entering, inner, size, 0, head_size)

    memory, decay = local_state(columns, None, rates[1:2], inner, size, column_rows, head_size)
    entering = entering_state(memory, decay, axes, True)
    backward = local_output(
        columns, None, rates[1:2], None, entering, inner, size, column_rows, head_size
    )
    returned = lax.all_to_all(backward, "spatial", 0, 0, tiled=True)
    returned = returned.reshape(col_total // GROUP, row_part * GROUP, inner)
    normed = finish(
        forward[0], returned, gate_rows, norm_gain[None], row_part, col_total, head_size
    )
    return normed.reshape(videos, frame_count, row_part, col_total, inner)


def solution(mesh):
    in_specs = (
        P("dp", "frame", "spatial", None, None),
        P(("spatial", "dp"), None),
        P(("spatial", "dp"), None),
        P(("spatial", "dp"), None),
        P(),
        P(),
        P(),
        P(),
    )
    out_specs = P("dp", "frame", "spatial", None, None)
    return jax.shard_map(local, mesh=mesh, in_specs=in_specs, out_specs=out_specs, check_vma=False)
```

time: 996 us -> 417 us (0.42); the launches traced: 976 us -> 414 us
  local copies, waits for them, and re-layouts: 309 us -> 11.9 us
  matrix products: 202 us -> 34.1 us
  other arithmetic: 159 us -> 4.16 us
  blocking collectives: 112 us -> 0 us
  waiting for transfers between devices: 144 us -> 229 us
  Pallas kernels: 0 us -> 83.3 us
    dot_general x21 -> x2, matrix products: 202 us -> 34.1 us  [the longest x1 18.9 us: local(): projected = jnp.dot(flattened, first_weight, preferred_element_type=F32)]
    all_to_all x5 -> x6, waiting for transfers between devices: 45.2 us -> 160 us  [the longest x1 104 us: local(): lax.all_to_all(mid.reshape(spatial, -1, full), 'spatial', 0, 0, tiled=True)]
    unnamed x1 -> x0, blocking collectives: 93 us -> none
    select_n x64 -> x0, other arithmetic: 83.5 us -> none  [step(): return jax.tree.map(lambda a, b: jnp.where(reached, a, b), new, before)]
    pallas_call x0 -> x8, Pallas kernels: none -> 83.3 us  [the longest x2 42.5 us: local_output(): pl.pallas_call(functools.partial(body, column_rows, head_size), grid=(cou...]
    slice x21 -> x2, local copies, waits for them, and re-layouts: 74.1 us -> 2.71 us  [the longest x1 2.13 us: local(): xz_weight[:, :inner]]
    mul x16 -> x0, local copies, waits for them, and re-layouts: 52.3 us -> none  [the longest x6 23.2 us: block_step(): weighted = scaled * jnp.exp(final_log[None, :] - running)[:, :, None]]
    rev x2 -> x0, local copies, waits for them, and re-layouts: 50.6 us -> none  [the longest x1 48 us: local(): result[:, ::-1].reshape(videos, frame_count, column_part, -1, inner)]
  transfers between devices with their start and end apart: 9 -> 8, of which waited for: 4 -> 6; matrix products, arithmetic and copies ran while one was open for 52% -> 11% of each run, Pallas kernels for 0% -> 18%
where the time goes in v1:
time: 417 us; the launch traced here: 414 us
  waiting for transfers between devices  229 us (55%)
  Pallas kernels  83.3 us (20%)
  starting transfers between devices  38.2 us (9%)
  matrix products  34.1 us (8%)
  between operations  13.5 us (3%)
  local copies, waits for them, and re-layouts  11.9 us (3%)
    all_to_all x1, waiting for transfers between devices, local(): lax.all_to_all(mid.reshape(spatial, -1, full), 'spatial', 0, 0, tiled=True)  104 us
    all_gather x1, waiting for transfers between devices, local(): lax.all_gather(first_part, ('spatial', 'dp'), axis=0, tiled=True)  68.5 us
    pallas_call x2, Pallas kernels, local_output(): pl.pallas_call(functools.partial(body, column_rows, head_size), grid=(cou...  42.5 us
    all_to_all x1, waiting for transfers between devices, local(): returned = lax.all_to_all(backward, 'spatial', 0, 0, tiled=True)  25.3 us
    all_to_all x2, waiting for transfers between devices, entering_state(): received = lax.all_to_all(sent, axes, 0, 0, tiled=True)  19.4 us
    dot_general x1, matrix products, local(): projected = jnp.dot(flattened, first_weight, preferred_element_type=F32)  18.9 us
    pallas_call x2, Pallas kernels, local_state(): pl.pallas_call(functools.partial(state_kernel, column_rows, head_size), g...  18.1 us
    dot_general x1, matrix products, local(): gate_rows = jnp.dot(flattened, gate_weight, preferred_element_type=F32)  15.2 us
  transfers between devices with their start and end apart: 8, of which 6 were waited for; matrix products, arithmetic and copies ran while one was open for 11% of the time, Pallas kernels for 18%

profile of v1, /device:TPU:2, one launch (start us, length us, event | category | flops | bytes accessed | tf_op | source)
XLA Modules:
  0.0 414.4 jit_solution(9482140768175977217)
XLA Ops:
  6.5 2.1 fusion.2
  8.7 0.8 copy.10
  9.5 1.8 fusion.1
  12.1 1.2 pad.13.bias_ref
  13.3 68.5 %all-gather.3.cloned.1.call-done = bf16[3072,1920]{1,0:T(8,128)(2,1)} async-done(((bf16[192,1920]{1,0:T(8,128)(2,1)}), bf16[3072,1920]{1,0:T(8,128)(2,1)}) %all-gather.3.cloned.1.call-update) | async-done | bytes 11796496 | tf_op jit(solution)/shard_map/all_gather | solution.py:358
  81.9 18.9 %fusion.4 = f32[1920,960]{0,1:T(8,128)} fusion(bf16[960,3072]{1,0:T(8,128)(2,1)} %bitcast.26, bf16[3072,1920]{1,0:T(8,128)(2,1)} %all-gather.3.cloned.1.call-done), kind=kOutput, calls=%fused_computation.10 | convolution fusion | flops 11324620800 | bytes 25067520 | tf_op jit(solution)/shard_map/dot_general | solution.py:360
  100.7 7.8 %shard_map.82 = (f32[20,48,1920]{2,1,0:T(8,128)}, f32[960,128]{1,0:T(8,128)}) custom-call(f32[960,1920]{1,0:T(8,128)} %bitcast.16, f32[1,128]{1,0:T(1,128)} %pad.13.bias_ref), custom_call_target="tpu_custom_call" | custom-call | tf_op jit(solution)/shard_map/pallas_call | solution.py:73
  108.6 6.3 %all-to-all-start.2 = ((f32[4,240,1920]{2,1,0:T(8,128)}), f32[4,240,1920]{2,1,0:T(8,128)}, u32[]{:S(2)}, u32[]{:S(2)}) async-start(f32[4,240,1920]{2,1,0:T(8,128)} %bitcast.23), calls=%async_computation.2 | async-start | bytes 14745600 | tf_op jit(solution)/shard_map/all_to_all | solution.py:369
  115.4 104.1 %all-to-all-done.2.values_ref.keys_ref.steps_ref.queries_ref = f32[4,240,1920]{2,1,0:T(8,128)} async-done(((f32[4,240,1920]{2,1,0:T(8,128)}), f32[4,240,1920]{2,1,0:T(8,128)}, u32[]{:S(2)}, u32[]{:S(2)}) %all-to-all-start.2) | async-done | bytes 7372832 | tf_op jit(solution)/shard_map/all_to_all | solution.py:369
  219.6 9.1 %shard_map.86 = (f32[128,1536]{1,0:T(8,128)}, f32[16,128]{1,0:T(8,128)}) custom-call(f32[4,240,1920]{2,1,0:T(8,128)} %all-to-all-done.2.values_ref.keys_ref.steps_ref.queries_ref, f32[4,240,1920]{2,1,0:T(8,128)} %all-to-all-done.2.values_ref.keys_ref.steps_ref.queries_ref, f32[4,240,1920]{2,1,0:T(8,128)} %all-to-all-done.2.values_ref.keys_ref.steps_ref.queries_ref, ...), custom_call_target="tpu_custom_call" | custom-call | tf_op jit(solution)/shard_map/pallas_call | solution.py:233
  228.6 1.2 reshape.31
  230.5 1.2 pad_maximum_fusion.1
  231.8 9.1 %all-to-all-start.3 = ((f32[32,64,128]{2,1,0:T(8,128)}), f32[32,64,128]{2,1,0:T(8,128)S(1)}, u32[]{:S(2)}, u32[]{:S(2)}) async-start(f32[32,64,128]{2,1,0:T(8,128)} %pad_maximum_fusion.1), calls=%async_computation.3 | async-start | bytes 2097152 | tf_op jit(solution)/shard_map/all_to_all | solution.py:290
  240.9 9.0 %shard_map.83 = (f32[128,1536]{1,0:T(8,128)}, f32[16,128]{1,0:T(8,128)}) custom-call(f32[1,960,1920]{2,1,0:T(8,128)} %bitcast.17, f32[1,960,1920]{2,1,0:T(8,128)} %bitcast.18, f32[1,960,128]{2,1,0:T(8,128)} %bitcast.24, f32[1,128]{1,0:T(1,128)} %get-tuple-element.20.rate_ref), custom_call_target="tpu_custom_call" | custom-call | tf_op jit(solution)/shard_map/pallas_call | solution.py:233
  249.9 1.2 reshape.28
  251.8 1.1 pad_maximum_fusion
  252.9 5.4 %all-to-all-done.3.source_ref = f32[32,64,128]{2,1,0:T(8,128)S(1)} async-done(((f32[32,64,128]{2,1,0:T(8,128)}), f32[32,64,128]{2,1,0:T(8,128)S(1)}, u32[]{:S(2)}, u32[]{:S(2)}) %all-to-all-start.3) | async-done | bytes 1048608 | tf_op jit(solution)/shard_map/all_to_all | solution.py:290
  258.3 5.7 %all-to-all-start = ((f32[32,64,128]{2,1,0:T(8,128)}), f32[32,64,128]{2,1,0:T(8,128)S(1)}, u32[]{:S(2)}, u32[]{:S(2)}) async-start(f32[32,64,128]{2,1,0:T(8,128)} %pad_maximum_fusion), calls=%async_computation | async-start | bytes 2097152 | tf_op jit(solution)/shard_map/all_to_all | solution.py:290
  264.0 2.3 shard_map.87
  266.3 14.1 %all-to-all-done.source_ref = f32[32,64,128]{2,1,0:T(8,128)S(1)} async-done(((f32[32,64,128]{2,1,0:T(8,128)}), f32[32,64,128]{2,1,0:T(8,128)S(1)}, u32[]{:S(2)}, u32[]{:S(2)}) %all-to-all-start) | async-done | bytes 1048608 | tf_op jit(solution)/shard_map/all_to_all | solution.py:290
  280.4 5.8 %all-to-all-start.4 = ((f32[32,48,128]{2,1,0:T(8,128)}), f32[32,48,128]{2,1,0:T(8,128)S(1)}, u32[]{:S(2)}, u32[]{:S(2)}) async-start(f32[32,48,128]{2,1,0:T(8,128)} %shard_map.87), calls=%async_computation.4 | async-start | bytes 1572864 | tf_op jit(solution)/shard_map/all_to_all | solution.py:296
  286.2 2.2 shard_map.84
  288.5 11.2 %all-to-all-done.4 = f32[32,48,128]{2,1,0:T(8,128)S(1)} async-done(((f32[32,48,128]{2,1,0:T(8,128)}), f32[32,48,128]{2,1,0:T(8,128)S(1)}, u32[]{:S(2)}, u32[]{:S(2)}) %all-to-all-start.4) | async-done | bytes 786464 | tf_op jit(solution)/shard_map/all_to_all | solution.py:296
  299.7 5.5 %all-to-all-start.1 = ((f32[32,48,128]{2,1,0:T(8,128)}), f32[32,48,128]{2,1,0:T(8,128)S(1)}, u32[]{:S(2)}, u32[]{:S(2)}) async-start(f32[32,48,128]{2,1,0:T(8,128)} %shard_map.84), calls=%async_computation.1 | async-start | bytes 1572864 | tf_op jit(solution)/shard_map/all_to_all | solution.py:296
  305.2 1.0 reshape.32.rest_0_
  306.2 20.9 %shard_map.88 = f32[4,240,1536]{2,1,0:T(8,128)} custom-call(f32[4,240,1920]{2,1,0:T(8,128)} %all-to-all-done.2.values_ref.keys_ref.steps_ref.queries_ref, f32[4,240,1920]{2,1,0:T(8,128)} %all-to-all-done.2.values_ref.keys_ref.steps_ref.queries_ref, f32[4,240,1920]{2,1,0:T(8,128)} %all-to-all-done.2.values_ref.keys_ref.steps_ref.queries_ref, ...), custom_call_target="tpu_custom_call" | custom-call | tf_op jit(solution)/shard_map/pallas_call | solution.py:253
  327.1 5.7 %all-to-all-start.5 = ((f32[4,240,1536]{2,1,0:T(8,128)}), f32[4,240,1536]{2,1,0:T(8,128)}, u32[]{:S(2)}, u32[]{:S(2)}) async-start(f32[4,240,1536]{2,1,0:T(8,128)} %shard_map.88), calls=%async_computation.5 | async-start | bytes 11796480 | tf_op jit(solution)/shard_map/all_to_all | solution.py:385
  334.1 15.2 %fusion.3.gate_ref = f32[960,1536]{1,0:T(8,128)} fusion(bf16[960,3072]{1,0:T(8,128)(2,1)} %bitcast.27, bf16[3072,1536]{1,0:T(8,128)(2,1)} %all-gather.5.cloned.1.call-done), kind=kOutput, calls=%fused_computation.9 | convolution fusion | flops 9059696640 | bytes 21233664 | tf_op jit(solution)/shard_map/dot_general | solution.py:361
  349.3 1.0 reshape.29.entering_ref
  350.3 21.6 %shard_map.85 = f32[1,960,1536]{2,1,0:T(8,128)} custom-call(f32[1,960,1920]{2,1,0:T(8,128)} %bitcast.19, f32[1,960,1920]{2,1,0:T(8,128)} %bitcast.20, f32[1,960,1920]{2,1,0:T(8,128)} %bitcast.21, f32[1,960,128]{2,1,0:T(8,128)} %bitcast.25, f32[1,128]{1,0:T(1,128)} %get-tuple-element.20.rate_ref, f32[1,1536]{1,0:T(1,128)} %broadcast_in_dim_reshape.3.skip_ref, ...), custom_call_target="tpu_custom_call" | custom-call | tf_op jit(solution)/shard_map/pallas_call | solution.py:253
  371.9 25.3 %all-to-all-done.5 = f32[4,240,1536]{2,1,0:T(8,128)} async-done(((f32[4,240,1536]{2,1,0:T(8,128)}), f32[4,240,1536]{2,1,0:T(8,128)}, u32[]{:S(2)}, u32[]{:S(2)}) %all-to-all-start.5) | async-done | bytes 5898272 | tf_op jit(solution)/shard_map/all_to_all | solution.py:385
  397.1 10.5 %shard_map.89 = bf16[960,1536]{1,0:T(8,128)(2,1)} custom-call(f32[960,1536]{1,0:T(8,128)} %bitcast.22, f32[20,48,1536]{2,1,0:T(8,128)} %bitcast.9.backward_ref, f32[960,1536]{1,0:T(8,128)} %fusion.3.gate_ref, f32[1,1536]{1,0:T(1,128)} %broadcast_in_dim.33.gain_ref), custom_call_target="tpu_custom_call" | custom-call | tf_op jit(solution)/shard_map/pallas_call | solution.py:326
  (23 shorter events, 4.1 us)
Async XLA Ops:
  6.5 75.3 %all-gather.3.cloned.1.call-start = ((), (), s32[]{:S(2)}) async-start(), calls=%async_computation.6 | async-start | bytes 12533760 | tf_op jit(solution)/shard_map/all_gather | solution.py:358
  11.3 322.8 %all-gather.5.cloned.1.call-start = ((), (), s32[]{:S(2)}) async-start(), calls=%async_computation.7 | async-start | bytes 10027008 | tf_op jit(solution)/shard_map/all_gather | solution.py:359
  108.6 6.3 %copy-start.3 = (f32[2,24]{1,0:T(2,128)S(1)}, f32[2,24]{1,0:T(2,128)}, u32[]{:S(2)}) copy-start(f32[2,24]{1,0:T(2,128)} %param.13) | copy-start | bytes 580
  108.6 111.0 %all-to-all-start.2 = ((f32[4,240,1920]{2,1,0:T(8,128)}), f32[4,240,1920]{2,1,0:T(8,128)}, u32[]{:S(2)}, u32[]{:S(2)}) async-start(f32[4,240,1920]{2,1,0:T(8,128)} %bitcast.23), calls=%async_computation.2 | async-start | bytes 14745600 | tf_op jit(solution)/shard_map/all_to_all | solution.py:369
  231.8 26.5 %all-to-all-start.3 = ((f32[32,64,128]{2,1,0:T(8,128)}), f32[32,64,128]{2,1,0:T(8,128)S(1)}, u32[]{:S(2)}, u32[]{:S(2)}) async-start(f32[32,64,128]{2,1,0:T(8,128)} %pad_maximum_fusion.1), calls=%async_computation.3 | async-start | bytes 2097152 | tf_op jit(solution)/shard_map/all_to_all | solution.py:290
  258.3 5.7 %copy-start = (f32[32,64,128]{2,1,0:T(8,128)}, f32[32,64,128]{2,1,0:T(8,128)S(1)}, u32[]{:S(2)}) copy-start(f32[32,64,128]{2,1,0:T(8,128)S(1)} %all-to-all-done.3.source_ref) | copy-start | bytes 3145732
  258.3 22.1 %all-to-all-start = ((f32[32,64,128]{2,1,0:T(8,128)}), f32[32,64,128]{2,1,0:T(8,128)S(1)}, u32[]{:S(2)}, u32[]{:S(2)}) async-start(f32[32,64,128]{2,1,0:T(8,128)} %pad_maximum_fusion), calls=%async_computation | async-start | bytes 2097152 | tf_op jit(solution)/shard_map/all_to_all | solution.py:290
  280.4 5.8 %copy-start.1 = (f32[32,64,128]{2,1,0:T(8,128)}, f32[32,64,128]{2,1,0:T(8,128)S(1)}, u32[]{:S(2)}) copy-start(f32[32,64,128]{2,1,0:T(8,128)S(1)} %all-to-all-done.source_ref) | copy-start | bytes 3145732
  280.4 19.3 %all-to-all-start.4 = ((f32[32,48,128]{2,1,0:T(8,128)}), f32[32,48,128]{2,1,0:T(8,128)S(1)}, u32[]{:S(2)}, u32[]{:S(2)}) async-start(f32[32,48,128]{2,1,0:T(8,128)} %shard_map.87), calls=%async_computation.4 | async-start | bytes 1572864 | tf_op jit(solution)/shard_map/all_to_all | solution.py:296
  299.7 27.4 %all-to-all-start.1 = ((f32[32,48,128]{2,1,0:T(8,128)}), f32[32,48,128]{2,1,0:T(8,128)S(1)}, u32[]{:S(2)}, u32[]{:S(2)}) async-start(f32[32,48,128]{2,1,0:T(8,128)} %shard_map.84), calls=%async_computation.1 | async-start | bytes 1572864 | tf_op jit(solution)/shard_map/all_to_all | solution.py:296
  327.1 5.7 %copy-start.4 = (f32[2,24]{1,0:T(2,128)S(1)}, f32[2,24]{1,0:T(2,128)}, u32[]{:S(2)}) copy-start(f32[2,24]{1,0:T(2,128)} %param.14) | copy-start | bytes 580
  327.1 6.5 %copy-start.2 = (f32[1536]{0:T(1024)S(1)}, f32[1536]{0:T(1024)}, u32[]{:S(2)}) copy-start(f32[1536]{0:T(1024)} %param.15) | copy-start | bytes 18436
  327.1 70.1 %all-to-all-start.5 = ((f32[4,240,1536]{2,1,0:T(8,128)}), f32[4,240,1536]{2,1,0:T(8,128)}, u32[]{:S(2)}, u32[]{:S(2)}) async-start(f32[4,240,1536]{2,1,0:T(8,128)} %shard_map.88), calls=%async_computation.5 | async-start | bytes 11796480 | tf_op jit(solution)/shard_map/all_to_all | solution.py:385
Sparse Core Ops, SparseCore 0:
  11.5 70.3 all-gather.2
  83.6 80.4 all-gather.4

commit v2 on v1

v2 whole, which is shorter than its diff:
```python
import functools

import jax
import jax.numpy as jnp
from jax import lax
from jax.experimental import pallas as pl
from jax.experimental.pallas import tpu as pltpu
from jax.sharding import PartitionSpec as P

F32 = jnp.float32
BF16 = jnp.bfloat16
LANES = 128
GROUP = 4
POWER = 17
CODE_TOP = 128.0
STEP_LANES = 24
MESH = pl.DeviceIdType.MESH
VMEM_BYTES = 56 * 1024 * 1024


def split(value):
    high = value.astype(BF16)
    return high, (value - high.astype(F32)).astype(BF16)


def dot(a, b):
    return lax.dot_general(a, b, (((1,), (0,)), ((), ())), preferred_element_type=F32)


def rows_iota(shape):
    return lax.broadcasted_iota(jnp.int32, shape, 0)


def lanes_iota(shape):
    return lax.broadcasted_iota(jnp.int32, shape, 1)


def spread(columns, pair, head_size):
    first, second = columns[:, 2 * pair : 2 * pair + 1], columns[:, 2 * pair + 1 : 2 * pair + 2]
    shape = (columns.shape[0], LANES)
    return jnp.where(lanes_iota(shape) < head_size, first, second)


def params(semantics=("arbitrary",)):
    return pltpu.CompilerParams(vmem_limit_bytes=VMEM_BYTES, dimension_semantics=semantics)


def encode(scaled):
    square = scaled * scaled
    fourth = square * square
    eighth = fourth * fourth
    return (eighth * eighth * scaled).astype(BF16)


def decode(coded):
    coded = coded.astype(F32)
    size = jnp.exp2(jnp.log2(jnp.abs(coded)) * (1.0 / POWER))
    return jnp.where(coded < 0.0, -size, size)


def code_scale(largest):
    scale = jnp.maximum(largest, 1e-30).astype(BF16)
    return scale, CODE_TOP / scale.astype(F32)


def column_groups(first, second):
    low = rows_iota(first.shape) < GROUP
    even = jnp.where(low, first, pltpu.roll(second, GROUP, 0))
    odd = jnp.where(low, pltpu.roll(first, GROUP, 0), second)
    return even, odd


def project_kernel(
    geometry,
    tokens_ref,
    state_ref,
    bias_ref,
    xz_ref,
    values_ref,
    keys_ref,
    columns_ref,
    weight,
    product,
    middle,
    own_sem,
    x_send,
    x_recv,
    y_send,
    y_recv,
    core_send,
    core_recv,
    move_send,
    move_recv,
    move_own,
    out_sem,
):
    row_part, col_total, inner, depth, blocks = geometry
    half = depth // 2
    frame, place, part = lax.axis_index("frame"), lax.axis_index("spatial"), lax.axis_index("dp")
    core, y = part % 2, (frame % 2) * 2 + part // 2
    right, left, across = (place + 1) % 4, (place + 3) % 4, (place + 2) % 4

    def y_device(other):
        return ((frame // 2) * 2 + other // 2, place, (other % 2) * 2 + core)

    x_right, x_left, x_across = (frame, right, part), (frame, left, part), (frame, across, part)
    y_up, y_down = y_device((y + 1) % 4), y_device((y + 3) % 4)
    partner = (frame, place, (part // 2) * 2 + 1 - core)

    barrier = pltpu.get_barrier_semaphore()
    peers = (x_right, x_left, x_across, y_up, y_down, partner)
    for peer in peers:
        pl.semaphore_signal(barrier, inc=1, device_id=peer, device_id_type=MESH)
    pl.semaphore_wait(barrier, len(peers))

    def slot(where, other_core, other_part):
        return where * 4 + other_part * 2 + other_core

    same, opposite = part // 2, 1 - part // 2
    sources = (place, left, right, across)

    def rows(index, first, count):
        return pl.ds(pl.multiple_of(index * depth + first, 16), count)

    def view(block, index, first, count):
        return weight.at[block, rows(index, first, count), pl.ds(0, blocks[block][1])]

    def own(block, first, count):
        start, width = blocks[block]
        if block == 0:
            return state_ref.at[pl.ds(first, count), :]
        return xz_ref.at[pl.ds(first, count), pl.ds(inner + start, width)]

    pending = []

    def send(source, target, send_sem, recv_sem, device):
        copy = pltpu.make_async_remote_copy(
            src_ref=source,
            dst_ref=target,
            send_sem=send_sem,
            recv_sem=recv_sem,
            device_id=device,
            device_id_type=MESH,
        )
        copy.start()
        pending.append(copy)

    def arrived(target, send_sem, recv_sem):
        pltpu.make_async_remote_copy(
            src_ref=target,
            dst_ref=target,
            send_sem=send_sem,
            recv_sem=recv_sem,
            device_id=x_right,
            device_id_type=MESH,
        ).wait_recv()

    def send_y(block, which, source_of):
        index = slot(sources[which], core, same)
        for part_at, device in ((0, y_up), (1, y_down)):
            first = part_at * half
            send(
                source_of(first),
                view(block, index, first, half),
                y_send.at[block, which, part_at],
                y_recv.at[block, which, part_at],
                device,
            )

    def send_core(block, at, index, source):
        send(
            source,
            view(block, index, 0, depth),
            core_send.at[block, at],
            core_recv.at[block, at],
            partner,
        )

    def send_own(block):
        index = slot(place, core, same)
        target = view(block, index, 0, depth)
        source = own(block, 0, depth)
        send(source, target, x_send.at[block, 0], x_recv.at[block, 0], x_right)
        send(source, target, x_send.at[block, 1], x_recv.at[block, 1], x_left)
        send_y(block, 0, lambda first: own(block, first, half))
        send_core(block, 0, index, source)
        copy = pltpu.make_async_copy(source, target, own_sem.at[block])
        copy.start()

    def relay(block):
        from_left, from_right = slot(left, core, same), slot(right, core, same)
        far = slot(across, core, same)
        for which, index in ((1, from_left), (2, from_right)):
            arrived(
                view(block, index, 0, depth),
                x_send.at[block, which - 1],
                x_recv.at[block, which - 1],
            )
            part_at = which - 1
            send(
                view(block, index, part_at * half, half),
                view(block, index, part_at * half, half),
                x_send.at[block, 2 + part_at],
                x_recv.at[block, 2 + part_at],
                (x_right, x_left)[part_at],
            )
            send_y(block, which, lambda first: view(block, index, first, half))
            send_core(block, which, index, view(block, index, 0, depth))
        for part_at in (0, 1):
            arrived(
                view(block, far, part_at * half, half),
                x_send.at[block, 2 + part_at],
                x_recv.at[block, 2 + part_at],
            )
        send_y(block, 3, lambda first: view(block, far, first, half))
        send_core(block, 3, far, view(block, far, 0, depth))

    def pass_on(block):
        for which in range(4):
            index = slot(sources[which], core, opposite)
            for part_at in (0, 1):
                arrived(
                    view(block, index, part_at * half, half),
                    y_send.at[block, which, part_at],
                    y_recv.at[block, which, part_at],
                )
            send_core(block, 4 + which, index, view(block, index, 0, depth))

    def gathered(block):
        for at in range(8):
            index = slot(sources[at % 4], 1 - core, same if at < 4 else opposite)
            arrived(
                view(block, index, 0, depth), core_send.at[block, at], core_recv.at[block, at]
            )
        index = slot(place, core, same)
        target = view(block, index, 0, depth)
        pltpu.make_async_copy(own(block, 0, depth), target, own_sem.at[block]).wait()

    tokens = row_part * col_total
    tile = tokens // 5
    groups = col_total // GROUP // 4
    piece_rows = groups * row_part * GROUP
    outs = {}

    def compute(block):
        start, width = blocks[block]
        lanes = pl.ds(0, width)
        buffer = block % 2
        if block - 2 in outs:
            outs.pop(block - 2).wait()

        def one_tile(i, largest):
            at = pl.ds(pl.multiple_of(i * tile, tile), tile)
            result = dot(tokens_ref[at, :], weight[block, :, lanes])
            if block == 0:
                raw = result[:, width - LANES :] + bias_ref[...]
                steps = jnp.maximum(raw, 0.0) + jnp.log1p(jnp.exp(-jnp.abs(raw)))
                result = jnp.concatenate([result[:, : width - LANES], steps], axis=1)
            product[buffer, at, lanes] = result
            return jnp.maximum(largest, jnp.max(jnp.abs(result), axis=0, keepdims=True))

        largest = lax.fori_loop(0, 5, one_tile, jnp.zeros((1, width), F32))
        if block == 0:
            out = keys_ref
        else:
            out = values_ref.at[:, pl.ds(start, width)]
        copy = pltpu.make_async_copy(product.at[buffer, :, lanes], out, out_sem.at[block])
        copy.start()
        outs[block] = copy

        scale, factor = code_scale(largest)

        def code(value):
            coded = encode(value * factor)
            if block == 0:
                exact = value[:, width - LANES :]
                high = exact.astype(BF16)
                rest = exact - high.astype(F32)
                second = rest.astype(BF16)
                third = (rest - second.astype(F32)).astype(BF16)
                lane = lanes_iota(exact.shape)
                heads = STEP_LANES
                parts = jnp.where(
                    lane < heads,
                    high.astype(F32),
                    jnp.where(lane < 2 * heads, second.astype(F32), third.astype(F32)),
                )
                coded = jnp.concatenate([coded[:, : width - LANES], parts.astype(BF16)], axis=1)
            return coded

        for quad in range(row_part // 4):

            def one_group(at, carry):
                both = []
                for pair in (2 * quad, 2 * quad + 1):
                    first = product[buffer, pl.ds(pl.multiple_of(2 * pair * col_total + 8 * at, 8), 8), lanes]
                    second = product[
                        buffer, pl.ds(pl.multiple_of((2 * pair + 1) * col_total + 8 * at, 8), 8), lanes
                    ]
                    both.append(column_groups(first, second))
                for odd in (0, 1):
                    group = 2 * at + odd
                    piece = group // groups
                    row = pl.multiple_of((group % groups) * row_part * GROUP + 16 * quad, 16)
                    value = jnp.concatenate([both[0][odd], both[1][odd]], axis=0)
                    middle[block, piece, pl.ds(row, 16), lanes] = code(value)
                return carry

            lax.fori_loop(0, col_total // 8, one_group, 0)
        for piece in range(4):
            middle[block, piece, pl.ds(piece_rows, 16), lanes] = jnp.broadcast_to(scale, (16, width))
        into = columns_ref.at[place, :, pl.ds(inner if block == 0 else start, width)]
        for at, (where, device) in enumerate(((right, x_right), (left, x_left), (across, x_across))):
            send(
                middle.at[block, where, :, lanes],
                into,
                move_send.at[block, at],
                move_recv.at[block, at],
                device,
            )
        pltpu.make_async_copy(middle.at[block, place, :, lanes], into, move_own.at[block]).start()

    count = len(blocks)
    send_own(0)
    send_own(1)
    relay(0)
    for block in range(count):
        if block + 2 < count:
            send_own(block + 2)
        if block + 1 < count:
            relay(block + 1)
        pass_on(block)
        gathered(block)
        compute(block)
    for block in range(count):
        start, width = blocks[block]
        lanes = pl.ds(0, width)
        for at, where in enumerate((left, right, across)):
            into = columns_ref.at[where, :, pl.ds(inner if block == 0 else start, width)]
            arrived(into, move_send.at[block, at], move_recv.at[block, at])
        into = columns_ref.at[place, :, pl.ds(inner if block == 0 else start, width)]
        pltpu.make_async_copy(middle.at[block, place, :, lanes], into, move_own.at[block]).wait()
    for copy in outs.values():
        copy.wait()
    for copy in pending:
        copy.wait_send()


def project(tokens, state_weight, bias, xz_weight, row_part, col_total, inner, block_width):
    depth, state_width = state_weight.shape
    count = inner // block_width + 1
    blocks = ((0, state_width),) + tuple((k * block_width, block_width) for k in range(count - 1))
    width = max(block_width, state_width)
    total = tokens.shape[0]
    piece_rows = total // 4 + 16
    vmem, hbm = pl.BlockSpec(memory_space=pltpu.VMEM), pl.BlockSpec(memory_space=pl.ANY)
    dma = pltpu.SemaphoreType.DMA
    return pl.pallas_call(
        functools.partial(project_kernel, (row_part, col_total, inner, depth, blocks)),
        in_specs=[vmem, vmem, vmem, hbm],
        out_specs=[hbm, hbm, hbm],
        out_shape=[
            jax.ShapeDtypeStruct((total, inner), F32),
            jax.ShapeDtypeStruct((total, state_width), F32),
            jax.ShapeDtypeStruct((4, piece_rows, inner + state_width), BF16),
        ],
        scratch_shapes=[
            pltpu.VMEM((count, tokens.shape[1], width), BF16),
            pltpu.VMEM((2, total, width), F32),
            pltpu.VMEM((count, 4, piece_rows, width), BF16),
            dma((count,)),
            dma((count, 4)),
            dma((count, 4)),
            dma((count, 4, 2)),
            dma((count, 4, 2)),
            dma((count, 8)),
            dma((count, 8)),
            dma((count, 3)),
            dma((count, 3)),
            dma((count,)),
            dma((count,)),
        ],
        compiler_params=pltpu.CompilerParams(
            collective_id=0, has_side_effects=True, vmem_limit_bytes=VMEM_BYTES
        ),
    )(tokens, state_weight, bias, xz_weight)


def earlier_mask(size, column_rows):
    shape = (size, size)
    t, s = rows_iota(shape), lanes_iota(shape)
    if column_rows:

        def place(index):
            return size - 1 - (lax.rem(index, GROUP) * column_rows + index // GROUP)

        t, s = place(t), place(s)
    return s <= t


def running_logs(steps, rate, earlier):
    logs = -steps * rate
    high, rest = split(logs)
    middle = logs - high.astype(F32)
    middle, low = split(middle)
    before = jnp.where(earlier, 1.0, 0.0).astype(BF16)
    running = dot(before, high) + dot(before, middle) + dot(before, low)
    return running, jnp.sum(logs, axis=0, keepdims=True)


def advance(memory, keys_t, weighted, decay):
    keys_high, keys_low = keys_t
    high, low = split(weighted)
    both = dot(keys_high, jnp.concatenate([high, low], axis=1))
    added = both[:, :LANES] + both[:, LANES:] + dot(keys_low, high)
    return memory * decay + added


class Chunk:
    def __init__(self, column_rows, values_ref, keys_ref, steps_ref, scale_ref):
        self.size = values_ref.shape[0] * values_ref.shape[1]
        self.inner = values_ref.shape[2]
        self.pairs = self.inner // LANES
        self.column_rows, self.values_ref, self.scale_ref = column_rows, values_ref, scale_ref
        self.keys_ref, self.steps_ref = keys_ref, steps_ref
        if column_rows:
            self.scales = [scale_ref[k, pl.ds(0, 16), :].astype(F32)[0:1] for k in range(4)]

    def read(self, ref, lanes, scale_lane):
        block = ref[:, :, lanes]
        if not self.column_rows:
            return block.reshape(self.size, LANES)
        block = decode(block)
        parts = [
            block[k] * (self.scales[k][:, scale_lane : scale_lane + LANES] * (1.0 / CODE_TOP))
            for k in range(4)
        ]
        return jnp.concatenate(parts, axis=0)

    def values(self, pair):
        return self.read(self.values_ref, pl.ds(pair * LANES, LANES), pair * LANES)

    def keys(self):
        return self.read(self.keys_ref, pl.ds(0, LANES), self.inner)

    def queries(self, ref):
        return self.read(ref, pl.ds(0, LANES), self.inner + LANES)

    def steps(self):
        block = self.steps_ref[...].reshape(self.size, LANES)
        if not self.column_rows:
            return block
        shape = (LANES, LANES)
        part, head = rows_iota(shape), lanes_iota(shape)
        fold = (lax.rem(part, STEP_LANES) == head) & (part < 3 * STEP_LANES)
        return dot(block, jnp.where(fold, 1.0, 0.0).astype(BF16))

    def earlier(self):
        return earlier_mask(self.size, self.column_rows)


def state_kernel(column_rows, head_size, values_ref, keys_ref, steps_ref, *rest):
    scale_ref = rest[0] if column_rows else None
    rate_ref, memory_ref, decay_ref = rest[-3:]
    chunk = Chunk(column_rows, values_ref, keys_ref, steps_ref, scale_ref)

    @pl.when(pl.program_id(0) == 0)
    def _():
        memory_ref[...] = jnp.zeros_like(memory_ref)
        decay_ref[...] = jnp.ones_like(decay_ref)

    steps = chunk.steps()
    keys_t = split(jnp.transpose(chunk.keys()))
    running, total = running_logs(steps, rate_ref[...], chunk.earlier())
    coefficient = steps * jnp.exp(jnp.minimum(total - running, 0.0))
    decay = jnp.exp(total)
    for pair in range(chunk.pairs):
        lanes = pl.ds(pair * LANES, LANES)
        weighted = chunk.values(pair) * spread(coefficient, pair, head_size)
        pair_decay = spread(decay, pair, head_size)
        memory_ref[:, lanes] = advance(memory_ref[:, lanes], keys_t, weighted, pair_decay)
        decay_ref[pl.ds(pair, 1), :] = decay_ref[pl.ds(pair, 1), :] * pair_decay


def output_kernel(column_rows, head_size, values_ref, keys_ref, steps_ref, *rest):
    if column_rows:
        scale_ref, queries_ref, rate_ref, entering_ref, out_ref, memory_ref, scales_ref = rest
        skip_ref = None
    else:
        queries_ref, rate_ref, entering_ref, skip_ref, out_ref, memory_ref = rest
        scale_ref = None
    chunk = Chunk(column_rows, values_ref, keys_ref, steps_ref, scale_ref)
    size = chunk.size

    @pl.when(pl.program_id(0) == 0)
    def _():
        memory_ref[...] = entering_ref[...]
        if column_rows:
            scales_ref[...] = jnp.zeros_like(scales_ref)

    steps = chunk.steps()
    keys_t = split(jnp.transpose(chunk.keys()))
    queries_high, queries_low = split(chunk.queries(queries_ref))
    earlier = chunk.earlier()
    running, total = running_logs(steps, rate_ref[...], earlier)
    across = jnp.transpose(running)
    scores = dot(queries_high, keys_t[0]) + dot(queries_high, keys_t[1]) + dot(queries_low, keys_t[0])
    scores = jnp.where(earlier, scores, 0.0)
    arrived = jnp.exp(running)
    leaving = jnp.exp(jnp.minimum(total - running, 0.0))
    decay = jnp.exp(total)
    first_half = lanes_iota((size, LANES)) < head_size
    at = pl.num_programs(0) - 1 - pl.program_id(0)
    for pair in range(chunk.pairs):
        lanes = pl.ds(pair * LANES, LANES)
        values = chunk.values(pair)
        scaled = values * spread(steps, pair, head_size)
        high, low = split(scaled)
        both = jnp.concatenate([high, low], axis=1)
        halves = []
        for head in (2 * pair, 2 * pair + 1):
            between = jnp.minimum(running[:, head : head + 1] - across[head : head + 1, :], 0.0)
            kernel_high, kernel_low = split(jnp.exp(between) * scores)
            part = dot(kernel_high, both)
            halves.append(part[:, :LANES] + part[:, LANES:] + dot(kernel_low, high))
        memory = memory_ref[:, lanes]
        memory_high, memory_low = split(memory)
        part = dot(queries_high, jnp.concatenate([memory_high, memory_low], axis=1))
        carried = part[:, :LANES] + part[:, LANES:] + dot(queries_low, memory_high)
        result = jnp.where(first_half, halves[0], halves[1])
        result = result + carried * spread(arrived, pair, head_size)
        if column_rows:
            scale, factor = code_scale(jnp.max(jnp.abs(result), axis=0, keepdims=True))
            coded = encode(result * factor).reshape(4, size // 4, LANES)
            first = pl.multiple_of(at * (size // 4), 16)
            out_ref[:, pl.ds(first, size // 4), lanes] = coded
            here = rows_iota((16, LANES)) == at
            scales_ref[:, lanes] = jnp.where(here, scale.astype(F32), scales_ref[:, lanes])
        else:
            result = result + values * skip_ref[:, lanes]
            out_ref[:, :, lanes] = result.reshape(1, size, LANES)
        weighted = scaled * spread(leaving, pair, head_size)
        memory_ref[:, lanes] = advance(memory, keys_t, weighted, spread(decay, pair, head_size))

    if column_rows:

        @pl.when(pl.program_id(0) == pl.num_programs(0) - 1)
        def _():
            scales = scales_ref[...].astype(BF16)
            for k in range(4):
                out_ref[k, pl.ds(out_ref.shape[1] - 16, 16), :] = scales


def chunk_specs(sources, inner, size, column_rows):
    pieces = 4 if column_rows else 1
    part = size // pieces
    count = sources[0].shape[1] // part
    first = inner // LANES if column_rows else 0

    def spec(lane_count, lane_block):
        def index(j):
            return (0, count - 1 - j if column_rows else j, lane_block)

        return pl.BlockSpec((pieces, part, lane_count), index)

    specs = [spec(inner, 0), spec(LANES, first), spec(LANES, first + 2)]
    arrays = [sources[0], sources[-1], sources[-1]]
    if column_rows:
        last = sources[0].shape[1] // 16 - 1
        specs.append(pl.BlockSpec((pieces, 16, sources[0].shape[2]), lambda j: (0, last, 0)))
        arrays.append(sources[0])
    return count, specs, arrays, spec(LANES, first + 1)


def whole(shape):
    return pl.BlockSpec(shape, lambda j: (0,) * len(shape))


def estimate(tokens, inner, passes, transfers):
    return pl.CostEstimate(
        flops=2 * tokens * inner * 192 * passes, bytes_accessed=transfers, transcendentals=0
    )


def local_state(sources, rate, inner, size, column_rows, head_size):
    count, specs, arrays, _ = chunk_specs(sources, inner, size, column_rows)
    return pl.pallas_call(
        functools.partial(state_kernel, column_rows, head_size),
        grid=(count,),
        in_specs=specs + [whole((1, LANES))],
        out_specs=[whole((LANES, inner)), whole((16, LANES))],
        out_shape=[
            jax.ShapeDtypeStruct((LANES, inner), F32),
            jax.ShapeDtypeStruct((16, LANES), F32),
        ],
        cost_estimate=estimate(count * size, inner, 10, 16 << 20),
        compiler_params=params(),
    )(*arrays, rate)


def local_output(sources, rate, entering, skip, inner, size, column_rows, head_size):
    count, specs, arrays, queries = chunk_specs(sources, inner, size, column_rows)
    shape = sources[0].shape[:2] + (inner,)
    extra = [] if column_rows else [skip]
    scratch = [pltpu.VMEM((LANES, inner), F32)]
    if column_rows:
        scratch.append(pltpu.VMEM((16, inner), F32))
    return pl.pallas_call(
        functools.partial(output_kernel, column_rows, head_size),
        grid=(count,),
        in_specs=specs
        + [queries, whole((1, LANES)), whole((LANES, inner))]
        + [whole((1, inner)) for _ in extra],
        out_specs=whole(shape) if column_rows else specs[0],
        out_shape=jax.ShapeDtypeStruct(shape, BF16 if column_rows else F32),
        scratch_shapes=scratch,
        cost_estimate=estimate(count * size, inner, 30, 32 << 20),
        compiler_params=params(),
    )(*arrays, sources[-1], rate, entering, *extra)


def prefix_kernel(reverse, rows, pairs, source_ref, out_ref):
    count = source_ref.shape[0]
    entering = jnp.zeros((rows, LANES), F32)
    for k in range(count):
        at = count - 1 - k if reverse else k
        out_ref[at] = entering
        decay = source_ref[at, pl.ds(rows, pairs), :]
        decay = jnp.concatenate([decay] * (rows // pairs), axis=0)
        entering = entering * decay + source_ref[at, pl.ds(0, rows), :]


def entering_state(memory, decay, axes, reverse):
    count = 1
    for axis in axes:
        count = count * lax.axis_size(axis)
    pairs = memory.shape[1] // LANES
    rows = memory.shape[0] * pairs // count
    sent = jnp.concatenate(
        [
            memory.reshape(count, rows, LANES),
            jnp.broadcast_to(decay[None], (count,) + decay.shape),
        ],
        axis=1,
    )
    received = lax.all_to_all(sent, axes, 0, 0, tiled=True)
    found = pl.pallas_call(
        functools.partial(prefix_kernel, reverse, rows, pairs),
        out_shape=jax.ShapeDtypeStruct((count, rows, LANES), F32),
        compiler_params=pltpu.CompilerParams(vmem_limit_bytes=VMEM_BYTES),
    )(received)
    returned = lax.all_to_all(found, axes, 0, 0, tiled=True)
    return returned.reshape(memory.shape)


def finish_kernel(head_size, groups, part, forward_ref, backward_ref, gate_ref, gain_ref, out_ref, moved_ref):
    col_total = forward_ref.shape[0] // 4
    quad = pl.program_id(0)
    last = backward_ref.shape[1] - 16
    scales = [backward_ref[k, pl.ds(last, 16), :].astype(F32) * (1.0 / CODE_TOP) for k in range(4)]

    def group_rows(group):
        piece, within = group // groups, group % groups
        first = pl.multiple_of(within * part + 16 * quad, 16)
        coded = backward_ref[piece, pl.ds(first, 16), :]
        return decode(coded) * scales[piece][within : within + 1, :]

    for at in range(col_total // 8):
        even, odd = group_rows(2 * at), group_rows(2 * at + 1)
        for k in (0, 1):
            low_half, high_half = even[8 * k : 8 * k + 8], odd[8 * k : 8 * k + 8]
            first, second = column_groups(low_half, high_half)
            moved_ref[pl.ds(2 * k * col_total + 8 * at, 8), :] = first
            moved_ref[pl.ds((2 * k + 1) * col_total + 8 * at, 8), :] = second
    wide = 2 * LANES
    same = rows_iota((wide, wide)) // head_size == lanes_iota((wide, wide)) // head_size
    ones = jnp.where(same, 1.0, 0.0).astype(BF16)
    for block in range(forward_ref.shape[1] // wide):
        lanes = pl.ds(block * wide, wide)
        gate = gate_ref[:, lanes]
        combined = forward_ref[:, lanes] + moved_ref[:, lanes]
        gated = combined * (gate / (1.0 + jnp.exp(-gate)))
        high, low = split(gated * gated)
        mean = (dot(high, ones) + dot(low, ones)) * (1.0 / head_size)
        normed = gated * lax.rsqrt(mean + 1e-5) * gain_ref[:, lanes]
        out_ref[:, lanes] = normed.astype(out_ref.dtype)


def finish(forward, backward, gate, gain, row_part, col_total, head_size):
    tokens, inner = forward.shape
    groups = col_total // GROUP // 4
    block = 4 * col_total
    flat = pl.BlockSpec((block, inner), lambda m: (m, 0))
    return pl.pallas_call(
        functools.partial(finish_kernel, head_size, groups, row_part * GROUP),
        grid=(row_part // 4,),
        in_specs=[flat, whole(backward.shape), flat, whole((1, inner))],
        out_specs=flat,
        out_shape=jax.ShapeDtypeStruct((tokens, inner), BF16),
        scratch_shapes=[pltpu.VMEM((block, inner), F32)],
        compiler_params=params(),
    )(forward, backward, gate, gain)


def pad_lanes(source):
    return jnp.pad(source, ((0, 0), (0, LANES - source.shape[1])))


def local(tokens, xz_weight, state_weight, step_weight, step_bias, decay_rate, skip, norm_gain):
    videos, frame_count, row_part, col_total, width = tokens.shape
    flattened = tokens.reshape(-1, width)
    inner = xz_weight.shape[1] // 2
    heads = step_weight.shape[1]
    head_size = inner // heads
    column_rows = row_part * lax.axis_size("spatial")
    size = column_rows * GROUP
    axes = ("frame", "spatial")

    thrice = pad_lanes(jnp.concatenate([step_weight] * 3, axis=1))
    bias = pad_lanes(jnp.concatenate([step_bias] * 3)[None])
    first_weight = jnp.concatenate([state_weight, thrice], axis=1)
    gate_weight = lax.all_gather(xz_weight[:, :inner], ("spatial", "dp"), axis=0, tiled=True)
    rates = pad_lanes(decay_rate)
    skips = jnp.repeat(skip[0] + skip[1], head_size)[None]

    values, keys, columns = project(
        flattened, first_weight, bias, xz_weight, row_part, col_total, inner, 512
    )
    rowwise = (values[None], keys[None])
    columnwise = (columns,)

    memory, decay = local_state(columnwise, rates[1:2], inner, size, column_rows, head_size)
    entering = entering_state(memory, decay, axes, True)
    forward_memory, forward_decay = local_state(rowwise, rates[0:1], inner, size, 0, head_size)
    forward_entering = entering_state(forward_memory, forward_decay, axes, False)
    backward = local_output(
        columnwise, rates[1:2], entering, None, inner, size, column_rows, head_size
    )
    returned = lax.all_to_all(backward, "spatial", 0, 0, tiled=True)
    forward = local_output(
        rowwise, rates[0:1], forward_entering, skips, inner, size, 0, head_size
    )
    gate_rows = jnp.dot(flattened, gate_weight, preferred_element_type=F32)
    normed = finish(
        forward[0], returned, gate_rows, norm_gain[None], row_part, col_total, head_size
    )
    return normed.reshape(videos, frame_count, row_part, col_total, inner)


def solution(mesh):
    in_specs = (
        P("dp", "frame", "spatial", None, None),
        P(("spatial", "dp"), None),
        P(("spatial", "dp"), None),
        P(("spatial", "dp"), None),
        P(),
        P(),
        P(),
        P(),
    )
    out_specs = P("dp", "frame", "spatial", None, None)
    return jax.shard_map(local, mesh=mesh, in_specs=in_specs, out_specs=out_specs, check_vma=False)
```

time: 417 us -> 323 us (0.77)
  waiting for transfers between devices: 229 us -> 31.9 us
  Pallas kernels: 83.3 us -> 209 us
  matrix products: 34.1 us -> 15.3 us
  starting transfers between devices: 38.2 us -> 32.7 us
    pallas_call x4, Pallas kernels: 60.8 us -> 186 us  [the longest x1 129 us: project(): pl.pallas_call(functools.partial(project_kernel, (row_part, col_total, in...]
    all_to_all x1 -> x0, waiting for transfers between devices: 104 us -> none  [local(): lax.all_to_all(mid.reshape(spatial, -1, full), 'spatial', 0, 0, tiled=True)]
    all_gather x1 -> x0, waiting for transfers between devices: 68.5 us -> none  [local(): lax.all_gather(first_part, ('spatial', 'dp'), axis=0, tiled=True)]
    all_to_all x1, waiting for transfers between devices: 25.3 us -> 0.01 us  [local(): returned = lax.all_to_all(backward, 'spatial', 0, 0, tiled=True)]
    dot_general x1 -> x0, matrix products: 18.9 us -> none  [local(): projected = jnp.dot(flattened, first_weight, preferred_element_type=F32)]
    all_to_all x1 -> x0, starting transfers between devices: 6.28 us -> none  [local(): lax.all_to_all(mid.reshape(spatial, -1, full), 'spatial', 0, 0, tiled=True)]
  transfers between devices with their start and end apart: 8 -> 6, of which waited for: 6 -> 3; matrix products, arithmetic and copies ran while one was open for 11% -> 9% of each run, Pallas kernels for 18% -> 62%
where the time goes in v2:
time: 323 us; the launch traced here: 322 us
  Pallas kernels  209 us (65%)
  starting transfers between devices  32.7 us (10%)
  waiting for transfers between devices  31.9 us (10%)
  matrix products  15.3 us (5%)
  local copies, waits for them, and re-layouts  14.8 us (5%)
  between operations  13.5 us (4%)
  other arithmetic  4.75 us (1%)
    pallas_call x1, Pallas kernels, project(): pl.pallas_call(functools.partial(project_kernel, (row_part, col_total, in...  129 us
    pallas_call x2, Pallas kernels, local_output(): pl.pallas_call(functools.partial(output_kernel, column_rows, head_size),...  46.6 us
    all_to_all x2, waiting for transfers between devices, entering_state(): received = lax.all_to_all(sent, axes, 0, 0, tiled=True)  22.1 us
    pallas_call x2, Pallas kernels, local_state(): pl.pallas_call(functools.partial(state_kernel, column_rows, head_size), g...  18.8 us
    all_to_all x2, starting transfers between devices, entering_state(): received = lax.all_to_all(sent, axes, 0, 0, tiled=True)  16.7 us
    dot_general x1, matrix products, local(): gate_rows = jnp.dot(flattened, gate_weight, preferred_element_type=F32)  15.3 us
    all_to_all x2, starting transfers between devices, entering_state(): returned = lax.all_to_all(found, axes, 0, 0, tiled=True)  11.3 us
    pallas_call x1, Pallas kernels, finish(): pl.pallas_call(functools.partial(finish_kernel, head_size, groups, row_pa...  10.8 us
  transfers between devices with their start and end apart: 6, of which 3 were waited for; matrix products, arithmetic and copies ran while one was open for 9% of the time, Pallas kernels for 62%

profile of v2, /device:TPU:2, one launch (start us, length us, event | category | flops | bytes accessed | tf_op | source)
XLA Modules:
  0.0 322.1 jit_solution(1067886241704648089)
XLA Ops:
  6.5 1.9 slice.21
  8.5 0.8 copy.9
  9.3 0.9 maximum_bitcast_fusion
  10.9 1.6 pad_maximum_fusion.2.state_ref
  12.5 128.6 %shard_map.82 = (f32[960,1536]{1,0:T(8,128)}, f32[960,384]{1,0:T(8,128)}, bf16[4,256,1920]{2,1,0:T(8,128)(2,1)}) custom-call(bf16[960,3072]{1,0:T(8,128)(2,1)} %bitcast.11, bf16[192,384]{1,0:T(8,128)(2,1)} %pad_maximum_fusion.2.state_ref, f32[1,128]{1,0:T(1,128)} %pad.13.bias_ref, bf16[192,3072]{1,0:T(8,128)(2,1)} %xz_ref.1), custom_call_target="tpu_custom_call" | custom-call | tf_op jit(solution)/shard_map/pallas_call | solution.py:358
  141.6 9.8 %shard_map.86 = (f32[128,1536]{1,0:T(8,128)}, f32[16,128]{1,0:T(8,128)}) custom-call(bf16[4,256,1920]{2,1,0:T(8,128)(2,1)} %get-tuple-element.16.values_ref.keys_ref.steps_ref.rest_0_.rest_1_, bf16[4,256,1920]{2,1,0:T(8,128)(2,1)} %get-tuple-element.16.values_ref.keys_ref.steps_ref.rest_0_.rest_1_, ...), custom_call_target="tpu_custom_call" | custom-call | flops 5662310400 | bytes 16777216 | tf_op jit(solution)/shard_map/pallas_call | solution.py:587
  151.5 1.2 reshape.24
  152.6 0.7 broadcast_in_dim.32
  153.4 1.1 pad_maximum_fusion.1
  154.5 11.6 %all-to-all-start.2 = ((f32[32,64,128]{2,1,0:T(8,128)}), f32[32,64,128]{2,1,0:T(8,128)S(1)}, u32[]{:S(2)}, u32[]{:S(2)}) async-start(f32[32,64,128]{2,1,0:T(8,128)} %pad_maximum_fusion.1), calls=%async_computation.2 | async-start | bytes 2097152 | tf_op jit(solution)/shard_map/all_to_all | solution.py:646
  166.1 9.0 %shard_map.83 = (f32[128,1536]{1,0:T(8,128)}, f32[16,128]{1,0:T(8,128)}) custom-call(f32[1,960,1536]{2,1,0:T(8,128)} %bitcast.14, f32[1,960,384]{2,1,0:T(8,128)} %bitcast.16, f32[1,960,384]{2,1,0:T(8,128)} %bitcast.17, f32[1,128]{1,0:T(1,128)} %get-tuple-element.20.rest_0_.rest_1_), custom_call_target="tpu_custom_call" | custom-call | flops 5662310400 | bytes 16777216 | tf_op jit(solution)/shard_map/pallas_call | solution.py:587
  175.1 1.2 reshape.22
  176.3 0.7 broadcast_in_dim.30
  177.0 1.1 pad_maximum_fusion
  178.1 7.1 %all-to-all-done.2.source_ref = f32[32,64,128]{2,1,0:T(8,128)S(1)} async-done(((f32[32,64,128]{2,1,0:T(8,128)}), f32[32,64,128]{2,1,0:T(8,128)S(1)}, u32[]{:S(2)}, u32[]{:S(2)}) %all-to-all-start.2) | async-done | bytes 1048608 | tf_op jit(solution)/shard_map/all_to_all | solution.py:646
  185.3 5.1 %all-to-all-start = ((f32[32,64,128]{2,1,0:T(8,128)}), f32[32,64,128]{2,1,0:T(8,128)S(1)}, u32[]{:S(2)}, u32[]{:S(2)}) async-start(f32[32,64,128]{2,1,0:T(8,128)} %pad_maximum_fusion), calls=%async_computation | async-start | bytes 2097152 | tf_op jit(solution)/shard_map/all_to_all | solution.py:646
  190.4 2.2 shard_map.87
  192.5 14.9 %all-to-all-done.source_ref = f32[32,64,128]{2,1,0:T(8,128)S(1)} async-done(((f32[32,64,128]{2,1,0:T(8,128)}), f32[32,64,128]{2,1,0:T(8,128)S(1)}, u32[]{:S(2)}, u32[]{:S(2)}) %all-to-all-start) | async-done | bytes 1048608 | tf_op jit(solution)/shard_map/all_to_all | solution.py:646
  207.5 5.8 %all-to-all-start.3 = ((f32[32,48,128]{2,1,0:T(8,128)}), f32[32,48,128]{2,1,0:T(8,128)S(1)}, u32[]{:S(2)}, u32[]{:S(2)}) async-start(f32[32,48,128]{2,1,0:T(8,128)} %shard_map.87), calls=%async_computation.3 | async-start | bytes 1572864 | tf_op jit(solution)/shard_map/all_to_all | solution.py:652
  214.0 0.7 broadcast_in_dim_reshape.3.rest_3_
  214.6 2.2 shard_map.84
  216.8 9.8 %all-to-all-done.3 = f32[32,48,128]{2,1,0:T(8,128)S(1)} async-done(((f32[32,48,128]{2,1,0:T(8,128)}), f32[32,48,128]{2,1,0:T(8,128)S(1)}, u32[]{:S(2)}, u32[]{:S(2)}) %all-to-all-start.3) | async-done | bytes 786464 | tf_op jit(solution)/shard_map/all_to_all | solution.py:652
  226.6 5.5 %all-to-all-start.1 = ((f32[32,48,128]{2,1,0:T(8,128)}), f32[32,48,128]{2,1,0:T(8,128)S(1)}, u32[]{:S(2)}, u32[]{:S(2)}) async-start(f32[32,48,128]{2,1,0:T(8,128)} %shard_map.84), calls=%async_computation.1 | async-start | bytes 1572864 | tf_op jit(solution)/shard_map/all_to_all | solution.py:652
  232.1 1.0 reshape.25.rest_3_
  233.1 25.0 %shard_map.88 = bf16[4,256,1536]{2,1,0:T(8,128)(2,1)} custom-call(bf16[4,256,1920]{2,1,0:T(8,128)(2,1)} %get-tuple-element.16.values_ref.keys_ref.steps_ref.rest_0_.rest_1_, bf16[4,256,1920]{2,1,0:T(8,128)(2,1)} %get-tuple-element.16.values_ref.keys_ref.steps_ref.rest_0_.rest_1_, ...), custom_call_target="tpu_custom_call" | custom-call | flops 16986931200 | bytes 33554432 | tf_op jit(solution)/shard_map/pallas_call | solution.py:608
  258.1 0.9 copy-done.3
  259.0 4.8 %all-to-all-start.4 = ((bf16[4,256,1536]{2,1,0:T(8,128)(2,1)}), bf16[4,256,1536]{2,1,0:T(8,128)(2,1)S(1)}, u32[]{:S(2)}, u32[]{:S(2)}) async-start(bf16[4,256,1536]{2,1,0:T(8,128)(2,1)} %shard_map.88), calls=%async_computation.4 | async-start | bytes 6291456 | tf_op jit(solution)/shard_map/all_to_all | solution.py:739
  263.8 2.1 reshape.23.rest_2_
  265.9 21.5 %shard_map.85 = f32[1,960,1536]{2,1,0:T(8,128)} custom-call(f32[1,960,1536]{2,1,0:T(8,128)} %bitcast.15, f32[1,960,384]{2,1,0:T(8,128)} %bitcast.18, f32[1,960,384]{2,1,0:T(8,128)} %bitcast.19, f32[1,960,384]{2,1,0:T(8,128)} %bitcast.20, f32[1,128]{1,0:T(1,128)} %get-tuple-element.20.rest_0_.rest_1_, f32[128,1536]{1,0:T(8,128)} %reshape.23.rest_2_, ...), custom_call_target="tpu_custom_call" | custom-call | flops 16986931200 | bytes 33554432 | tf_op jit(solution)/shard_map/pallas_call | solution.py:608
  287.5 15.3 %fusion.5.gate_ref = f32[960,1536]{1,0:T(8,128)} fusion(bf16[960,3072]{1,0:T(8,128)(2,1)} %bitcast.12, bf16[3072,1536]{1,0:T(8,128)(2,1)} %all-gather.2.cloned.1.call-done), kind=kOutput, calls=%fused_computation.13 | convolution fusion | flops 9059696640 | bytes 21233664 | tf_op jit(solution)/shard_map/dot_general | solution.py:743
  302.8 1.6 copy-done
  304.4 10.8 %shard_map.89 = bf16[960,1536]{1,0:T(8,128)(2,1)} custom-call(f32[960,1536]{1,0:T(8,128)} %bitcast.13, bf16[4,256,1536]{2,1,0:T(8,128)(2,1)} %copy-done, f32[960,1536]{1,0:T(8,128)} %fusion.5.gate_ref, f32[1,1536]{1,0:T(1,128)} %broadcast_in_dim.33.gain_ref), custom_call_target="tpu_custom_call" | custom-call | tf_op jit(solution)/shard_map/pallas_call | solution.py:694
  (23 shorter events, 2.0 us)
Async XLA Ops:
  6.5 134.5 %copy-start.5 = (f32[2,24]{1,0:T(2,128)S(1)}, f32[2,24]{1,0:T(2,128)}, u32[]{:S(2)}) copy-start(f32[2,24]{1,0:T(2,128)} %param.13) | copy-start | bytes 580
  6.5 280.9 %all-gather.2.cloned.1.call-start = ((), (), s32[]{:S(2)}) async-start(), calls=%async_computation.5 | async-start | bytes 10027008 | tf_op jit(solution)/shard_map/all_gather | solution.py:722
  154.5 30.8 %all-to-all-start.2 = ((f32[32,64,128]{2,1,0:T(8,128)}), f32[32,64,128]{2,1,0:T(8,128)S(1)}, u32[]{:S(2)}, u32[]{:S(2)}) async-start(f32[32,64,128]{2,1,0:T(8,128)} %pad_maximum_fusion.1), calls=%async_computation.2 | async-start | bytes 2097152 | tf_op jit(solution)/shard_map/all_to_all | solution.py:646
  175.1 38.2 %copy-start.4 = (f32[1536]{0:T(1024)S(1)}, f32[1536]{0:T(1024)}, u32[]{:S(2)}) copy-start(f32[1536]{0:T(1024)} %param.15) | copy-start | bytes 18436
  175.1 38.8 %copy-start.6 = (f32[2,24]{1,0:T(2,128)S(1)}, f32[2,24]{1,0:T(2,128)}, u32[]{:S(2)}) copy-start(f32[2,24]{1,0:T(2,128)} %param.14) | copy-start | bytes 580
  185.3 5.1 %copy-start.1 = (f32[32,64,128]{2,1,0:T(8,128)}, f32[32,64,128]{2,1,0:T(8,128)S(1)}, u32[]{:S(2)}) copy-start(f32[32,64,128]{2,1,0:T(8,128)S(1)} %all-to-all-done.2.source_ref) | copy-start | bytes 3145732
  185.3 22.2 %all-to-all-start = ((f32[32,64,128]{2,1,0:T(8,128)}), f32[32,64,128]{2,1,0:T(8,128)S(1)}, u32[]{:S(2)}, u32[]{:S(2)}) async-start(f32[32,64,128]{2,1,0:T(8,128)} %pad_maximum_fusion), calls=%async_computation | async-start | bytes 2097152 | tf_op jit(solution)/shard_map/all_to_all | solution.py:646
  207.5 7.2 %copy-start.2 = (f32[32,64,128]{2,1,0:T(8,128)}, f32[32,64,128]{2,1,0:T(8,128)S(1)}, u32[]{:S(2)}) copy-start(f32[32,64,128]{2,1,0:T(8,128)S(1)} %all-to-all-done.source_ref) | copy-start | bytes 3145732
  207.5 19.1 %all-to-all-start.3 = ((f32[32,48,128]{2,1,0:T(8,128)}), f32[32,48,128]{2,1,0:T(8,128)S(1)}, u32[]{:S(2)}, u32[]{:S(2)}) async-start(f32[32,48,128]{2,1,0:T(8,128)} %shard_map.87), calls=%async_computation.3 | async-start | bytes 1572864 | tf_op jit(solution)/shard_map/all_to_all | solution.py:652
  226.6 31.5 %all-to-all-start.1 = ((f32[32,48,128]{2,1,0:T(8,128)}), f32[32,48,128]{2,1,0:T(8,128)S(1)}, u32[]{:S(2)}, u32[]{:S(2)}) async-start(f32[32,48,128]{2,1,0:T(8,128)} %shard_map.84), calls=%async_computation.1 | async-start | bytes 1572864 | tf_op jit(solution)/shard_map/all_to_all | solution.py:652
  258.1 0.9 copy-start.3
  259.0 43.8 %all-to-all-start.4 = ((bf16[4,256,1536]{2,1,0:T(8,128)(2,1)}), bf16[4,256,1536]{2,1,0:T(8,128)(2,1)S(1)}, u32[]{:S(2)}, u32[]{:S(2)}) async-start(bf16[4,256,1536]{2,1,0:T(8,128)(2,1)} %shard_map.88), calls=%async_computation.4 | async-start | bytes 6291456 | tf_op jit(solution)/shard_map/all_to_all | solution.py:739
  302.8 1.6 copy-start
Sparse Core Ops, SparseCore 0:
  9.1 86.9 all-gather.1

commit v3 on v2

--- a/solution.py
+++ b/solution.py
@@ -70,15 +70,62 @@
     return even, odd
 
 
+def earlier_mask(size, column_rows):
+    shape = (size, size)
+    t, s = rows_iota(shape), lanes_iota(shape)
+    if column_rows:
+
+        def place(index):
+            return size - 1 - (lax.rem(index, GROUP) * column_rows + index // GROUP)
+
+        t, s = place(t), place(s)
+    return s <= t
+
+
+def running_logs(steps, rate, earlier):
+    logs = -steps * rate
+    high, rest = split(logs)
+    middle = logs - high.astype(F32)
+    middle, low = split(middle)
+    before = jnp.where(earlier, 1.0, 0.0).astype(BF16)
+    running = dot(before, high) + dot(before, middle) + dot(before, low)
+    return running, jnp.sum(logs, axis=0, keepdims=True)
+
+
+def advance(memory, keys_t, weighted, decay):
+    keys_high, keys_low = keys_t
+    high, low = split(weighted)
+    both = dot(keys_high, jnp.concatenate([high, low], axis=1))
+    added = both[:, :LANES] + both[:, LANES:] + dot(keys_low, high)
+    return memory * decay + added
+
+
+def fold_chunk(values, keys, steps, rate, earlier, head_size, memory_ref, total_ref):
+    keys_t = split(jnp.transpose(keys))
+    running, total = running_logs(steps, rate, earlier)
+    coefficient = steps * jnp.exp(jnp.minimum(total - running, 0.0))
+    decay = jnp.exp(total)
+    for pair in range(memory_ref.shape[1] // LANES):
+        lanes = pl.ds(pair * LANES, LANES)
+        weighted = values(pair) * spread(coefficient, pair, head_size)
+        memory_ref[:, lanes] = advance(
+            memory_ref[:, lanes], keys_t, weighted, spread(decay, pair, head_size)
+        )
+    total_ref[...] = total_ref[...] + total
+
+
 def project_kernel(
     geometry,
     tokens_ref,
     state_ref,
     bias_ref,
+    rate_ref,
     xz_ref,
     values_ref,
     keys_ref,
     columns_ref,
+    memory_ref,
+    total_ref,
     weight,
     product,
     middle,
@@ -94,7 +141,7 @@
     move_own,
     out_sem,
 ):
-    row_part, col_total, inner, depth, blocks = geometry
+    row_part, col_total, inner, depth, blocks, head_size = geometry
     half = depth // 2
     frame, place, part = lax.axis_index("frame"), lax.axis_index("spatial"), lax.axis_index("dp")
     core, y = part % 2, (frame % 2) * 2 + part // 2
@@ -189,7 +236,6 @@
 
     def relay(block):
         from_left, from_right = slot(left, core, same), slot(right, core, same)
-        far = slot(across, core, same)
         for which, index in ((1, from_left), (2, from_right)):
             arrived(
                 view(block, index, 0, depth),
@@ -206,6 +252,8 @@
             )
             send_y(block, which, lambda first: view(block, index, first, half))
             send_core(block, which, index, view(block, index, 0, depth))
+    def relay_far(block):
+        far = slot(across, core, same)
         for part_at in (0, 1):
             arrived(
                 view(block, far, part_at * half, half),
@@ -245,9 +293,7 @@
     def compute(block):
         start, width = blocks[block]
         lanes = pl.ds(0, width)
-        buffer = block % 2
-        if block - 2 in outs:
-            outs.pop(block - 2).wait()
+        buffer = block
 
         def one_tile(i, largest):
             at = pl.ds(pl.multiple_of(i * tile, tile), tile)
@@ -321,17 +367,43 @@
         pltpu.make_async_copy(middle.at[block, place, :, lanes], into, move_own.at[block]).start()
 
     count = len(blocks)
-    send_own(0)
-    send_own(1)
+    for block in range(count):
+        send_own(block)
     relay(0)
+    relay(1)
+    relay_far(0)
     for block in range(count):
         if block + 2 < count:
-            send_own(block + 2)
+            relay(block + 2)
         if block + 1 < count:
-            relay(block + 1)
+            relay_far(block + 1)
         pass_on(block)
         gathered(block)
         compute(block)
+
+    memory_ref[...] = jnp.zeros_like(memory_ref)
+    total_ref[...] = jnp.zeros_like(total_ref)
+
+    def fold_rows(step, carry):
+        at = pl.ds(pl.multiple_of(step * tile, 16), tile)
+        block_pairs = blocks[1][1] // LANES
+
+        def values(pair):
+            return product[1 + pair // block_pairs, at, pl.ds(pair % block_pairs * LANES, LANES)]
+
+        fold_chunk(
+            values,
+            product[0, at, pl.ds(0, LANES)],
+            product[0, at, pl.ds(2 * LANES, LANES)],
+            rate_ref[...],
+            earlier_mask(tile, 0),
+            head_size,
+            memory_ref,
+            total_ref,
+        )
+        return carry
+
+    lax.fori_loop(0, 5, fold_rows, 0)
     for block in range(count):
         start, width = blocks[block]
         lanes = pl.ds(0, width)
@@ -346,7 +418,7 @@
         copy.wait_send()
 
 
-def project(tokens, state_weight, bias, xz_weight, row_part, col_total, inner, block_width):
+def project(tokens, state_weight, bias, rate, xz_weight, row_part, col_total, inner, head_size, block_width):
     depth, state_width = state_weight.shape
     count = inner // block_width + 1
     blocks = ((0, state_width),) + tuple((k * block_width, block_width) for k in range(count - 1))
@@ -356,17 +428,19 @@
     vmem, hbm = pl.BlockSpec(memory_space=pltpu.VMEM), pl.BlockSpec(memory_space=pl.ANY)
     dma = pltpu.SemaphoreType.DMA
     return pl.pallas_call(
-        functools.partial(project_kernel, (row_part, col_total, inner, depth, blocks)),
-        in_specs=[vmem, vmem, vmem, hbm],
-        out_specs=[hbm, hbm, hbm],
+        functools.partial(project_kernel, (row_part, col_total, inner, depth, blocks, head_size)),
+        in_specs=[vmem, vmem, vmem, vmem, hbm],
+        out_specs=[hbm, hbm, hbm, vmem, vmem],
         out_shape=[
             jax.ShapeDtypeStruct((total, inner), F32),
             jax.ShapeDtypeStruct((total, state_width), F32),
             jax.ShapeDtypeStruct((4, piece_rows, inner + state_width), BF16),
+            jax.ShapeDtypeStruct((LANES, inner), F32),
+            jax.ShapeDtypeStruct((8, LANES), F32),
         ],
         scratch_shapes=[
             pltpu.VMEM((count, tokens.shape[1], width), BF16),
-            pltpu.VMEM((2, total, width), F32),
+            pltpu.VMEM((count, total, width), F32),
             pltpu.VMEM((count, 4, piece_rows, width), BF16),
             dma((count,)),
             dma((count, 4)),
@@ -383,37 +457,7 @@
         compiler_params=pltpu.CompilerParams(
             collective_id=0, has_side_effects=True, vmem_limit_bytes=VMEM_BYTES
         ),
-    )(tokens, state_weight, bias, xz_weight)
-
-
-def earlier_mask(size, column_rows):
-    shape = (size, size)
-    t, s = rows_iota(shape), lanes_iota(shape)
-    if column_rows:
-
-        def place(index):
-            return size - 1 - (lax.rem(index, GROUP) * column_rows + index // GROUP)
-
-        t, s = place(t), place(s)
-    return s <= t
-
-
-def running_logs(steps, rate, earlier):
-    logs = -steps * rate
-    high, rest = split(logs)
-    middle = logs - high.astype(F32)
-    middle, low = split(middle)
-    before = jnp.where(earlier, 1.0, 0.0).astype(BF16)
-    running = dot(before, high) + dot(before, middle) + dot(before, low)
-    return running, jnp.sum(logs, axis=0, keepdims=True)
-
-
-def advance(memory, keys_t, weighted, decay):
-    keys_high, keys_low = keys_t
-    high, low = split(weighted)
-    both = dot(keys_high, jnp.concatenate([high, low], axis=1))
-    added = both[:, :LANES] + both[:, LANES:] + dot(keys_low, high)
-    return memory * decay + added
+    )(tokens, state_weight, bias, rate, xz_weight)
 
 
 class Chunk:
@@ -457,29 +501,6 @@
 
     def earlier(self):
         return earlier_mask(self.size, self.column_rows)
-
-
-def state_kernel(column_rows, head_size, values_ref, keys_ref, steps_ref, *rest):
-    scale_ref = rest[0] if column_rows else None
-    rate_ref, memory_ref, decay_ref = rest[-3:]
-    chunk = Chunk(column_rows, values_ref, keys_ref, steps_ref, scale_ref)
-
-    @pl.when(pl.program_id(0) == 0)
-    def _():
-        memory_ref[...] = jnp.zeros_like(memory_ref)
-        decay_ref[...] = jnp.ones_like(decay_ref)
-
-    steps = chunk.steps()
-    keys_t = split(jnp.transpose(chunk.keys()))
-    running, total = running_logs(steps, rate_ref[...], chunk.earlier())
-    coefficient = steps * jnp.exp(jnp.minimum(total - running, 0.0))
-    decay = jnp.exp(total)
-    for pair in range(chunk.pairs):
-        lanes = pl.ds(pair * LANES, LANES)
-        weighted = chunk.values(pair) * spread(coefficient, pair, head_size)
-        pair_decay = spread(decay, pair, head_size)
-        memory_ref[:, lanes] = advance(memory_ref[:, lanes], keys_t, weighted, pair_decay)
-        decay_ref[pl.ds(pair, 1), :] = decay_ref[pl.ds(pair, 1), :] * pair_decay
 
 
 def output_kernel(column_rows, head_size, values_ref, keys_ref, steps_ref, *rest):
@@ -582,22 +603,6 @@
     )
 
 
-def local_state(sources, rate, inner, size, column_rows, head_size):
-    count, specs, arrays, _ = chunk_specs(sources, inner, size, column_rows)
-    return pl.pallas_call(
-        functools.partial(state_kernel, column_rows, head_size),
-        grid=(count,),
-        in_specs=specs + [whole((1, LANES))],
-        out_specs=[whole((LANES, inner)), whole((16, LANES))],
-        out_shape=[
-            jax.ShapeDtypeStruct((LANES, inner), F32),
-            jax.ShapeDtypeStruct((16, LANES), F32),
-        ],
-        cost_estimate=estimate(count * size, inner, 10, 16 << 20),
-        compiler_params=params(),
-    )(*arrays, rate)
-
-
 def local_output(sources, rate, entering, skip, inner, size, column_rows, head_size):
     count, specs, arrays, queries = chunk_specs(sources, inner, size, column_rows)
     shape = sources[0].shape[:2] + (inner,)
@@ -619,38 +624,203 @@
     )(*arrays, sources[-1], rate, entering, *extra)
 
 
-def prefix_kernel(reverse, rows, pairs, source_ref, out_ref):
-    count = source_ref.shape[0]
-    entering = jnp.zeros((rows, LANES), F32)
-    for k in range(count):
-        at = count - 1 - k if reverse else k
-        out_ref[at] = entering
-        decay = source_ref[at, pl.ds(rows, pairs), :]
-        decay = jnp.concatenate([decay] * (rows // pairs), axis=0)
-        entering = entering * decay + source_ref[at, pl.ds(0, rows), :]
-
-
-def entering_state(memory, decay, axes, reverse):
-    count = 1
-    for axis in axes:
-        count = count * lax.axis_size(axis)
-    pairs = memory.shape[1] // LANES
-    rows = memory.shape[0] * pairs // count
-    sent = jnp.concatenate(
-        [
-            memory.reshape(count, rows, LANES),
-            jnp.broadcast_to(decay[None], (count,) + decay.shape),
+def states_kernel(
+    geometry,
+    columns_ref,
+    rate_ref,
+    forward_ref,
+    forward_total_ref,
+    entering_forward_ref,
+    entering_backward_ref,
+    memory,
+    total,
+    sent,
+    received,
+    found,
+    out_send,
+    out_recv,
+    back_send,
+    back_recv,
+    own_sem,
+):
+    inner, size, column_rows, head_size, count, spatial = geometry
+    slices = count // 2
+    rows, wide = LANES // slices, inner // 2
+    pairs = wide // LANES
+    frame, place, part = lax.axis_index("frame"), lax.axis_index("spatial"), lax.axis_index("dp")
+    me = frame * spatial + place
+
+    def device(index):
+        return (index // spatial, index % spatial, part)
+
+    barrier = pltpu.get_barrier_semaphore()
+
+    def greet(k, carry):
+        peer = device((me + k) % count)
+        pl.semaphore_signal(barrier, inc=1, device_id=peer, device_id_type=MESH)
+        return carry
+
+    lax.fori_loop(1, count, greet, 0)
+    pl.semaphore_wait(barrier, count - 1)
+
+    def send_slices(way, memory_ref, total_ref):
+        totals = total_ref[...]
+        shifted = pltpu.roll(totals, LANES - 2 * pairs, 1)
+        for index in range(count):
+            first, lane = rows * (index // 2), wide * (index % 2)
+            sent[way, index, :, pl.ds(0, wide)] = memory_ref[pl.ds(first, rows), pl.ds(lane, wide)]
+            sent[way, index, :, pl.ds(wide, LANES)] = shifted if index % 2 else totals
+
+        def one(k, carry):
+            to = (me + k) % count
+            pltpu.make_async_remote_copy(
+                src_ref=sent.at[way, to],
+                dst_ref=received.at[way, me],
+                send_sem=out_send.at[way, k],
+                recv_sem=out_recv.at[way, k],
+                device_id=device(to),
+                device_id_type=MESH,
+            ).start()
+            return carry
+
+        lax.fori_loop(1, count, one, 0)
+        received[way, me] = sent[way, me]
+
+    def scan(way, reverse, entering_ref):
+        def arrive(k, carry):
+            source = (me + count - k) % count
+            pltpu.make_async_remote_copy(
+                src_ref=received.at[way, source],
+                dst_ref=received.at[way, source],
+                send_sem=out_send.at[way, k],
+                recv_sem=out_recv.at[way, k],
+                device_id=device(source),
+                device_id_type=MESH,
+            ).wait_recv()
+            return carry
+
+        lax.fori_loop(1, count, arrive, 0)
+        entering = jnp.zeros((rows, wide), F32)
+        for k in range(count):
+            at = count - 1 - k if reverse else k
+            found[way, at] = entering
+            decay = jnp.exp(received[way, at, :, pl.ds(wide, LANES)])
+            spreads = [spread(decay, pair, head_size) for pair in range(pairs)]
+            decay = jnp.concatenate(spreads, axis=1)
+            entering = entering * decay + received[way, at, :, pl.ds(0, wide)]
+
+        def one(k, carry):
+            to = (me + k) % count
+            pltpu.make_async_remote_copy(
+                src_ref=found.at[way, to],
+                dst_ref=place_of(entering_ref, me),
+                send_sem=back_send.at[way, k],
+                recv_sem=back_recv.at[way, k],
+                device_id=device(to),
+                device_id_type=MESH,
+            ).start()
+            return carry
+
+        lax.fori_loop(1, count, one, 0)
+        copy = pltpu.make_async_copy(found.at[way, me], place_of(entering_ref, me), own_sem.at[way])
+        copy.start()
+
+    def place_of(entering_ref, index):
+        first = pl.multiple_of(rows * (index // 2), rows)
+        lane = pl.multiple_of(wide * (index % 2), LANES)
+        return entering_ref.at[pl.ds(first, rows), pl.ds(lane, wide)]
+
+    def finish_way(way, entering_ref):
+        def arrive(k, carry):
+            source = (me + count - k) % count
+            to = (me + k) % count
+            pltpu.make_async_remote_copy(
+                src_ref=found.at[way, source],
+                dst_ref=place_of(entering_ref, source),
+                send_sem=back_send.at[way, k],
+                recv_sem=back_recv.at[way, k],
+                device_id=device(to),
+                device_id_type=MESH,
+            ).wait()
+            pltpu.make_async_remote_copy(
+                src_ref=sent.at[way, to],
+                dst_ref=received.at[way, me],
+                send_sem=out_send.at[way, k],
+                recv_sem=out_recv.at[way, k],
+                device_id=device(to),
+                device_id_type=MESH,
+            ).wait_send()
+            return carry
+
+        lax.fori_loop(1, count, arrive, 0)
+        pltpu.make_async_copy(
+            found.at[way, me], place_of(entering_ref, me), own_sem.at[way]
+        ).wait()
+
+    send_slices(0, forward_ref, forward_total_ref)
+    memory[...] = jnp.zeros_like(memory)
+    total[...] = jnp.zeros_like(total)
+    chunks = (columns_ref.shape[1] - 16) // (size // 4)
+    last = columns_ref.shape[1] - 16
+
+    def fold_columns(step, carry):
+        at = pl.ds(pl.multiple_of((chunks - 1 - step) * (size // 4), 16), size // 4)
+        chunk = Chunk(
+            column_rows,
+            columns_ref.at[:, at, pl.ds(0, inner)],
+            columns_ref.at[:, at, pl.ds(inner, LANES)],
+            columns_ref.at[:, at, pl.ds(inner + 2 * LANES, LANES)],
+            columns_ref.at[:, pl.ds(last, 16), :],
+        )
+        fold_chunk(
+            chunk.values,
+            chunk.keys(),
+            chunk.steps(),
+            rate_ref[...],
+            chunk.earlier(),
+            head_size,
+            memory,
+            total,
+        )
+        return carry
+
+    lax.fori_loop(0, chunks, fold_columns, 0)
+    send_slices(1, memory, total)
+    scan(0, False, entering_forward_ref)
+    scan(1, True, entering_backward_ref)
+    finish_way(0, entering_forward_ref)
+    finish_way(1, entering_backward_ref)
+
+
+def entering_states(columns, rate, memory, total, inner, size, column_rows, head_size):
+    spatial = lax.axis_size("spatial")
+    count = lax.axis_size("frame") * spatial
+    rows, wide = LANES * 2 // count, inner // 2
+    vmem, hbm = pl.BlockSpec(memory_space=pltpu.VMEM), pl.BlockSpec(memory_space=pl.ANY)
+    dma = pltpu.SemaphoreType.DMA
+    state = jax.ShapeDtypeStruct((LANES, inner), F32)
+    geometry = (inner, size, column_rows, head_size, count, spatial)
+    return pl.pallas_call(
+        functools.partial(states_kernel, geometry),
+        in_specs=[vmem] * 4,
+        out_specs=[hbm, hbm],
+        out_shape=[state, state],
+        scratch_shapes=[
+            pltpu.VMEM((LANES, inner), F32),
+            pltpu.VMEM((8, LANES), F32),
+            pltpu.VMEM((2, count, rows, wide + LANES), F32),
+            pltpu.VMEM((2, count, rows, wide + LANES), F32),
+            pltpu.VMEM((2, count, rows, wide), F32),
+            dma((2, count)),
+            dma((2, count)),
+            dma((2, count)),
+            dma((2, count)),
+            dma((2,)),
         ],
-        axis=1,
-    )
-    received = lax.all_to_all(sent, axes, 0, 0, tiled=True)
-    found = pl.pallas_call(
-        functools.partial(prefix_kernel, reverse, rows, pairs),
-        out_shape=jax.ShapeDtypeStruct((count, rows, LANES), F32),
-        compiler_params=pltpu.CompilerParams(vmem_limit_bytes=VMEM_BYTES),
-    )(received)
-    returned = lax.all_to_all(found, axes, 0, 0, tiled=True)
-    return returned.reshape(memory.shape)
+        compiler_params=pltpu.CompilerParams(
+            collective_id=1, has_side_effects=True, vmem_limit_bytes=VMEM_BYTES
+        ),
+    )(columns, rate, memory, total)
 
 
 def finish_kernel(head_size, groups, part, forward_ref, backward_ref, gate_ref, gain_ref, out_ref, moved_ref):
@@ -719,20 +889,28 @@
     thrice = pad_lanes(jnp.concatenate([step_weight] * 3, axis=1))
     bias = pad_lanes(jnp.concatenate([step_bias] * 3)[None])
     first_weight = jnp.concatenate([state_weight, thrice], axis=1)
-    gate_weight = lax.all_gather(xz_weight[:, :inner], ("spatial", "dp"), axis=0, tiled=True)
     rates = pad_lanes(decay_rate)
     skips = jnp.repeat(skip[0] + skip[1], head_size)[None]
 
-    values, keys, columns = project(
-        flattened, first_weight, bias, xz_weight, row_part, col_total, inner, 512
+    values, keys, columns, memory, total = project(
+        flattened,
+        first_weight,
+        bias,
+        rates[0:1],
+        xz_weight,
+        row_part,
+        col_total,
+        inner,
+        head_size,
+        512,
     )
+    gate_part, total = lax.optimization_barrier((xz_weight[:, :inner], total))
+    gate_weight = lax.all_gather(gate_part, ("spatial", "dp"), axis=0, tiled=True)
     rowwise = (values[None], keys[None])
     columnwise = (columns,)
-
-    memory, decay = local_state(columnwise, rates[1:2], inner, size, column_rows, head_size)
-    entering = entering_state(memory, decay, axes, True)
-    forward_memory, forward_decay = local_state(rowwise, rates[0:1], inner, size, 0, head_size)
-    forward_entering = entering_state(forward_memory, forward_decay, axes, False)
+    forward_entering, entering = entering_states(
+        columns, rates[1:2], memory, total, inner, size, column_rows, head_size
+    )
     backward = local_output(
         columnwise, rates[1:2], entering, None, inner, size, column_rows, head_size
     )

time: 323 us -> 268 us (0.83)
  waiting for transfers between devices: 31.9 us -> 0.02 us
  starting transfers between devices: 32.7 us -> 5.2 us
  Pallas kernels: 209 us -> 224 us
  local copies, waits for them, and re-layouts: 14.8 us -> 7.63 us
    pallas_call x4 -> x1, Pallas kernels: 23.1 us -> 79.6 us  [entering_states(): pl.pallas_call(functools.partial(states_kernel, geometry), in_specs=[vmem...]
    pallas_call x1, Pallas kernels: 129 us -> 86.4 us  [project(): pl.pallas_call(functools.partial(project_kernel, (row_part, col_total, in...]
    all_to_all x4 -> x0, waiting for transfers between devices: 31.9 us -> none  [the longest x2 22.1 us: entering_state(): received = lax.all_to_all(sent, axes, 0, 0, tiled=True)]
    all_to_all x4 -> x0, starting transfers between devices: 27.9 us -> none  [the longest x2 16.7 us: entering_state(): received = lax.all_to_all(sent, axes, 0, 0, tiled=True)]
    reshape x4 -> x0, local copies, waits for them, and re-layouts: 5.53 us -> none  [the longest x2 3.13 us: entering_state(): return returned.reshape(memory.shape)]
  transfers between devices with their start and end apart: 6 -> 2, of which waited for: 3 -> 0; matrix products, arithmetic and copies ran while one was open for 9% -> 6% of each run, Pallas kernels for 62% -> 47%
where the time goes in v3:
time: 268 us
  Pallas kernels  224 us (84%)
  matrix products  15.2 us (6%)
  between operations  13.4 us (5%)
  local copies, waits for them, and re-layouts  7.63 us (3%)
  starting transfers between devices  5.2 us (2%)
    pallas_call x1, Pallas kernels, project(): pl.pallas_call(functools.partial(project_kernel, (row_part, col_total, in...  86.4 us
    pallas_call x1, Pallas kernels, entering_states(): pl.pallas_call(functools.partial(states_kernel, geometry), in_specs=[vmem...  79.6 us
    pallas_call x2, Pallas kernels, local_output(): pl.pallas_call(functools.partial(output_kernel, column_rows, head_size),...  46.8 us
    dot_general x1, matrix products, local(): gate_rows = jnp.dot(flattened, gate_weight, preferred_element_type=F32)  15.2 us
    pallas_call x1, Pallas kernels, finish(): pl.pallas_call(functools.partial(finish_kernel, head_size, groups, row_pa...  10.8 us
  transfers between devices with their start and end apart: 2, of which 0 were waited for; matrix products, arithmetic and copies ran while one was open for 6% of the time, Pallas kernels for 47%

profile of v3, /device:TPU:2, one launch (start us, length us, event | category | flops | bytes accessed | tf_op | source)
XLA Modules:
  0.0 267.6 jit_solution(15718497942352453641)
XLA Ops:
  6.5 0.0 all-gather.2.cloned.1.call-start
  6.5 1.3 pad_slice_fusion
  7.9 0.8 copy.9
  8.7 0.1 fusion.4
  8.8 0.8 maximum_bitcast_fusion
  9.7 1.9 slice.19
  11.6 1.6 pad_maximum_fusion.state_ref
  13.1 0.6 pad.13.bias_ref
  13.7 86.4 %shard_map.82 = (f32[960,1536]{1,0:T(8,128)}, f32[960,384]{1,0:T(8,128)}, bf16[4,256,1920]{2,1,0:T(8,128)(2,1)}, f32[128,1536]{1,0:T(8,128)}, f32[8,128]{1,0:T(8,128)}) custom-call(bf16[960,3072]{1,0:T(8,128)(2,1)} %bitcast.13, bf16[192,384]{1,0:T(8,128)(2,1)} %pad_maximum_fusion.state_ref, f32[1,128]{1,0:T(1,128)} %pad.13.bias_ref, ...), custom_call_target="tpu_custom_call" | custom-call | tf_op jit(solution)/shard_map/pallas_call | solution.py:430
  100.1 0.0 all-gather.2.cloned.1.call-update
  100.1 79.6 %shard_map.83 = (f32[128,1536]{1,0:T(8,128)}, f32[128,1536]{1,0:T(8,128)}) custom-call(bf16[4,256,1920]{2,1,0:T(8,128)(2,1)} %get-tuple-element.16.columns_ref.values_ref.keys_ref.steps_ref.rest_0_.rest_1_, f32[1,128]{1,0:T(1,128)} %get-tuple-element.23.rate_ref.rest_2_, f32[128,1536]{1,0:T(8,128)} %get-tuple-element.17.forward_ref, ...), custom_call_target="tpu_custom_call" | custom-call | tf_op jit(solution)/shard_map/pallas_call | solution.py:803
  179.7 25.3 %shard_map.85 = bf16[4,256,1536]{2,1,0:T(8,128)(2,1)} custom-call(bf16[4,256,1920]{2,1,0:T(8,128)(2,1)} %get-tuple-element.16.columns_ref.values_ref.keys_ref.steps_ref.rest_0_.rest_1_, bf16[4,256,1920]{2,1,0:T(8,128)(2,1)} %get-tuple-element.16.columns_ref.values_ref.keys_ref.steps_ref.rest_0_.rest_1_, ...), custom_call_target="tpu_custom_call" | custom-call | flops 16986931200 | bytes 33554432 | tf_op jit(solution)/shard_map/pallas_call | solution.py:613
  205.0 0.0 copy-start.2
  205.0 5.2 %all-to-all-start = ((bf16[4,256,1536]{2,1,0:T(8,128)(2,1)}), bf16[4,256,1536]{2,1,0:T(8,128)(2,1)S(1)}, u32[]{:S(2)}, u32[]{:S(2)}) async-start(bf16[4,256,1536]{2,1,0:T(8,128)(2,1)} %shard_map.85), calls=%async_computation | async-start | bytes 6291456 | tf_op jit(solution)/shard_map/all_to_all | solution.py:917
  210.2 0.0 copy-done.2
  210.2 0.1 broadcast_in_dim.18
  210.3 0.7 broadcast_in_dim_reshape.3.rest_3_
  211.0 0.0 copy-start.1
  211.0 21.5 %shard_map.84 = f32[1,960,1536]{2,1,0:T(8,128)} custom-call(f32[1,960,1536]{2,1,0:T(8,128)} %bitcast.16, f32[1,960,384]{2,1,0:T(8,128)} %bitcast.17, f32[1,960,384]{2,1,0:T(8,128)} %bitcast.18, f32[1,960,384]{2,1,0:T(8,128)} %bitcast.19, f32[1,128]{1,0:T(1,128)} %get-tuple-element.24.rate_ref.rest_1_, f32[128,1536]{1,0:T(8,128)} %get-tuple-element.20.rest_2_, ...), custom_call_target="tpu_custom_call" | custom-call | flops 16986931200 | bytes 33554432 | tf_op jit(solution)/shard_map/pallas_call | solution.py:613
  232.5 0.0 copy-done.1
  232.5 0.6 broadcast_in_dim.19.gain_ref
  233.1 0.0 all-gather.2.cloned.1.call-done
  233.1 15.2 %convolution_bitcast_fusion.gate_ref = f32[960,1536]{1,0:T(8,128)} fusion(bf16[960,3072]{1,0:T(8,128)(2,1)} %bitcast.14, bf16[3072,1536]{1,0:T(8,128)(2,1)} %all-gather.2.cloned.1.call-done), kind=kOutput, calls=%fused_computation | convolution fusion | flops 9059696640 | bytes 21233664 | tf_op jit(solution)/shard_map/dot_general | solution.py:921
  248.3 0.0 all-to-all-done.backward_ref
  248.3 0.0 copy-start
  248.3 1.6 copy-done
  250.0 10.8 %shard_map.86 = bf16[960,1536]{1,0:T(8,128)(2,1)} custom-call(f32[960,1536]{1,0:T(8,128)} %bitcast.15, bf16[4,256,1536]{2,1,0:T(8,128)(2,1)} %copy-done, f32[960,1536]{1,0:T(8,128)} %convolution_bitcast_fusion.gate_ref, f32[1,1536]{1,0:T(1,128)} %broadcast_in_dim.19.gain_ref), custom_call_target="tpu_custom_call" | custom-call | tf_op jit(solution)/shard_map/pallas_call | solution.py:864
  (1 shorter events, 0.0 us)
Async XLA Ops:
  6.5 226.6 %all-gather.2.cloned.1.call-start = ((), (), s32[]{:S(2)}) async-start(), calls=%async_computation.1 | async-start | bytes 10027008 | tf_op jit(solution)/shard_map/all_gather | solution.py:908
  205.0 5.2 %copy-start.2 = (f32[2,24]{1,0:T(2,128)S(1)}, f32[2,24]{1,0:T(2,128)}, u32[]{:S(2)}) copy-start(f32[2,24]{1,0:T(2,128)} %param.14) | copy-start | bytes 580
  205.0 43.3 %all-to-all-start = ((bf16[4,256,1536]{2,1,0:T(8,128)(2,1)}), bf16[4,256,1536]{2,1,0:T(8,128)(2,1)S(1)}, u32[]{:S(2)}, u32[]{:S(2)}) async-start(bf16[4,256,1536]{2,1,0:T(8,128)(2,1)} %shard_map.85), calls=%async_computation | async-start | bytes 6291456 | tf_op jit(solution)/shard_map/all_to_all | solution.py:917
  211.0 21.5 %copy-start.1 = (f32[1536]{0:T(1024)S(1)}, f32[1536]{0:T(1024)}, u32[]{:S(2)}) copy-start(f32[1536]{0:T(1024)} %param.15) | copy-start | bytes 18436
  248.3 1.6 copy-start
Sparse Core Ops, SparseCore 0:
  100.3 92.6 all-gather.1

commit v4 on v3

--- a/solution.py
+++ b/solution.py
@@ -114,6 +114,40 @@
     total_ref[...] = total_ref[...] + total
 
 
+def in_order(ref, depth):
+    parts = []
+    for row in range(16):
+        where, part, core = row // 4, (row // 2) % 2, row % 2
+        parts.append(ref[pl.ds((core * 8 + part * 4 + where) * depth, depth), :])
+    return jnp.concatenate(parts, axis=0)
+
+
+def gate_kernel(depth, tokens_ref, weight_ref, gate_ref):
+    width = weight_ref.shape[2]
+    for quarter in range(0, 4, 2):
+        weight = jnp.concatenate(
+            [in_order(weight_ref.at[quarter + k], depth) for k in range(2)], axis=1
+        )
+        gate_ref[:, pl.ds(quarter * width, 2 * width)] = dot(tokens_ref[...], weight)
+
+
+def gate_rows_of(tokens, weight, depth):
+    total, model = tokens.shape
+    inner = 4 * weight.shape[2]
+    tile = total // 5
+    return pl.pallas_call(
+        functools.partial(gate_kernel, depth),
+        grid=(5,),
+        in_specs=[pl.BlockSpec((tile, model), lambda m: (m, 0)), whole(weight.shape)],
+        out_specs=pl.BlockSpec((tile, inner), lambda m: (m, 0)),
+        out_shape=jax.ShapeDtypeStruct((total, inner), F32),
+        cost_estimate=pl.CostEstimate(
+            flops=2 * total * model * inner, bytes_accessed=20 << 20, transcendentals=0
+        ),
+        compiler_params=params(),
+    )(tokens, weight)
+
+
 def project_kernel(
     geometry,
     tokens_ref,
@@ -126,7 +160,9 @@
     columns_ref,
     memory_ref,
     total_ref,
+    gate_ref,
     weight,
+    gate_weight,
     product,
     middle,
     own_sem,
@@ -140,6 +176,9 @@
     move_recv,
     move_own,
     out_sem,
+    gate_send,
+    gate_recv,
+    gate_out,
 ):
     row_part, col_total, inner, depth, blocks, head_size = geometry
     half = depth // 2
@@ -147,6 +186,11 @@
     core, y = part % 2, (frame % 2) * 2 + part // 2
     right, left, across = (place + 1) % 4, (place + 3) % 4, (place + 2) % 4
 
+    z = frame // 2
+
+    def z_device(other):
+        return (other * 2 + frame % 2, place, part)
+
     def y_device(other):
         return ((frame // 2) * 2 + other // 2, place, (other % 2) * 2 + core)
 
@@ -155,13 +199,14 @@
     partner = (frame, place, (part // 2) * 2 + 1 - core)
 
     barrier = pltpu.get_barrier_semaphore()
-    peers = (x_right, x_left, x_across, y_up, y_down, partner)
+    z_up, z_down = z_device((z + 1) % 4), z_device((z + 3) % 4)
+    peers = (x_right, x_left, x_across, y_up, y_down, z_up, z_down, partner)
     for peer in peers:
         pl.semaphore_signal(barrier, inc=1, device_id=peer, device_id_type=MESH)
     pl.semaphore_wait(barrier, len(peers))
 
     def slot(where, other_core, other_part):
-        return where * 4 + other_part * 2 + other_core
+        return other_core * 8 + other_part * 4 + where
 
     same, opposite = part // 2, 1 - part // 2
     sources = (place, left, right, across)
@@ -284,6 +329,69 @@
         target = view(block, index, 0, depth)
         pltpu.make_async_copy(own(block, 0, depth), target, own_sem.at[block]).wait()
 
+
+    quarter_width = gate_weight.shape[2]
+    many, core_rows = 4 * depth, 8 * depth
+
+    def gate_view(quarter, first, rows_count):
+        return gate_weight.at[quarter, pl.ds(pl.multiple_of(first, 16), rows_count), :]
+
+    def gate_copy(source, at, device):
+        send(source, source, gate_send.at[at], gate_recv.at[at], device)
+
+    def gate_arrived(target, at):
+        arrived(target, gate_send.at[at], gate_recv.at[at])
+
+    def gate_own():
+        first = pl.multiple_of(z * quarter_width, LANES)
+        return xz_ref.at[:, pl.ds(first, quarter_width)]
+
+    def gate_start():
+        target = gate_view(z, slot(place, core, same) * depth, depth)
+        send(gate_own(), target, gate_send.at[0], gate_recv.at[0], x_right)
+        send(gate_own(), target, gate_send.at[1], gate_recv.at[1], x_left)
+        pltpu.make_async_copy(gate_own(), target, own_sem.at[len(blocks)]).start()
+
+    def gate_x():
+        for at, index in ((0, slot(left, core, same)), (1, slot(right, core, same))):
+            gate_arrived(gate_view(z, index * depth, depth), at)
+            gate_copy(gate_view(z, index * depth + at * half, half), 2 + at, (x_right, x_left)[at])
+
+    def gate_y():
+        far = slot(across, core, same) * depth
+        for at in (0, 1):
+            gate_arrived(gate_view(z, far + at * half, half), 2 + at)
+        target = gate_view(z, slot(place, core, same) * depth, depth)
+        pltpu.make_async_copy(gate_own(), target, own_sem.at[len(blocks)]).wait()
+        first = slot(0, core, same) * depth
+        for at, device in ((0, y_up), (1, y_down)):
+            gate_copy(gate_view(z, first + at * (many // 2), many // 2), 4 + at, device)
+
+    def gate_z():
+        first = slot(0, core, opposite) * depth
+        for at in (0, 1):
+            gate_arrived(gate_view(z, first + at * (many // 2), many // 2), 4 + at)
+        mine = gate_view(z, core * core_rows, core_rows)
+        gate_copy(mine, 6, z_up)
+        gate_copy(mine, 7, z_down)
+        gate_copy(mine, 10, partner)
+
+    def gate_pass():
+        for at, quarter in ((0, (z + 3) % 4), (1, (z + 1) % 4)):
+            mine = gate_view(quarter, core * core_rows, core_rows)
+            gate_arrived(mine, 6 + at)
+            part_rows = gate_view(quarter, core * core_rows + at * many, many)
+            gate_copy(part_rows, 8 + at, (z_up, z_down)[at])
+            gate_copy(mine, 11 + at, partner)
+
+    def gate_end():
+        quarter = (z + 2) % 4
+        for at in (0, 1):
+            gate_arrived(gate_view(quarter, core * core_rows + at * many, many), 8 + at)
+        gate_copy(gate_view(quarter, core * core_rows, core_rows), 13, partner)
+        for at, quarter in enumerate((z, (z + 3) % 4, (z + 1) % 4, (z + 2) % 4)):
+            gate_arrived(gate_view(quarter, (1 - core) * core_rows, core_rows), 10 + at)
+
     tokens = row_part * col_total
     tile = tokens // 5
     groups = col_total // GROUP // 4
@@ -297,7 +405,7 @@
 
         def one_tile(i, largest):
             at = pl.ds(pl.multiple_of(i * tile, tile), tile)
-            result = dot(tokens_ref[at, :], weight[block, :, lanes])
+            result = dot(tokens_ref[at, :], in_order(weight.at[block, :, lanes], depth))
             if block == 0:
                 raw = result[:, width - LANES :] + bias_ref[...]
                 steps = jnp.maximum(raw, 0.0) + jnp.log1p(jnp.exp(-jnp.abs(raw)))
@@ -369,18 +477,23 @@
     count = len(blocks)
     for block in range(count):
         send_own(block)
+    gate_start()
     relay(0)
     relay(1)
+    gate_x()
     relay_far(0)
     for block in range(count):
         if block + 2 < count:
             relay(block + 2)
         if block + 1 < count:
             relay_far(block + 1)
+        if block < 2:
+            (gate_y, gate_z)[block]()
         pass_on(block)
         gathered(block)
         compute(block)
 
+    gate_pass()
     memory_ref[...] = jnp.zeros_like(memory_ref)
     total_ref[...] = jnp.zeros_like(total_ref)
 
@@ -404,6 +517,13 @@
         return carry
 
     lax.fori_loop(0, 5, fold_rows, 0)
+    gate_end()
+    gate_copies = [
+        pltpu.make_async_copy(gate_weight.at[quarter], gate_ref.at[quarter], gate_out.at[quarter])
+        for quarter in range(4)
+    ]
+    for copy in gate_copies:
+        copy.start()
     for block in range(count):
         start, width = blocks[block]
         lanes = pl.ds(0, width)
@@ -412,7 +532,7 @@
             arrived(into, move_send.at[block, at], move_recv.at[block, at])
         into = columns_ref.at[place, :, pl.ds(inner if block == 0 else start, width)]
         pltpu.make_async_copy(middle.at[block, place, :, lanes], into, move_own.at[block]).wait()
-    for copy in outs.values():
+    for copy in list(outs.values()) + gate_copies:
         copy.wait()
     for copy in pending:
         copy.wait_send()
@@ -430,19 +550,21 @@
     return pl.pallas_call(
         functools.partial(project_kernel, (row_part, col_total, inner, depth, blocks, head_size)),
         in_specs=[vmem, vmem, vmem, vmem, hbm],
-        out_specs=[hbm, hbm, hbm, vmem, vmem],
+        out_specs=[hbm, hbm, hbm, vmem, vmem, hbm],
         out_shape=[
             jax.ShapeDtypeStruct((total, inner), F32),
             jax.ShapeDtypeStruct((total, state_width), F32),
             jax.ShapeDtypeStruct((4, piece_rows, inner + state_width), BF16),
             jax.ShapeDtypeStruct((LANES, inner), F32),
             jax.ShapeDtypeStruct((8, LANES), F32),
+            jax.ShapeDtypeStruct((4, tokens.shape[1], inner // 4), BF16),
         ],
         scratch_shapes=[
             pltpu.VMEM((count, tokens.shape[1], width), BF16),
+            pltpu.VMEM((4, tokens.shape[1], inner // 4), BF16),
             pltpu.VMEM((count, total, width), F32),
             pltpu.VMEM((count, 4, piece_rows, width), BF16),
-            dma((count,)),
+            dma((count + 1,)),
             dma((count, 4)),
             dma((count, 4)),
             dma((count, 4, 2)),
@@ -453,6 +575,9 @@
             dma((count, 3)),
             dma((count,)),
             dma((count,)),
+            dma((14,)),
+            dma((14,)),
+            dma((4,)),
         ],
         compiler_params=pltpu.CompilerParams(
             collective_id=0, has_side_effects=True, vmem_limit_bytes=VMEM_BYTES
@@ -892,7 +1017,7 @@
     rates = pad_lanes(decay_rate)
     skips = jnp.repeat(skip[0] + skip[1], head_size)[None]
 
-    values, keys, columns, memory, total = project(
+    values, keys, columns, memory, total, gate_weight = project(
         flattened,
         first_weight,
         bias,
@@ -904,8 +1029,6 @@
         head_size,
         512,
     )
-    gate_part, total = lax.optimization_barrier((xz_weight[:, :inner], total))
-    gate_weight = lax.all_gather(gate_part, ("spatial", "dp"), axis=0, tiled=True)
     rowwise = (values[None], keys[None])
     columnwise = (columns,)
     forward_entering, entering = entering_states(
@@ -918,7 +1041,8 @@
     forward = local_output(
         rowwise, rates[0:1], forward_entering, skips, inner, size, 0, head_size
     )
-    gate_rows = jnp.dot(flattened, gate_weight, preferred_element_type=F32)
+    gate_weight, forward = lax.optimization_barrier((gate_weight, forward))
+    gate_rows = gate_rows_of(flattened, gate_weight, xz_weight.shape[0])
     normed = finish(
         forward[0], returned, gate_rows, norm_gain[None], row_part, col_total, head_size
     )

time: 268 us -> 246 us (0.918)
  matrix products: 15.2 us -> 0 us
  between operations: 13.4 us -> 0.04 us
  Pallas kernels: 224 us -> 232 us
    pallas_call x1, Pallas kernels: 79.6 us -> 64.2 us  [entering_states(): pl.pallas_call(functools.partial(states_kernel, geometry), in_specs=[vmem...]
    dot_general x1 -> x0, matrix products: 15.2 us -> none  [local(): gate_rows = jnp.dot(flattened, gate_weight, preferred_element_type=F32)]
    pallas_call x0 -> x1, Pallas kernels: none -> 15.1 us  [gate_rows_of(): pl.pallas_call(functools.partial(gate_kernel, depth), grid=(5,), in_specs...]
    pallas_call x1, Pallas kernels: 86.4 us -> 94.8 us  [project(): pl.pallas_call(functools.partial(project_kernel, (row_part, col_total, in...]
  transfers between devices with their start and end apart: 2 -> 1, of which waited for: 0 -> 0; matrix products, arithmetic and copies ran while one was open for 6% -> 1% of each run, Pallas kernels for 47% -> 15%
where the time goes in v4:
time: 246 us; the launch traced here: 245 us
  Pallas kernels  232 us (94%)
  local copies, waits for them, and re-layouts  5.75 us (2%)
  starting transfers between devices  5.19 us (2%)
  other arithmetic  2.52 us (1%)
    pallas_call x1, Pallas kernels, project(): pl.pallas_call(functools.partial(project_kernel, (row_part, col_total, in...  94.8 us
    pallas_call x1, Pallas kernels, entering_states(): pl.pallas_call(functools.partial(states_kernel, geometry), in_specs=[vmem...  64.2 us
    pallas_call x2, Pallas kernels, local_output(): pl.pallas_call(functools.partial(output_kernel, column_rows, head_size),...  46.8 us
    pallas_call x1, Pallas kernels, gate_rows_of(): pl.pallas_call(functools.partial(gate_kernel, depth), grid=(5,), in_specs...  15.1 us
    pallas_call x1, Pallas kernels, finish(): pl.pallas_call(functools.partial(finish_kernel, head_size, groups, row_pa...  10.8 us
    all_to_all x1, starting transfers between devices, local(): returned = lax.all_to_all(backward, 'spatial', 0, 0, tiled=True)  5.19 us
  transfers between devices with their start and end apart: 1, of which 0 were waited for; matrix products, arithmetic and copies ran while one was open for 1% of the time, Pallas kernels for 15%

profile of v4, /device:TPU:2, one launch (start us, length us, event | category | flops | bytes accessed | tf_op | source)
XLA Modules:
  0.0 245.2 jit_solution(11884174960562303241)
XLA Ops:
  0.0 0.8 maximum_bitcast_fusion
  0.8 1.3 pad_slice_fusion
  2.2 0.8 copy.9
  3.0 0.1 fusion.4
  3.1 0.6 pad.13.bias_ref
  3.7 1.6 pad_maximum_fusion.state_ref
  5.3 94.8 %shard_map.82 = (f32[960,1536]{1,0:T(8,128)}, f32[960,384]{1,0:T(8,128)}, bf16[4,256,1920]{2,1,0:T(8,128)(2,1)}, f32[128,1536]{1,0:T(8,128)}, f32[8,128]{1,0:T(8,128)}, /*index=5*/bf16[4,3072,384]{2,1,0:T(8,128)(2,1)}) custom-call(bf16[960,3072]{1,0:T(8,128)(2,1)} %bitcast.9, bf16[192,384]{1,0:T(8,128)(2,1)} %pad_maximum_fusion.state_ref, ...), custom_call_target="tpu_custom_call" | custom-call | tf_op jit(solution)/shard_map/pallas_call | solution.py:550
  100.1 64.2 %shard_map.83 = (f32[128,1536]{1,0:T(8,128)}, f32[128,1536]{1,0:T(8,128)}) custom-call(bf16[4,256,1920]{2,1,0:T(8,128)(2,1)} %get-tuple-element.18.columns_ref.values_ref.keys_ref.steps_ref.rest_0_.rest_1_, f32[1,128]{1,0:T(1,128)} %get-tuple-element.25.rate_ref.rest_2_, f32[128,1536]{1,0:T(8,128)} %get-tuple-element.19.forward_ref, ...), custom_call_target="tpu_custom_call" | custom-call | tf_op jit(solution)/shard_map/pallas_call | solution.py:928
  164.2 25.3 %shard_map.85 = bf16[4,256,1536]{2,1,0:T(8,128)(2,1)} custom-call(bf16[4,256,1920]{2,1,0:T(8,128)(2,1)} %get-tuple-element.18.columns_ref.values_ref.keys_ref.steps_ref.rest_0_.rest_1_, bf16[4,256,1920]{2,1,0:T(8,128)(2,1)} %get-tuple-element.18.columns_ref.values_ref.keys_ref.steps_ref.rest_0_.rest_1_, ...), custom_call_target="tpu_custom_call" | custom-call | flops 16986931200 | bytes 33554432 | tf_op jit(solution)/shard_map/pallas_call | solution.py:738
  189.5 0.0 copy-start.2
  189.5 0.0 copy-start.1
  189.5 5.2 %all-to-all-start = ((bf16[4,256,1536]{2,1,0:T(8,128)(2,1)}), bf16[4,256,1536]{2,1,0:T(8,128)(2,1)S(1)}, u32[]{:S(2)}, u32[]{:S(2)}) async-start(bf16[4,256,1536]{2,1,0:T(8,128)(2,1)} %shard_map.85), calls=%async_computation | async-start | bytes 6291456 | tf_op jit(solution)/shard_map/all_to_all | solution.py:1040
  194.7 0.0 copy-done.2
  194.7 0.0 copy-done.1
  194.7 0.6 broadcast_in_dim.19.gain_ref
  195.3 0.1 broadcast_in_dim.18
  195.4 0.7 broadcast_in_dim_reshape.3.rest_3_
  196.1 21.5 %shard_map.84 = f32[1,960,1536]{2,1,0:T(8,128)} custom-call(f32[1,960,1536]{2,1,0:T(8,128)} %bitcast.12, f32[1,960,384]{2,1,0:T(8,128)} %bitcast.13, f32[1,960,384]{2,1,0:T(8,128)} %bitcast.14, f32[1,960,384]{2,1,0:T(8,128)} %bitcast.15, f32[1,128]{1,0:T(1,128)} %get-tuple-element.26.rate_ref.rest_1_, f32[128,1536]{1,0:T(8,128)} %get-tuple-element.21.rest_2_, ...), custom_call_target="tpu_custom_call" | custom-call | flops 16986931200 | bytes 33554432 | tf_op jit(solution)/shard_map/pallas_call | solution.py:738
  217.6 15.1 %shard_map.86.gate_ref = f32[960,1536]{1,0:T(8,128)} custom-call(bf16[960,3072]{1,0:T(8,128)(2,1)} %bitcast.10, bf16[4,3072,384]{2,1,0:T(8,128)(2,1)} %get-tuple-element.24.weight_ref), custom_call_target="tpu_custom_call" | custom-call | flops 9059696640 | bytes 20971520 | tf_op jit(solution)/shard_map/pallas_call | solution.py:138
  232.8 0.0 all-to-all-done.backward_ref
  232.8 0.0 copy-start
  232.8 1.6 copy-done
  234.4 10.8 %shard_map.87 = bf16[960,1536]{1,0:T(8,128)(2,1)} custom-call(f32[960,1536]{1,0:T(8,128)} %bitcast.11, bf16[4,256,1536]{2,1,0:T(8,128)(2,1)} %copy-done, f32[960,1536]{1,0:T(8,128)} %shard_map.86.gate_ref, f32[1,1536]{1,0:T(1,128)} %broadcast_in_dim.19.gain_ref), custom_call_target="tpu_custom_call" | custom-call | tf_op jit(solution)/shard_map/pallas_call | solution.py:989
  (1 shorter events, 0.0 us)
Async XLA Ops:
  189.5 5.2 %copy-start.2 = (f32[2,24]{1,0:T(2,128)S(1)}, f32[2,24]{1,0:T(2,128)}, u32[]{:S(2)}) copy-start(f32[2,24]{1,0:T(2,128)} %param.14) | copy-start | bytes 580
  189.5 5.2 %copy-start.1 = (f32[1536]{0:T(1024)S(1)}, f32[1536]{0:T(1024)}, u32[]{:S(2)}) copy-start(f32[1536]{0:T(1024)} %param.15) | copy-start | bytes 18436
  189.5 43.2 %all-to-all-start = ((bf16[4,256,1536]{2,1,0:T(8,128)(2,1)}), bf16[4,256,1536]{2,1,0:T(8,128)(2,1)S(1)}, u32[]{:S(2)}, u32[]{:S(2)}) async-start(bf16[4,256,1536]{2,1,0:T(8,128)(2,1)} %shard_map.85), calls=%async_computation | async-start | bytes 6291456 | tf_op jit(solution)/shard_map/all_to_all | solution.py:1040
  232.8 1.6 copy-start

commit v5 on v4

--- a/solution.py
+++ b/solution.py
@@ -628,27 +628,13 @@
         return earlier_mask(self.size, self.column_rows)
 
 
-def output_kernel(column_rows, head_size, values_ref, keys_ref, steps_ref, *rest):
-    if column_rows:
-        scale_ref, queries_ref, rate_ref, entering_ref, out_ref, memory_ref, scales_ref = rest
-        skip_ref = None
-    else:
-        queries_ref, rate_ref, entering_ref, skip_ref, out_ref, memory_ref = rest
-        scale_ref = None
-    chunk = Chunk(column_rows, values_ref, keys_ref, steps_ref, scale_ref)
+def output_chunk(chunk, queries, rate, memory_ref, head_size, emit):
     size = chunk.size
-
-    @pl.when(pl.program_id(0) == 0)
-    def _():
-        memory_ref[...] = entering_ref[...]
-        if column_rows:
-            scales_ref[...] = jnp.zeros_like(scales_ref)
-
     steps = chunk.steps()
     keys_t = split(jnp.transpose(chunk.keys()))
-    queries_high, queries_low = split(chunk.queries(queries_ref))
+    queries_high, queries_low = queries
     earlier = chunk.earlier()
-    running, total = running_logs(steps, rate_ref[...], earlier)
+    running, total = running_logs(steps, rate, earlier)
     across = jnp.transpose(running)
     scores = dot(queries_high, keys_t[0]) + dot(queries_high, keys_t[1]) + dot(queries_low, keys_t[0])
     scores = jnp.where(earlier, scores, 0.0)
@@ -656,7 +642,6 @@
     leaving = jnp.exp(jnp.minimum(total - running, 0.0))
     decay = jnp.exp(total)
     first_half = lanes_iota((size, LANES)) < head_size
-    at = pl.num_programs(0) - 1 - pl.program_id(0)
     for pair in range(chunk.pairs):
         lanes = pl.ds(pair * LANES, LANES)
         values = chunk.values(pair)
@@ -670,52 +655,36 @@
             part = dot(kernel_high, both)
             halves.append(part[:, :LANES] + part[:, LANES:] + dot(kernel_low, high))
         memory = memory_ref[:, lanes]
-        memory_high, memory_low = split(memory)
-        part = dot(queries_high, jnp.concatenate([memory_high, memory_low], axis=1))
-        carried = part[:, :LANES] + part[:, LANES:] + dot(queries_low, memory_high)
         result = jnp.where(first_half, halves[0], halves[1])
-        result = result + carried * spread(arrived, pair, head_size)
-        if column_rows:
-            scale, factor = code_scale(jnp.max(jnp.abs(result), axis=0, keepdims=True))
-            coded = encode(result * factor).reshape(4, size // 4, LANES)
-            first = pl.multiple_of(at * (size // 4), 16)
-            out_ref[:, pl.ds(first, size // 4), lanes] = coded
-            here = rows_iota((16, LANES)) == at
-            scales_ref[:, lanes] = jnp.where(here, scale.astype(F32), scales_ref[:, lanes])
-        else:
-            result = result + values * skip_ref[:, lanes]
-            out_ref[:, :, lanes] = result.reshape(1, size, LANES)
+        result = result + carried(queries, memory) * spread(arrived, pair, head_size)
+        emit(pair, result, values)
         weighted = scaled * spread(leaving, pair, head_size)
         memory_ref[:, lanes] = advance(memory, keys_t, weighted, spread(decay, pair, head_size))
-
-    if column_rows:
-
-        @pl.when(pl.program_id(0) == pl.num_programs(0) - 1)
-        def _():
-            scales = scales_ref[...].astype(BF16)
-            for k in range(4):
-                out_ref[k, pl.ds(out_ref.shape[1] - 16, 16), :] = scales
-
-
-def chunk_specs(sources, inner, size, column_rows):
-    pieces = 4 if column_rows else 1
-    part = size // pieces
-    count = sources[0].shape[1] // part
-    first = inner // LANES if column_rows else 0
-
-    def spec(lane_count, lane_block):
-        def index(j):
-            return (0, count - 1 - j if column_rows else j, lane_block)
-
-        return pl.BlockSpec((pieces, part, lane_count), index)
-
-    specs = [spec(inner, 0), spec(LANES, first), spec(LANES, first + 2)]
-    arrays = [sources[0], sources[-1], sources[-1]]
-    if column_rows:
-        last = sources[0].shape[1] // 16 - 1
-        specs.append(pl.BlockSpec((pieces, 16, sources[0].shape[2]), lambda j: (0, last, 0)))
-        arrays.append(sources[0])
-    return count, specs, arrays, spec(LANES, first + 1)
+    return running, total
+
+
+def carried(queries, memory):
+    queries_high, queries_low = queries
+    memory_high, memory_low = split(memory)
+    part = dot(queries_high, jnp.concatenate([memory_high, memory_low], axis=1))
+    return part[:, :LANES] + part[:, LANES:] + dot(queries_low, memory_high)
+
+
+def output_kernel(
+    head_size, values_ref, keys_ref, steps_ref, queries_ref, rate_ref, entering_ref, skip_ref, out_ref, memory_ref
+):
+    chunk = Chunk(0, values_ref, keys_ref, steps_ref, None)
+
+    @pl.when(pl.program_id(0) == 0)
+    def _():
+        memory_ref[...] = entering_ref[...]
+
+    def emit(pair, result, values):
+        lanes = pl.ds(pair * LANES, LANES)
+        result = result + values * skip_ref[:, lanes]
+        out_ref[:, :, lanes] = result.reshape(1, chunk.size, LANES)
+
+    output_chunk(chunk, split(chunk.queries(queries_ref)), rate_ref[...], memory_ref, head_size, emit)
 
 
 def whole(shape):
@@ -728,25 +697,30 @@
     )
 
 
-def local_output(sources, rate, entering, skip, inner, size, column_rows, head_size):
-    count, specs, arrays, queries = chunk_specs(sources, inner, size, column_rows)
-    shape = sources[0].shape[:2] + (inner,)
-    extra = [] if column_rows else [skip]
-    scratch = [pltpu.VMEM((LANES, inner), F32)]
-    if column_rows:
-        scratch.append(pltpu.VMEM((16, inner), F32))
+def row_output(values, keys, rate, entering, skip, inner, size, head_size):
+    count = values.shape[1] // size
+
+    def spec(lane_count, lane_block):
+        return pl.BlockSpec((1, size, lane_count), lambda j: (0, j, lane_block))
+
     return pl.pallas_call(
-        functools.partial(output_kernel, column_rows, head_size),
+        functools.partial(output_kernel, head_size),
         grid=(count,),
-        in_specs=specs
-        + [queries, whole((1, LANES)), whole((LANES, inner))]
-        + [whole((1, inner)) for _ in extra],
-        out_specs=whole(shape) if column_rows else specs[0],
-        out_shape=jax.ShapeDtypeStruct(shape, BF16 if column_rows else F32),
-        scratch_shapes=scratch,
+        in_specs=[
+            spec(inner, 0),
+            spec(LANES, 0),
+            spec(LANES, 2),
+            spec(LANES, 1),
+            whole((1, LANES)),
+            whole((LANES, inner)),
+            whole((1, inner)),
+        ],
+        out_specs=spec(inner, 0),
+        out_shape=jax.ShapeDtypeStruct(values.shape, F32),
+        scratch_shapes=[pltpu.VMEM((LANES, inner), F32)],
         cost_estimate=estimate(count * size, inner, 30, 32 << 20),
         compiler_params=params(),
-    )(*arrays, sources[-1], rate, entering, *extra)
+    )(values, keys, keys, keys, rate, entering, skip)
 
 
 def states_kernel(
@@ -756,7 +730,13 @@
     forward_ref,
     forward_total_ref,
     entering_forward_ref,
+    out_ref,
     entering_backward_ref,
+    outputs,
+    logs,
+    before,
+    scales_ref,
+    local_memory,
     memory,
     total,
     sent,
@@ -888,8 +868,10 @@
     chunks = (columns_ref.shape[1] - 16) // (size // 4)
     last = columns_ref.shape[1] - 16
 
-    def fold_columns(step, carry):
-        at = pl.ds(pl.multiple_of((chunks - 1 - step) * (size // 4), 16), size // 4)
+    part_rows = size // 4
+
+    def chunk_at(step):
+        at = pl.ds(pl.multiple_of((chunks - 1 - step) * part_rows, 16), part_rows)
         chunk = Chunk(
             column_rows,
             columns_ref.at[:, at, pl.ds(0, inner)],
@@ -897,6 +879,10 @@
             columns_ref.at[:, at, pl.ds(inner + 2 * LANES, LANES)],
             columns_ref.at[:, pl.ds(last, 16), :],
         )
+        return chunk, split(chunk.queries(columns_ref.at[:, at, pl.ds(inner + LANES, LANES)]))
+
+    def fold_columns(step, carry):
+        chunk, _ = chunk_at(step)
         fold_chunk(
             chunk.values,
             chunk.keys(),
@@ -909,28 +895,81 @@
         )
         return carry
 
+    def output_columns(step, carry):
+        chunk, queries = chunk_at(step)
+
+        def emit(pair, result, values):
+            outputs[step, :, pl.ds(pair * LANES, LANES)] = result
+
+        running, chunk_total = output_chunk(
+            chunk, queries, rate_ref[...], local_memory, head_size, emit
+        )
+        logs[step] = before[0:1] + running
+        before[...] = before[...] + chunk_total
+
+        @pl.when(step == 1)
+        def _():
+            scan(0, False, entering_forward_ref)
+
+        @pl.when(step == 2)
+        def _():
+            scan(1, True, entering_backward_ref)
+
+        return carry
+
+    def correct(step, carry):
+        _, queries = chunk_at(step)
+        arrived = jnp.exp(logs[step])
+        first = pl.multiple_of((chunks - 1 - step) * part_rows, 16)
+        here = rows_iota((16, LANES)) == chunks - 1 - step
+        for pair in range(inner // LANES):
+            lanes = pl.ds(pair * LANES, LANES)
+            added = carried(queries, memory[:, lanes]) * spread(arrived, pair, head_size)
+            result = outputs[step, :, lanes] + added
+            scale, factor = code_scale(jnp.max(jnp.abs(result), axis=0, keepdims=True))
+            out_ref[:, pl.ds(first, part_rows), lanes] = encode(result * factor).reshape(
+                4, part_rows, LANES
+            )
+            scales_ref[:, lanes] = jnp.where(here, scale.astype(F32), scales_ref[:, lanes])
+        return carry
+
     lax.fori_loop(0, chunks, fold_columns, 0)
     send_slices(1, memory, total)
-    scan(0, False, entering_forward_ref)
-    scan(1, True, entering_backward_ref)
+    local_memory[...] = jnp.zeros_like(local_memory)
+    before[...] = jnp.zeros_like(before)
+    scales_ref[...] = jnp.zeros_like(scales_ref)
+    lax.fori_loop(0, chunks, output_columns, 0)
+    finish_way(1, entering_backward_ref)
+    memory[...] = entering_backward_ref[...]
+    lax.fori_loop(0, chunks, correct, 0)
+    for k in range(4):
+        out_ref[k, pl.ds(last, 16), :] = scales_ref[...].astype(BF16)
     finish_way(0, entering_forward_ref)
-    finish_way(1, entering_backward_ref)
-
-
-def entering_states(columns, rate, memory, total, inner, size, column_rows, head_size):
+
+
+def column_output(columns, rate, memory, total, inner, size, column_rows, head_size):
     spatial = lax.axis_size("spatial")
     count = lax.axis_size("frame") * spatial
     rows, wide = LANES * 2 // count, inner // 2
+    chunks = (columns.shape[1] - 16) * 4 // size
     vmem, hbm = pl.BlockSpec(memory_space=pltpu.VMEM), pl.BlockSpec(memory_space=pl.ANY)
     dma = pltpu.SemaphoreType.DMA
-    state = jax.ShapeDtypeStruct((LANES, inner), F32)
     geometry = (inner, size, column_rows, head_size, count, spatial)
     return pl.pallas_call(
         functools.partial(states_kernel, geometry),
         in_specs=[vmem] * 4,
-        out_specs=[hbm, hbm],
-        out_shape=[state, state],
+        out_specs=[hbm, vmem],
+        out_shape=[
+            jax.ShapeDtypeStruct((LANES, inner), F32),
+            jax.ShapeDtypeStruct(columns.shape[:2] + (inner,), BF16),
+        ],
         scratch_shapes=[
+            pltpu.VMEM((LANES, inner), F32),
+            pltpu.VMEM((chunks, size, inner), F32),
+            pltpu.VMEM((chunks, size, LANES), F32),
+            pltpu.VMEM((8, LANES), F32),
+            pltpu.VMEM((16, inner), F32),
+            pltpu.VMEM((LANES, inner), F32),
             pltpu.VMEM((LANES, inner), F32),
             pltpu.VMEM((8, LANES), F32),
             pltpu.VMEM((2, count, rows, wide + LANES), F32),
@@ -1029,17 +1068,12 @@
         head_size,
         512,
     )
-    rowwise = (values[None], keys[None])
-    columnwise = (columns,)
-    forward_entering, entering = entering_states(
+    entering, backward = column_output(
         columns, rates[1:2], memory, total, inner, size, column_rows, head_size
     )
-    backward = local_output(
-        columnwise, rates[1:2], entering, None, inner, size, column_rows, head_size
-    )
     returned = lax.all_to_all(backward, "spatial", 0, 0, tiled=True)
-    forward = local_output(
-        rowwise, rates[0:1], forward_entering, skips, inner, size, 0, head_size
+    forward = row_output(
+        values[None], keys[None], rates[0:1], entering, skips, inner, size, head_size
     )
     gate_weight, forward = lax.optimization_barrier((gate_weight, forward))
     gate_rows = gate_rows_of(flattened, gate_weight, xz_weight.shape[0])

time: 246 us -> 229 us (0.931); the launches traced: 245 us -> 226 us
  Pallas kernels: 232 us -> 213 us
    pallas_call x3 -> x2, Pallas kernels: 111 us -> 91.8 us  [the longest x1 70.7 us: column_output(): pl.pallas_call(functools.partial(states_kernel, geometry), in_specs=[vmem...]
  transfers between devices with their start and end apart: 1 -> 1, of which waited for: 0 -> 0; matrix products, arithmetic and copies ran while one was open for 1% -> 1% of each run, Pallas kernels for 15% -> 16%
where the time goes in v5:
time: 229 us; the launch traced here: 226 us
  Pallas kernels  213 us (93%)
  local copies, waits for them, and re-layouts  5.61 us (2%)
  starting transfers between devices  5.07 us (2%)
  other arithmetic  2.53 us (1%)
    pallas_call x1, Pallas kernels, project(): pl.pallas_call(functools.partial(project_kernel, (row_part, col_total, in...  94.7 us
    pallas_call x1, Pallas kernels, column_output(): pl.pallas_call(functools.partial(states_kernel, geometry), in_specs=[vmem...  70.7 us
    pallas_call x1, Pallas kernels, row_output(): pl.pallas_call(functools.partial(output_kernel, head_size), grid=(count,)...  21.2 us
    pallas_call x1, Pallas kernels, gate_rows_of(): pl.pallas_call(functools.partial(gate_kernel, depth), grid=(5,), in_specs...  15.1 us
    pallas_call x1, Pallas kernels, finish(): pl.pallas_call(functools.partial(finish_kernel, head_size, groups, row_pa...  10.8 us
    all_to_all x1, starting transfers between devices, local(): returned = lax.all_to_all(backward, 'spatial', 0, 0, tiled=True)  5.07 us
  transfers between devices with their start and end apart: 1, of which 0 were waited for; matrix products, arithmetic and copies ran while one was open for 1% of the time, Pallas kernels for 16%

profile of v5, /device:TPU:2, one launch (start us, length us, event | category | flops | bytes accessed | tf_op | source)
XLA Modules:
  0.0 225.8 jit_solution(1597659284596864835)
XLA Ops:
  0.0 0.8 copy.9
  0.8 0.1 fusion.4
  0.9 0.8 maximum_bitcast_fusion
  1.8 1.3 pad_slice_fusion
  3.1 1.6 pad_maximum_fusion.state_ref
  4.6 0.5 pad.13.bias_ref
  5.1 94.7 %shard_map.82 = (f32[960,1536]{1,0:T(8,128)}, f32[960,384]{1,0:T(8,128)}, bf16[4,256,1920]{2,1,0:T(8,128)(2,1)}, f32[128,1536]{1,0:T(8,128)}, f32[8,128]{1,0:T(8,128)}, /*index=5*/bf16[4,3072,384]{2,1,0:T(8,128)(2,1)}) custom-call(bf16[960,3072]{1,0:T(8,128)(2,1)} %bitcast.9, bf16[192,384]{1,0:T(8,128)(2,1)} %pad_maximum_fusion.state_ref, ...), custom_call_target="tpu_custom_call" | custom-call | tf_op jit(solution)/shard_map/pallas_call | solution.py:550
  99.9 70.7 %shard_map.83 = (f32[128,1536]{1,0:T(8,128)}, bf16[4,256,1536]{2,1,0:T(8,128)(2,1)}) custom-call(bf16[4,256,1920]{2,1,0:T(8,128)(2,1)} %get-tuple-element.18.columns_ref, f32[1,128]{1,0:T(1,128)} %get-tuple-element.25.rate_ref, f32[128,1536]{1,0:T(8,128)} %get-tuple-element.19.forward_ref, f32[8,128]{1,0:T(8,128)} %get-tuple-element.20.forward_total_ref), custom_call_target="tpu_custom_call" | custom-call | tf_op jit(solution)/shard_map/pallas_call | solution.py:958
  170.6 0.0 copy-start.2
  170.6 5.1 %all-to-all-start = ((bf16[4,256,1536]{2,1,0:T(8,128)(2,1)}), bf16[4,256,1536]{2,1,0:T(8,128)(2,1)S(1)}, u32[]{:S(2)}, u32[]{:S(2)}) async-start(bf16[4,256,1536]{2,1,0:T(8,128)(2,1)} %get-tuple-element.23), calls=%async_computation | async-start | bytes 6291456 | tf_op jit(solution)/shard_map/all_to_all | solution.py:1074
  175.7 0.0 copy-done.2
  175.7 0.1 broadcast_in_dim.18
  175.7 0.7 broadcast_in_dim_reshape.3.skip_ref
  176.4 0.0 copy-start.1
  176.4 21.2 %shard_map.84 = f32[1,960,1536]{2,1,0:T(8,128)} custom-call(f32[1,960,1536]{2,1,0:T(8,128)} %bitcast.12, f32[1,960,384]{2,1,0:T(8,128)} %bitcast.13, f32[1,960,384]{2,1,0:T(8,128)} %bitcast.14, f32[1,960,384]{2,1,0:T(8,128)} %bitcast.15, f32[1,128]{1,0:T(1,128)} %get-tuple-element.26.rate_ref, f32[128,1536]{1,0:T(8,128)} %get-tuple-element.21.entering_ref, ...), custom_call_target="tpu_custom_call" | custom-call | flops 16986931200 | bytes 33554432 | tf_op jit(solution)/shard_map/pallas_call | solution.py:706
  197.6 0.0 copy-done.1
  197.6 0.6 broadcast_in_dim.19.gain_ref
  198.2 15.1 %shard_map.85.gate_ref = f32[960,1536]{1,0:T(8,128)} custom-call(bf16[960,3072]{1,0:T(8,128)(2,1)} %bitcast.10, bf16[4,3072,384]{2,1,0:T(8,128)(2,1)} %get-tuple-element.24.weight_ref), custom_call_target="tpu_custom_call" | custom-call | flops 9059696640 | bytes 20971520 | tf_op jit(solution)/shard_map/pallas_call | solution.py:138
  213.3 0.0 all-to-all-done.backward_ref
  213.3 0.0 copy-start
  213.3 1.6 copy-done
  215.0 10.8 %shard_map.86 = bf16[960,1536]{1,0:T(8,128)(2,1)} custom-call(f32[960,1536]{1,0:T(8,128)} %bitcast.11, bf16[4,256,1536]{2,1,0:T(8,128)(2,1)} %copy-done, f32[960,1536]{1,0:T(8,128)} %shard_map.85.gate_ref, f32[1,1536]{1,0:T(1,128)} %broadcast_in_dim.19.gain_ref), custom_call_target="tpu_custom_call" | custom-call | tf_op jit(solution)/shard_map/pallas_call | solution.py:1028
  (1 shorter events, 0.0 us)
Async XLA Ops:
  170.6 5.1 %copy-start.2 = (f32[2,24]{1,0:T(2,128)S(1)}, f32[2,24]{1,0:T(2,128)}, u32[]{:S(2)}) copy-start(f32[2,24]{1,0:T(2,128)} %param.14) | copy-start | bytes 580
  170.6 42.7 %all-to-all-start = ((bf16[4,256,1536]{2,1,0:T(8,128)(2,1)}), bf16[4,256,1536]{2,1,0:T(8,128)(2,1)S(1)}, u32[]{:S(2)}, u32[]{:S(2)}) async-start(bf16[4,256,1536]{2,1,0:T(8,128)(2,1)} %get-tuple-element.23), calls=%async_computation | async-start | bytes 6291456 | tf_op jit(solution)/shard_map/all_to_all | solution.py:1074
  176.4 21.2 %copy-start.1 = (f32[1536]{0:T(1024)S(1)}, f32[1536]{0:T(1024)}, u32[]{:S(2)}) copy-start(f32[1536]{0:T(1024)} %param.15) | copy-start | bytes 18436
  213.3 1.6 copy-start

commit v6 on v5

--- a/solution.py
+++ b/solution.py
@@ -12,6 +12,7 @@
 LANES = 128
 GROUP = 4
 POWER = 17
+LOG2_E = 1.4426950408889634
 CODE_TOP = 128.0
 STEP_LANES = 24
 MESH = pl.DeviceIdType.MESH
@@ -165,6 +166,7 @@
     gate_weight,
     product,
     middle,
+    tokens,
     own_sem,
     x_send,
     x_recv,
@@ -392,8 +394,7 @@
         for at, quarter in enumerate((z, (z + 3) % 4, (z + 1) % 4, (z + 2) % 4)):
             gate_arrived(gate_view(quarter, (1 - core) * core_rows, core_rows), 10 + at)
 
-    tokens = row_part * col_total
-    tile = tokens // 5
+    tile = row_part * col_total // 5
     groups = col_total // GROUP // 4
     piece_rows = groups * row_part * GROUP
     outs = {}
@@ -405,7 +406,7 @@
 
         def one_tile(i, largest):
             at = pl.ds(pl.multiple_of(i * tile, tile), tile)
-            result = dot(tokens_ref[at, :], in_order(weight.at[block, :, lanes], depth))
+            result = dot(tokens[at, :], in_order(weight.at[block, :, lanes], depth))
             if block == 0:
                 raw = result[:, width - LANES :] + bias_ref[...]
                 steps = jnp.maximum(raw, 0.0) + jnp.log1p(jnp.exp(-jnp.abs(raw)))
@@ -478,6 +479,8 @@
     for block in range(count):
         send_own(block)
     gate_start()
+    tokens_copy = pltpu.make_async_copy(tokens_ref, tokens, own_sem.at[count + 1])
+    tokens_copy.start()
     relay(0)
     relay(1)
     gate_x()
@@ -491,9 +494,12 @@
             (gate_y, gate_z)[block]()
         pass_on(block)
         gathered(block)
+        if block == 0:
+            tokens_copy.wait()
         compute(block)
 
     gate_pass()
+
     memory_ref[...] = jnp.zeros_like(memory_ref)
     total_ref[...] = jnp.zeros_like(total_ref)
 
@@ -549,7 +555,7 @@
     dma = pltpu.SemaphoreType.DMA
     return pl.pallas_call(
         functools.partial(project_kernel, (row_part, col_total, inner, depth, blocks, head_size)),
-        in_specs=[vmem, vmem, vmem, vmem, hbm],
+        in_specs=[hbm, vmem, vmem, vmem, hbm],
         out_specs=[hbm, hbm, hbm, vmem, vmem, hbm],
         out_shape=[
             jax.ShapeDtypeStruct((total, inner), F32),
@@ -564,7 +570,8 @@
             pltpu.VMEM((4, tokens.shape[1], inner // 4), BF16),
             pltpu.VMEM((count, total, width), F32),
             pltpu.VMEM((count, 4, piece_rows, width), BF16),
-            dma((count + 1,)),
+            pltpu.VMEM(tokens.shape, BF16),
+            dma((count + 2,)),
             dma((count, 4)),
             dma((count, 4)),
             dma((count, 4, 2)),
@@ -628,14 +635,15 @@
         return earlier_mask(self.size, self.column_rows)
 
 
-def output_chunk(chunk, queries, rate, memory_ref, head_size, emit):
+def output_chunk(chunk, values_of, queries, rate, memory_ref, head_size, emit):
     size = chunk.size
     steps = chunk.steps()
     keys_t = split(jnp.transpose(chunk.keys()))
     queries_high, queries_low = queries
     earlier = chunk.earlier()
     running, total = running_logs(steps, rate, earlier)
-    across = jnp.transpose(running)
+    running_bits = running * LOG2_E
+    across = jnp.transpose(running_bits)
     scores = dot(queries_high, keys_t[0]) + dot(queries_high, keys_t[1]) + dot(queries_low, keys_t[0])
     scores = jnp.where(earlier, scores, 0.0)
     arrived = jnp.exp(running)
@@ -644,14 +652,14 @@
     first_half = lanes_iota((size, LANES)) < head_size
     for pair in range(chunk.pairs):
         lanes = pl.ds(pair * LANES, LANES)
-        values = chunk.values(pair)
+        values = values_of(pair)
         scaled = values * spread(steps, pair, head_size)
         high, low = split(scaled)
         both = jnp.concatenate([high, low], axis=1)
         halves = []
         for head in (2 * pair, 2 * pair + 1):
-            between = jnp.minimum(running[:, head : head + 1] - across[head : head + 1, :], 0.0)
-            kernel_high, kernel_low = split(jnp.exp(between) * scores)
+            between = running_bits[:, head : head + 1] - across[head : head + 1, :]
+            kernel_high, kernel_low = split(jnp.exp2(jnp.minimum(between, 0.0)) * scores)
             part = dot(kernel_high, both)
             halves.append(part[:, :LANES] + part[:, LANES:] + dot(kernel_low, high))
         memory = memory_ref[:, lanes]
@@ -684,7 +692,8 @@
         result = result + values * skip_ref[:, lanes]
         out_ref[:, :, lanes] = result.reshape(1, chunk.size, LANES)
 
-    output_chunk(chunk, split(chunk.queries(queries_ref)), rate_ref[...], memory_ref, head_size, emit)
+    queries = split(chunk.queries(queries_ref))
+    output_chunk(chunk, chunk.values, queries, rate_ref[...], memory_ref, head_size, emit)
 
 
 def whole(shape):
@@ -883,8 +892,14 @@
 
     def fold_columns(step, carry):
         chunk, _ = chunk_at(step)
+
+        def keep_values(pair):
+            values = chunk.values(pair)
+            outputs[step, :, pl.ds(pair * LANES, LANES)] = values
+            return values
+
         fold_chunk(
-            chunk.values,
+            keep_values,
             chunk.keys(),
             chunk.steps(),
             rate_ref[...],
@@ -901,19 +916,22 @@
         def emit(pair, result, values):
             outputs[step, :, pl.ds(pair * LANES, LANES)] = result
 
+        def kept_values(pair):
+            return outputs[step, :, pl.ds(pair * LANES, LANES)]
+
         running, chunk_total = output_chunk(
-            chunk, queries, rate_ref[...], local_memory, head_size, emit
+            chunk, kept_values, queries, rate_ref[...], local_memory, head_size, emit
         )
         logs[step] = before[0:1] + running
         before[...] = before[...] + chunk_total
 
-        @pl.when(step == 1)
-        def _():
-            scan(0, False, entering_forward_ref)
-
         @pl.when(step == 2)
         def _():
             scan(1, True, entering_backward_ref)
+
+        @pl.when(step == 3)
+        def _():
+            scan(0, False, entering_forward_ref)
 
         return carry
 

time: 229 us -> 215 us (0.939)
  Pallas kernels: 213 us -> 200 us
    pallas_call x1, Pallas kernels: 70.7 us -> 59.6 us  [column_output(): pl.pallas_call(functools.partial(states_kernel, geometry), in_specs=[vmem...]
  transfers between devices with their start and end apart: 1 -> 1, of which waited for: 0 -> 0; matrix products, arithmetic and copies ran while one was open for 1% -> 1% of each run, Pallas kernels for 16% -> 17%
where the time goes in v6:
time: 215 us; the launch traced here: 213 us
  Pallas kernels  200 us (93%)
  local copies, waits for them, and re-layouts  5.61 us (3%)
  starting transfers between devices  5.18 us (2%)
  other arithmetic  2.53 us (1%)
    pallas_call x1, Pallas kernels, project(): pl.pallas_call(functools.partial(project_kernel, (row_part, col_total, in...  92.9 us
    pallas_call x1, Pallas kernels, column_output(): pl.pallas_call(functools.partial(states_kernel, geometry), in_specs=[vmem...  59.6 us
    pallas_call x1, Pallas kernels, row_output(): pl.pallas_call(functools.partial(output_kernel, head_size), grid=(count,)...  21.3 us
    pallas_call x1, Pallas kernels, gate_rows_of(): pl.pallas_call(functools.partial(gate_kernel, depth), grid=(5,), in_specs...  15.1 us
    pallas_call x1, Pallas kernels, finish(): pl.pallas_call(functools.partial(finish_kernel, head_size, groups, row_pa...  10.8 us
    all_to_all x1, starting transfers between devices, local(): returned = lax.all_to_all(backward, 'spatial', 0, 0, tiled=True)  5.18 us
  transfers between devices with their start and end apart: 1, of which 0 were waited for; matrix products, arithmetic and copies ran while one was open for 1% of the time, Pallas kernels for 17%

profile of v6, /device:TPU:2, one launch (start us, length us, event | category | flops | bytes accessed | tf_op | source)
XLA Modules:
  0.0 213.2 jit_solution(10558213577477040495)
XLA Ops:
  0.0 0.8 copy.9
  0.8 0.1 fusion.4
  0.9 0.8 maximum_bitcast_fusion
  1.8 1.3 pad_slice_fusion
  3.1 1.6 pad_maximum_fusion.state_ref
  4.6 0.5 pad.13.bias_ref
  5.1 92.9 %shard_map.82 = (f32[960,1536]{1,0:T(8,128)}, f32[960,384]{1,0:T(8,128)}, bf16[4,256,1920]{2,1,0:T(8,128)(2,1)}, f32[128,1536]{1,0:T(8,128)}, f32[8,128]{1,0:T(8,128)}, /*index=5*/bf16[4,3072,384]{2,1,0:T(8,128)(2,1)}) custom-call(bf16[960,3072]{1,0:T(8,128)(2,1)} %bitcast.9, bf16[192,384]{1,0:T(8,128)(2,1)} %pad_maximum_fusion.state_ref, ...), custom_call_target="tpu_custom_call" | custom-call | tf_op jit(solution)/shard_map/pallas_call | solution.py:556
  98.1 59.6 %shard_map.83 = (f32[128,1536]{1,0:T(8,128)}, bf16[4,256,1536]{2,1,0:T(8,128)(2,1)}) custom-call(bf16[4,256,1920]{2,1,0:T(8,128)(2,1)} %get-tuple-element.18.columns_ref, f32[1,128]{1,0:T(1,128)} %get-tuple-element.25.rate_ref, f32[128,1536]{1,0:T(8,128)} %get-tuple-element.19.forward_ref, f32[8,128]{1,0:T(8,128)} %get-tuple-element.20.forward_total_ref), custom_call_target="tpu_custom_call" | custom-call | tf_op jit(solution)/shard_map/pallas_call | solution.py:976
  157.7 0.0 copy-start.2
  157.7 5.2 %all-to-all-start = ((bf16[4,256,1536]{2,1,0:T(8,128)(2,1)}), bf16[4,256,1536]{2,1,0:T(8,128)(2,1)S(1)}, u32[]{:S(2)}, u32[]{:S(2)}) async-start(bf16[4,256,1536]{2,1,0:T(8,128)(2,1)} %get-tuple-element.23), calls=%async_computation | async-start | bytes 6291456 | tf_op jit(solution)/shard_map/all_to_all | solution.py:1092
  162.9 0.0 copy-done.2
  162.9 0.1 broadcast_in_dim.18
  163.0 0.7 broadcast_in_dim_reshape.3.skip_ref
  163.7 0.0 copy-start.1
  163.7 21.3 %shard_map.84 = f32[1,960,1536]{2,1,0:T(8,128)} custom-call(f32[1,960,1536]{2,1,0:T(8,128)} %bitcast.12, f32[1,960,384]{2,1,0:T(8,128)} %bitcast.13, f32[1,960,384]{2,1,0:T(8,128)} %bitcast.14, f32[1,960,384]{2,1,0:T(8,128)} %bitcast.15, f32[1,128]{1,0:T(1,128)} %get-tuple-element.26.rate_ref, f32[128,1536]{1,0:T(8,128)} %get-tuple-element.21.entering_ref, ...), custom_call_target="tpu_custom_call" | custom-call | flops 16986931200 | bytes 33554432 | tf_op jit(solution)/shard_map/pallas_call | solution.py:715
  184.9 0.0 copy-done.1
  184.9 0.6 broadcast_in_dim.19.gain_ref
  185.5 15.1 %shard_map.85.gate_ref = f32[960,1536]{1,0:T(8,128)} custom-call(bf16[960,3072]{1,0:T(8,128)(2,1)} %bitcast.10, bf16[4,3072,384]{2,1,0:T(8,128)(2,1)} %get-tuple-element.24.weight_ref), custom_call_target="tpu_custom_call" | custom-call | flops 9059696640 | bytes 20971520 | tf_op jit(solution)/shard_map/pallas_call | solution.py:139
  200.7 0.0 all-to-all-done.backward_ref
  200.7 0.0 copy-start
  200.7 1.6 copy-done
  202.3 10.8 %shard_map.86 = bf16[960,1536]{1,0:T(8,128)(2,1)} custom-call(f32[960,1536]{1,0:T(8,128)} %bitcast.11, bf16[4,256,1536]{2,1,0:T(8,128)(2,1)} %copy-done, f32[960,1536]{1,0:T(8,128)} %shard_map.85.gate_ref, f32[1,1536]{1,0:T(1,128)} %broadcast_in_dim.19.gain_ref), custom_call_target="tpu_custom_call" | custom-call | tf_op jit(solution)/shard_map/pallas_call | solution.py:1046
  (1 shorter events, 0.0 us)
Async XLA Ops:
  157.7 5.2 %copy-start.2 = (f32[2,24]{1,0:T(2,128)S(1)}, f32[2,24]{1,0:T(2,128)}, u32[]{:S(2)}) copy-start(f32[2,24]{1,0:T(2,128)} %param.14) | copy-start | bytes 580
  157.7 43.0 %all-to-all-start = ((bf16[4,256,1536]{2,1,0:T(8,128)(2,1)}), bf16[4,256,1536]{2,1,0:T(8,128)(2,1)S(1)}, u32[]{:S(2)}, u32[]{:S(2)}) async-start(bf16[4,256,1536]{2,1,0:T(8,128)(2,1)} %get-tuple-element.23), calls=%async_computation | async-start | bytes 6291456 | tf_op jit(solution)/shard_map/all_to_all | solution.py:1092
  163.7 21.3 %copy-start.1 = (f32[1536]{0:T(1024)S(1)}, f32[1536]{0:T(1024)}, u32[]{:S(2)}) copy-start(f32[1536]{0:T(1024)} %param.15) | copy-start | bytes 18436
  200.7 1.6 copy-start

commit v7 on v6

--- a/solution.py
+++ b/solution.py
@@ -44,6 +44,19 @@
 
 def params(semantics=("arbitrary",)):
     return pltpu.CompilerParams(vmem_limit_bytes=VMEM_BYTES, dimension_semantics=semantics)
+
+
+def widen(columns, copies):
+    heads = columns.shape[1]
+    shape = (heads, LANES)
+    head, lane = rows_iota(shape), lanes_iota(shape)
+    place = (lax.rem(lane, heads) == head) & (lane < copies * heads)
+    place = jnp.where(place, 1.0, 0.0).astype(BF16)
+    if columns.dtype == BF16:
+        return dot(columns, place)
+    high = columns.astype(BF16)
+    middle, low = split(columns - high.astype(F32))
+    return dot(high, place) + dot(middle, place) + dot(low, place)
 
 
 def encode(scaled):
@@ -113,6 +126,7 @@
             memory_ref[:, lanes], keys_t, weighted, spread(decay, pair, head_size)
         )
     total_ref[...] = total_ref[...] + total
+    return running
 
 
 def in_order(ref, depth):
@@ -152,7 +166,8 @@
 def project_kernel(
     geometry,
     tokens_ref,
-    state_ref,
+    state_weight_ref,
+    step_weight_ref,
     bias_ref,
     rate_ref,
     xz_ref,
@@ -167,6 +182,7 @@
     product,
     middle,
     tokens,
+    state_ref,
     own_sem,
     x_send,
     x_recv,
@@ -408,7 +424,7 @@
             at = pl.ds(pl.multiple_of(i * tile, tile), tile)
             result = dot(tokens[at, :], in_order(weight.at[block, :, lanes], depth))
             if block == 0:
-                raw = result[:, width - LANES :] + bias_ref[...]
+                raw = result[:, width - LANES :] + widen(bias_ref[...], 3)
                 steps = jnp.maximum(raw, 0.0) + jnp.log1p(jnp.exp(-jnp.abs(raw)))
                 result = jnp.concatenate([result[:, : width - LANES], steps], axis=1)
             product[buffer, at, lanes] = result
@@ -476,6 +492,9 @@
         pltpu.make_async_copy(middle.at[block, place, :, lanes], into, move_own.at[block]).start()
 
     count = len(blocks)
+    state_columns = state_weight_ref.shape[1]
+    state_ref[:, pl.ds(0, state_columns)] = state_weight_ref[...]
+    state_ref[:, pl.ds(state_columns, LANES)] = widen(step_weight_ref[...], 3).astype(BF16)
     for block in range(count):
         send_own(block)
     gate_start()
@@ -503,6 +522,8 @@
     memory_ref[...] = jnp.zeros_like(memory_ref)
     total_ref[...] = jnp.zeros_like(total_ref)
 
+    rate = widen(rate_ref[...], 1)[0:1]
+
     def fold_rows(step, carry):
         at = pl.ds(pl.multiple_of(step * tile, 16), tile)
         block_pairs = blocks[1][1] // LANES
@@ -514,7 +535,7 @@
             values,
             product[0, at, pl.ds(0, LANES)],
             product[0, at, pl.ds(2 * LANES, LANES)],
-            rate_ref[...],
+            rate,
             earlier_mask(tile, 0),
             head_size,
             memory_ref,
@@ -544,8 +565,11 @@
         copy.wait_send()
 
 
-def project(tokens, state_weight, bias, rate, xz_weight, row_part, col_total, inner, head_size, block_width):
-    depth, state_width = state_weight.shape
+def project(
+    tokens, state_weight, step_weight, bias, rate, xz_weight, row_part, col_total, inner, head_size, block_width
+):
+    depth = state_weight.shape[0]
+    state_width = state_weight.shape[1] + LANES
     count = inner // block_width + 1
     blocks = ((0, state_width),) + tuple((k * block_width, block_width) for k in range(count - 1))
     width = max(block_width, state_width)
@@ -555,7 +579,7 @@
     dma = pltpu.SemaphoreType.DMA
     return pl.pallas_call(
         functools.partial(project_kernel, (row_part, col_total, inner, depth, blocks, head_size)),
-        in_specs=[hbm, vmem, vmem, vmem, hbm],
+        in_specs=[hbm, vmem, vmem, vmem, vmem, hbm],
         out_specs=[hbm, hbm, hbm, vmem, vmem, hbm],
         out_shape=[
             jax.ShapeDtypeStruct((total, inner), F32),
@@ -571,6 +595,7 @@
             pltpu.VMEM((count, total, width), F32),
             pltpu.VMEM((count, 4, piece_rows, width), BF16),
             pltpu.VMEM(tokens.shape, BF16),
+            pltpu.VMEM((depth, state_width), BF16),
             dma((count + 2,)),
             dma((count, 4)),
             dma((count, 4)),
@@ -589,7 +614,7 @@
         compiler_params=pltpu.CompilerParams(
             collective_id=0, has_side_effects=True, vmem_limit_bytes=VMEM_BYTES
         ),
-    )(tokens, state_weight, bias, rate, xz_weight)
+    )(tokens, state_weight, step_weight, bias, rate, xz_weight)
 
 
 class Chunk:
@@ -635,40 +660,45 @@
         return earlier_mask(self.size, self.column_rows)
 
 
-def output_chunk(chunk, values_of, queries, rate, memory_ref, head_size, emit):
-    size = chunk.size
+def score_matrix(queries, keys_t, earlier):
+    queries_high, queries_low = queries
+    scores = dot(queries_high, keys_t[0]) + dot(queries_high, keys_t[1]) + dot(queries_low, keys_t[0])
+    return jnp.where(earlier, scores, 0.0)
+
+
+def within_pair(pair, scaled, running_bits, across, scores, head_size):
+    high, low = scaled
+    both = jnp.concatenate([high, low], axis=1)
+    halves = []
+    for head in (2 * pair, 2 * pair + 1):
+        between = running_bits[:, head : head + 1] - across[head : head + 1, :]
+        kernel_high, kernel_low = split(jnp.exp2(jnp.minimum(between, 0.0)) * scores)
+        part = dot(kernel_high, both)
+        halves.append(part[:, :LANES] + part[:, LANES:] + dot(kernel_low, high))
+    return jnp.where(lanes_iota(halves[0].shape) < head_size, halves[0], halves[1])
+
+
+def output_chunk(chunk, queries, rate, memory_ref, head_size, emit):
     steps = chunk.steps()
     keys_t = split(jnp.transpose(chunk.keys()))
-    queries_high, queries_low = queries
     earlier = chunk.earlier()
     running, total = running_logs(steps, rate, earlier)
     running_bits = running * LOG2_E
     across = jnp.transpose(running_bits)
-    scores = dot(queries_high, keys_t[0]) + dot(queries_high, keys_t[1]) + dot(queries_low, keys_t[0])
-    scores = jnp.where(earlier, scores, 0.0)
+    scores = score_matrix(queries, keys_t, earlier)
     arrived = jnp.exp(running)
     leaving = jnp.exp(jnp.minimum(total - running, 0.0))
     decay = jnp.exp(total)
-    first_half = lanes_iota((size, LANES)) < head_size
     for pair in range(chunk.pairs):
         lanes = pl.ds(pair * LANES, LANES)
-        values = values_of(pair)
+        values = chunk.values(pair)
         scaled = values * spread(steps, pair, head_size)
-        high, low = split(scaled)
-        both = jnp.concatenate([high, low], axis=1)
-        halves = []
-        for head in (2 * pair, 2 * pair + 1):
-            between = running_bits[:, head : head + 1] - across[head : head + 1, :]
-            kernel_high, kernel_low = split(jnp.exp2(jnp.minimum(between, 0.0)) * scores)
-            part = dot(kernel_high, both)
-            halves.append(part[:, :LANES] + part[:, LANES:] + dot(kernel_low, high))
+        result = within_pair(pair, split(scaled), running_bits, across, scores, head_size)
         memory = memory_ref[:, lanes]
-        result = jnp.where(first_half, halves[0], halves[1])
         result = result + carried(queries, memory) * spread(arrived, pair, head_size)
         emit(pair, result, values)
         weighted = scaled * spread(leaving, pair, head_size)
         memory_ref[:, lanes] = advance(memory, keys_t, weighted, spread(decay, pair, head_size))
-    return running, total
 
 
 def carried(queries, memory):
@@ -693,7 +723,7 @@
         out_ref[:, :, lanes] = result.reshape(1, chunk.size, LANES)
 
     queries = split(chunk.queries(queries_ref))
-    output_chunk(chunk, chunk.values, queries, rate_ref[...], memory_ref, head_size, emit)
+    output_chunk(chunk, queries, widen(rate_ref[...], 1)[0:1], memory_ref, head_size, emit)
 
 
 def whole(shape):
@@ -720,7 +750,7 @@
             spec(LANES, 0),
             spec(LANES, 2),
             spec(LANES, 1),
-            whole((1, LANES)),
+            whole(rate.shape),
             whole((LANES, inner)),
             whole((1, inner)),
         ],
@@ -745,21 +775,21 @@
     logs,
     before,
     scales_ref,
-    local_memory,
+    kept_memory,
+    kept_steps,
     memory,
     total,
     sent,
     received,
     found,
+    returned,
     out_send,
     out_recv,
     back_send,
     back_recv,
-    own_sem,
 ):
     inner, size, column_rows, head_size, count, spatial = geometry
-    slices = count // 2
-    rows, wide = LANES // slices, inner // 2
+    rows, wide = LANES * 4 // count, inner // 4
     pairs = wide // LANES
     frame, place, part = lax.axis_index("frame"), lax.axis_index("spatial"), lax.axis_index("dp")
     me = frame * spatial + place
@@ -777,13 +807,38 @@
     lax.fori_loop(1, count, greet, 0)
     pl.semaphore_wait(barrier, count - 1)
 
+    def place_of(index):
+        return pl.ds(rows * (index // 4), rows), pl.ds(wide * (index % 4), wide)
+
+    def put(ref, way, index, block, extra):
+        scale, factor = code_scale(jnp.max(jnp.abs(block), axis=0, keepdims=True))
+        ref[way, index, :, pl.ds(0, wide)] = encode(block * factor)
+        scale = scale.astype(F32)
+        beside = [scale[:, k * LANES : (k + 1) * LANES] for k in range(pairs)] + extra
+        row = rows_iota((rows, LANES))
+        filled = jnp.zeros((rows, LANES), F32)
+        for k, line in enumerate(beside):
+            filled = jnp.where(row == k, line, filled)
+        ref[way, index, :, pl.ds(wide, LANES)] = filled.astype(BF16)
+
+    def take(ref, way, index):
+        beside = ref[way, index, :, pl.ds(wide, LANES)].astype(F32)
+        scale = jnp.concatenate([beside[k : k + 1] for k in range(pairs)], axis=1)
+        block = decode(ref[way, index, :, pl.ds(0, wide)]) * (scale * (1.0 / CODE_TOP))
+        return block, beside
+
     def send_slices(way, memory_ref, total_ref):
         totals = total_ref[...]
-        shifted = pltpu.roll(totals, LANES - 2 * pairs, 1)
+        parts = []
+        for quarter in range(4):
+            shift = (LANES - 2 * pairs * quarter) % LANES
+            turned = (pltpu.roll(totals, shift, 1) if shift else totals)[0:1]
+            high = turned.astype(BF16).astype(F32)
+            middle = (turned - high).astype(BF16).astype(F32)
+            parts.append([high, middle, turned - high - middle])
         for index in range(count):
-            first, lane = rows * (index // 2), wide * (index % 2)
-            sent[way, index, :, pl.ds(0, wide)] = memory_ref[pl.ds(first, rows), pl.ds(lane, wide)]
-            sent[way, index, :, pl.ds(wide, LANES)] = shifted if index % 2 else totals
+            where_rows, where_lanes = place_of(index)
+            put(sent, way, index, memory_ref[where_rows, where_lanes], parts[index % 4])
 
         def one(k, carry):
             to = (me + k) % count
@@ -800,7 +855,7 @@
         lax.fori_loop(1, count, one, 0)
         received[way, me] = sent[way, me]
 
-    def scan(way, reverse, entering_ref):
+    def scan(way, reverse):
         def arrive(k, carry):
             source = (me + count - k) % count
             pltpu.make_async_remote_copy(
@@ -817,17 +872,18 @@
         entering = jnp.zeros((rows, wide), F32)
         for k in range(count):
             at = count - 1 - k if reverse else k
-            found[way, at] = entering
-            decay = jnp.exp(received[way, at, :, pl.ds(wide, LANES)])
+            put(found, way, at, entering, [])
+            block, beside = take(received, way, at)
+            total_at = beside[pairs : pairs + 1] + beside[pairs + 1 : pairs + 2]
+            decay = jnp.exp(total_at + beside[pairs + 2 : pairs + 3])
             spreads = [spread(decay, pair, head_size) for pair in range(pairs)]
-            decay = jnp.concatenate(spreads, axis=1)
-            entering = entering * decay + received[way, at, :, pl.ds(0, wide)]
+            entering = entering * jnp.concatenate(spreads, axis=1) + block
 
         def one(k, carry):
             to = (me + k) % count
             pltpu.make_async_remote_copy(
                 src_ref=found.at[way, to],
-                dst_ref=place_of(entering_ref, me),
+                dst_ref=returned.at[way, me],
                 send_sem=back_send.at[way, k],
                 recv_sem=back_recv.at[way, k],
                 device_id=device(to),
@@ -836,21 +892,15 @@
             return carry
 
         lax.fori_loop(1, count, one, 0)
-        copy = pltpu.make_async_copy(found.at[way, me], place_of(entering_ref, me), own_sem.at[way])
-        copy.start()
-
-    def place_of(entering_ref, index):
-        first = pl.multiple_of(rows * (index // 2), rows)
-        lane = pl.multiple_of(wide * (index % 2), LANES)
-        return entering_ref.at[pl.ds(first, rows), pl.ds(lane, wide)]
+        returned[way, me] = found[way, me]
 
     def finish_way(way, entering_ref):
         def arrive(k, carry):
             source = (me + count - k) % count
             to = (me + k) % count
             pltpu.make_async_remote_copy(
-                src_ref=found.at[way, source],
-                dst_ref=place_of(entering_ref, source),
+                src_ref=found.at[way, to],
+                dst_ref=returned.at[way, source],
                 send_sem=back_send.at[way, k],
                 recv_sem=back_recv.at[way, k],
                 device_id=device(to),
@@ -867,10 +917,11 @@
             return carry
 
         lax.fori_loop(1, count, arrive, 0)
-        pltpu.make_async_copy(
-            found.at[way, me], place_of(entering_ref, me), own_sem.at[way]
-        ).wait()
-
+        for index in range(count):
+            where_rows, where_lanes = place_of(index)
+            entering_ref[where_rows, where_lanes] = take(returned, way, index)[0]
+
+    rate = widen(rate_ref[...], 1)[1:2]
     send_slices(0, forward_ref, forward_total_ref)
     memory[...] = jnp.zeros_like(memory)
     total[...] = jnp.zeros_like(total)
@@ -892,58 +943,55 @@
 
     def fold_columns(step, carry):
         chunk, _ = chunk_at(step)
+        steps = chunk.steps()
+        kept_memory[step] = memory[...]
+        before[step] = total[...]
+        kept_steps[step] = steps
 
         def keep_values(pair):
             values = chunk.values(pair)
             outputs[step, :, pl.ds(pair * LANES, LANES)] = values
             return values
 
-        fold_chunk(
-            keep_values,
-            chunk.keys(),
-            chunk.steps(),
-            rate_ref[...],
-            chunk.earlier(),
-            head_size,
-            memory,
-            total,
+        logs[step] = fold_chunk(
+            keep_values, chunk.keys(), steps, rate, chunk.earlier(), head_size, memory, total
         )
         return carry
 
     def output_columns(step, carry):
         chunk, queries = chunk_at(step)
-
-        def emit(pair, result, values):
-            outputs[step, :, pl.ds(pair * LANES, LANES)] = result
-
-        def kept_values(pair):
-            return outputs[step, :, pl.ds(pair * LANES, LANES)]
-
-        running, chunk_total = output_chunk(
-            chunk, kept_values, queries, rate_ref[...], local_memory, head_size, emit
-        )
-        logs[step] = before[0:1] + running
-        before[...] = before[...] + chunk_total
+        running_bits = logs[step] * LOG2_E
+        across = jnp.transpose(running_bits)
+        scores = score_matrix(queries, split(jnp.transpose(chunk.keys())), chunk.earlier())
+        steps = kept_steps[step]
+        for pair in range(chunk.pairs):
+            lanes = pl.ds(pair * LANES, LANES)
+            scaled = split(outputs[step, :, lanes] * spread(steps, pair, head_size))
+            outputs[step, :, lanes] = within_pair(
+                pair, scaled, running_bits, across, scores, head_size
+            )
 
         @pl.when(step == 2)
         def _():
-            scan(1, True, entering_backward_ref)
+            scan(1, True)
 
         @pl.when(step == 3)
         def _():
-            scan(0, False, entering_forward_ref)
+            scan(0, False)
 
         return carry
 
     def correct(step, carry):
         _, queries = chunk_at(step)
         arrived = jnp.exp(logs[step])
+        decayed = jnp.exp(before[step][0:1])
         first = pl.multiple_of((chunks - 1 - step) * part_rows, 16)
         here = rows_iota((16, LANES)) == chunks - 1 - step
         for pair in range(inner // LANES):
             lanes = pl.ds(pair * LANES, LANES)
-            added = carried(queries, memory[:, lanes]) * spread(arrived, pair, head_size)
-            result = outputs[step, :, lanes] + added
+            entering = entering_backward_ref[:, lanes] * spread(decayed, pair, head_size)
+            added = carried(queries, kept_memory[step, :, lanes] + entering)
+            result = outputs[step, :, lanes] + added * spread(arrived, pair, head_size)
             scale, factor = code_scale(jnp.max(jnp.abs(result), axis=0, keepdims=True))
             out_ref[:, pl.ds(first, part_rows), lanes] = encode(result * factor).reshape(
                 4, part_rows, LANES
@@ -953,12 +1001,9 @@
 
     lax.fori_loop(0, chunks, fold_columns, 0)
     send_slices(1, memory, total)
-    local_memory[...] = jnp.zeros_like(local_memory)
-    before[...] = jnp.zeros_like(before)
     scales_ref[...] = jnp.zeros_like(scales_ref)
     lax.fori_loop(0, chunks, output_columns, 0)
     finish_way(1, entering_backward_ref)
-    memory[...] = entering_backward_ref[...]
     lax.fori_loop(0, chunks, correct, 0)
     for k in range(4):
         out_ref[k, pl.ds(last, 16), :] = scales_ref[...].astype(BF16)
@@ -968,15 +1013,15 @@
 def column_output(columns, rate, memory, total, inner, size, column_rows, head_size):
     spatial = lax.axis_size("spatial")
     count = lax.axis_size("frame") * spatial
-    rows, wide = LANES * 2 // count, inner // 2
+    slices = (2, count, LANES * 4 // count, inner // 4 + LANES)
     chunks = (columns.shape[1] - 16) * 4 // size
-    vmem, hbm = pl.BlockSpec(memory_space=pltpu.VMEM), pl.BlockSpec(memory_space=pl.ANY)
+    vmem = pl.BlockSpec(memory_space=pltpu.VMEM)
     dma = pltpu.SemaphoreType.DMA
     geometry = (inner, size, column_rows, head_size, count, spatial)
     return pl.pallas_call(
         functools.partial(states_kernel, geometry),
         in_specs=[vmem] * 4,
-        out_specs=[hbm, vmem],
+        out_specs=[vmem, vmem],
         out_shape=[
             jax.ShapeDtypeStruct((LANES, inner), F32),
             jax.ShapeDtypeStruct(columns.shape[:2] + (inner,), BF16),
@@ -985,19 +1030,20 @@
             pltpu.VMEM((LANES, inner), F32),
             pltpu.VMEM((chunks, size, inner), F32),
             pltpu.VMEM((chunks, size, LANES), F32),
-            pltpu.VMEM((8, LANES), F32),
+            pltpu.VMEM((chunks, 8, LANES), F32),
             pltpu.VMEM((16, inner), F32),
-            pltpu.VMEM((LANES, inner), F32),
+            pltpu.VMEM((chunks, LANES, inner), F32),
+            pltpu.VMEM((chunks, size, LANES), F32),
             pltpu.VMEM((LANES, inner), F32),
             pltpu.VMEM((8, LANES), F32),
-            pltpu.VMEM((2, count, rows, wide + LANES), F32),
-            pltpu.VMEM((2, count, rows, wide + LANES), F32),
-            pltpu.VMEM((2, count, rows, wide), F32),
+            pltpu.VMEM(slices, BF16),
+            pltpu.VMEM(slices, BF16),
+            pltpu.VMEM(slices, BF16),
+            pltpu.VMEM(slices, BF16),
             dma((2, count)),
             dma((2, count)),
             dma((2, count)),
             dma((2, count)),
-            dma((2,)),
         ],
         compiler_params=pltpu.CompilerParams(
             collective_id=1, has_side_effects=True, vmem_limit_bytes=VMEM_BYTES
@@ -1054,10 +1100,6 @@
     )(forward, backward, gate, gain)
 
 
-def pad_lanes(source):
-    return jnp.pad(source, ((0, 0), (0, LANES - source.shape[1])))
-
-
 def local(tokens, xz_weight, state_weight, step_weight, step_bias, decay_rate, skip, norm_gain):
     videos, frame_count, row_part, col_total, width = tokens.shape
     flattened = tokens.reshape(-1, width)
@@ -1068,17 +1110,14 @@
     size = column_rows * GROUP
     axes = ("frame", "spatial")
 
-    thrice = pad_lanes(jnp.concatenate([step_weight] * 3, axis=1))
-    bias = pad_lanes(jnp.concatenate([step_bias] * 3)[None])
-    first_weight = jnp.concatenate([state_weight, thrice], axis=1)
-    rates = pad_lanes(decay_rate)
     skips = jnp.repeat(skip[0] + skip[1], head_size)[None]
 
     values, keys, columns, memory, total, gate_weight = project(
         flattened,
-        first_weight,
-        bias,
-        rates[0:1],
+        state_weight,
+        step_weight,
+        step_bias[None],
+        decay_rate,
         xz_weight,
         row_part,
         col_total,
@@ -1087,11 +1126,11 @@
         512,
     )
     entering, backward = column_output(
-        columns, rates[1:2], memory, total, inner, size, column_rows, head_size
+        columns, decay_rate, memory, total, inner, size, column_rows, head_size
     )
     returned = lax.all_to_all(backward, "spatial", 0, 0, tiled=True)
     forward = row_output(
-        values[None], keys[None], rates[0:1], entering, skips, inner, size, head_size
+        values[None], keys[None], decay_rate, entering, skips, inner, size, head_size
     )
     gate_weight, forward = lax.optimization_barrier((gate_weight, forward))
     gate_rows = gate_rows_of(flattened, gate_weight, xz_weight.shape[0])

time: 215 us -> 197 us (0.916)
  Pallas kernels: 200 us -> 188 us
  other arithmetic: 2.53 us -> 0.01 us
    pallas_call x1, Pallas kernels: 59.6 us -> 47.6 us  [column_output(): pl.pallas_call(functools.partial(states_kernel, geometry), in_specs=[vmem...]
  transfers between devices with their start and end apart: 1 -> 1, of which waited for: 0 -> 0; matrix products, arithmetic and copies ran while one was open for 1% -> 1% of each run, Pallas kernels for 17% -> 19%
where the time goes in v7:
time: 197 us
  Pallas kernels  188 us (95%)
  starting transfers between devices  4.91 us (2%)
  local copies, waits for them, and re-layouts  4.43 us (2%)
    pallas_call x1, Pallas kernels, project(): pl.pallas_call(functools.partial(project_kernel, (row_part, col_total, in...  92.4 us
    pallas_call x1, Pallas kernels, column_output(): pl.pallas_call(functools.partial(states_kernel, geometry), in_specs=[vmem...  47.6 us
    pallas_call x1, Pallas kernels, row_output(): pl.pallas_call(functools.partial(output_kernel, head_size), grid=(count,)...  21.7 us
    pallas_call x1, Pallas kernels, gate_rows_of(): pl.pallas_call(functools.partial(gate_kernel, depth), grid=(5,), in_specs...  15.1 us
    pallas_call x1, Pallas kernels, finish(): pl.pallas_call(functools.partial(finish_kernel, head_size, groups, row_pa...  10.8 us
    all_to_all x1, starting transfers between devices, local(): returned = lax.all_to_all(backward, 'spatial', 0, 0, tiled=True)  4.91 us
  transfers between devices with their start and end apart: 1, of which 0 were waited for; matrix products, arithmetic and copies ran while one was open for 1% of the time, Pallas kernels for 19%

profile of v7, /device:TPU:2, one launch (start us, length us, event | category | flops | bytes accessed | tf_op | source)
XLA Modules:
  0.0 197.1 jit_solution(5869341743141537713)
XLA Ops:
  0.0 1.4 copy.9.step_weight_ref
  1.4 92.4 %shard_map.82 = (f32[960,1536]{1,0:T(8,128)}, f32[960,384]{1,0:T(8,128)}, bf16[4,256,1920]{2,1,0:T(8,128)(2,1)}, f32[128,1536]{1,0:T(8,128)}, f32[8,128]{1,0:T(8,128)}, /*index=5*/bf16[4,3072,384]{2,1,0:T(8,128)(2,1)}) custom-call(bf16[960,3072]{1,0:T(8,128)(2,1)} %bitcast.8, bf16[192,256]{1,0:T(8,128)(2,1)} %state_weight_ref.1, ...), custom_call_target="tpu_custom_call" | custom-call | tf_op jit(solution)/shard_map/pallas_call | solution.py:580
  93.9 47.6 %shard_map.83 = (f32[128,1536]{1,0:T(8,128)}, bf16[4,256,1536]{2,1,0:T(8,128)(2,1)}) custom-call(bf16[4,256,1920]{2,1,0:T(8,128)(2,1)} %get-tuple-element.18.columns_ref, f32[2,24]{1,0:T(2,128)} %rate_ref.5, f32[128,1536]{1,0:T(8,128)} %get-tuple-element.19.forward_ref, f32[8,128]{1,0:T(8,128)} %get-tuple-element.20.forward_total_ref), custom_call_target="tpu_custom_call" | custom-call | tf_op jit(solution)/shard_map/pallas_call | solution.py:1021
  141.4 0.0 copy-start.2
  141.4 4.9 %all-to-all-start = ((bf16[4,256,1536]{2,1,0:T(8,128)(2,1)}), bf16[4,256,1536]{2,1,0:T(8,128)(2,1)S(1)}, u32[]{:S(2)}, u32[]{:S(2)}) async-start(bf16[4,256,1536]{2,1,0:T(8,128)(2,1)} %get-tuple-element.23), calls=%async_computation | async-start | bytes 6291456 | tf_op jit(solution)/shard_map/all_to_all | solution.py:1131
  146.3 0.0 copy-done.2
  146.4 0.1 broadcast_in_dim.18
  146.4 0.7 broadcast_in_dim_reshape.3.skip_ref
  147.1 0.0 copy-start.1
  147.1 21.7 %shard_map.84 = f32[1,960,1536]{2,1,0:T(8,128)} custom-call(f32[1,960,1536]{2,1,0:T(8,128)} %bitcast.12, f32[1,960,384]{2,1,0:T(8,128)} %bitcast.13, f32[1,960,384]{2,1,0:T(8,128)} %bitcast.14, f32[1,960,384]{2,1,0:T(8,128)} %bitcast.15, f32[2,24]{1,0:T(2,128)} %rate_ref.5, f32[128,1536]{1,0:T(8,128)} %get-tuple-element.21.entering_ref, ...), custom_call_target="tpu_custom_call" | custom-call | flops 16986931200 | bytes 33554432 | tf_op jit(solution)/shard_map/pallas_call | solution.py:745
  168.8 0.0 copy-done.1
  168.8 0.6 broadcast_in_dim.19.gain_ref
  169.4 15.1 %shard_map.85.gate_ref = f32[960,1536]{1,0:T(8,128)} custom-call(bf16[960,3072]{1,0:T(8,128)(2,1)} %bitcast.9, bf16[4,3072,384]{2,1,0:T(8,128)(2,1)} %get-tuple-element.24.weight_ref), custom_call_target="tpu_custom_call" | custom-call | flops 9059696640 | bytes 20971520 | tf_op jit(solution)/shard_map/pallas_call | solution.py:153
  184.6 0.0 all-to-all-done.backward_ref
  184.6 0.0 copy-start
  184.6 1.6 copy-done
  186.2 10.8 %shard_map.86 = bf16[960,1536]{1,0:T(8,128)(2,1)} custom-call(f32[960,1536]{1,0:T(8,128)} %bitcast.10, bf16[4,256,1536]{2,1,0:T(8,128)(2,1)} %copy-done, f32[960,1536]{1,0:T(8,128)} %shard_map.85.gate_ref, f32[1,1536]{1,0:T(1,128)} %broadcast_in_dim.19.gain_ref), custom_call_target="tpu_custom_call" | custom-call | tf_op jit(solution)/shard_map/pallas_call | solution.py:1092
  (1 shorter events, 0.0 us)
Async XLA Ops:
  141.4 4.9 %copy-start.2 = (f32[2,24]{1,0:T(2,128)S(1)}, f32[2,24]{1,0:T(2,128)}, u32[]{:S(2)}) copy-start(f32[2,24]{1,0:T(2,128)} %param.14) | copy-start | bytes 580
  141.4 43.1 %all-to-all-start = ((bf16[4,256,1536]{2,1,0:T(8,128)(2,1)}), bf16[4,256,1536]{2,1,0:T(8,128)(2,1)S(1)}, u32[]{:S(2)}, u32[]{:S(2)}) async-start(bf16[4,256,1536]{2,1,0:T(8,128)(2,1)} %get-tuple-element.23), calls=%async_computation | async-start | bytes 6291456 | tf_op jit(solution)/shard_map/all_to_all | solution.py:1131
  147.1 21.7 %copy-start.1 = (f32[1536]{0:T(1024)S(1)}, f32[1536]{0:T(1024)}, u32[]{:S(2)}) copy-start(f32[1536]{0:T(1024)} %param.15) | copy-start | bytes 18436
  184.6 1.7 copy-start

commit v8 on v7

--- a/solution.py
+++ b/solution.py
@@ -149,10 +149,10 @@
 def gate_rows_of(tokens, weight, depth):
     total, model = tokens.shape
     inner = 4 * weight.shape[2]
-    tile = total // 5
+    tile = total // 2
     return pl.pallas_call(
         functools.partial(gate_kernel, depth),
-        grid=(5,),
+        grid=(2,),
         in_specs=[pl.BlockSpec((tile, model), lambda m: (m, 0)), whole(weight.shape)],
         out_specs=pl.BlockSpec((tile, inner), lambda m: (m, 0)),
         out_shape=jax.ShapeDtypeStruct((total, inner), F32),
@@ -177,12 +177,15 @@
     memory_ref,
     total_ref,
     gate_ref,
+    kept_ref,
+    before_ref,
     weight,
     gate_weight,
     product,
     middle,
     tokens,
     state_ref,
+    kept,
     own_sem,
     x_send,
     x_recv,
@@ -197,6 +200,7 @@
     gate_send,
     gate_recv,
     gate_out,
+    kept_sem,
 ):
     row_part, col_total, inner, depth, blocks, head_size = geometry
     half = depth // 2
@@ -526,6 +530,8 @@
 
     def fold_rows(step, carry):
         at = pl.ds(pl.multiple_of(step * tile, 16), tile)
+        kept[step] = memory_ref[...]
+        before_ref[step] = total_ref[...]
         block_pairs = blocks[1][1] // LANES
 
         def values(pair):
@@ -544,6 +550,8 @@
         return carry
 
     lax.fori_loop(0, 5, fold_rows, 0)
+    kept_copy = pltpu.make_async_copy(kept, kept_ref, kept_sem.at[0])
+    kept_copy.start()
     gate_end()
     gate_copies = [
         pltpu.make_async_copy(gate_weight.at[quarter], gate_ref.at[quarter], gate_out.at[quarter])
@@ -559,7 +567,7 @@
             arrived(into, move_send.at[block, at], move_recv.at[block, at])
         into = columns_ref.at[place, :, pl.ds(inner if block == 0 else start, width)]
         pltpu.make_async_copy(middle.at[block, place, :, lanes], into, move_own.at[block]).wait()
-    for copy in list(outs.values()) + gate_copies:
+    for copy in list(outs.values()) + gate_copies + [kept_copy]:
         copy.wait()
     for copy in pending:
         copy.wait_send()
@@ -580,7 +588,7 @@
     return pl.pallas_call(
         functools.partial(project_kernel, (row_part, col_total, inner, depth, blocks, head_size)),
         in_specs=[hbm, vmem, vmem, vmem, vmem, hbm],
-        out_specs=[hbm, hbm, hbm, vmem, vmem, hbm],
+        out_specs=[hbm, hbm, hbm, vmem, vmem, hbm, hbm, vmem],
         out_shape=[
             jax.ShapeDtypeStruct((total, inner), F32),
             jax.ShapeDtypeStruct((total, state_width), F32),
@@ -588,6 +596,8 @@
             jax.ShapeDtypeStruct((LANES, inner), F32),
             jax.ShapeDtypeStruct((8, LANES), F32),
             jax.ShapeDtypeStruct((4, tokens.shape[1], inner // 4), BF16),
+            jax.ShapeDtypeStruct((5, LANES, inner), F32),
+            jax.ShapeDtypeStruct((5, 8, LANES), F32),
         ],
         scratch_shapes=[
             pltpu.VMEM((count, tokens.shape[1], width), BF16),
@@ -596,6 +606,7 @@
             pltpu.VMEM((count, 4, piece_rows, width), BF16),
             pltpu.VMEM(tokens.shape, BF16),
             pltpu.VMEM((depth, state_width), BF16),
+            pltpu.VMEM((5, LANES, inner), F32),
             dma((count + 2,)),
             dma((count, 4)),
             dma((count, 4)),
@@ -610,6 +621,7 @@
             dma((14,)),
             dma((14,)),
             dma((4,)),
+            dma((1,)),
         ],
         compiler_params=pltpu.CompilerParams(
             collective_id=0, has_side_effects=True, vmem_limit_bytes=VMEM_BYTES
@@ -678,29 +690,6 @@
     return jnp.where(lanes_iota(halves[0].shape) < head_size, halves[0], halves[1])
 
 
-def output_chunk(chunk, queries, rate, memory_ref, head_size, emit):
-    steps = chunk.steps()
-    keys_t = split(jnp.transpose(chunk.keys()))
-    earlier = chunk.earlier()
-    running, total = running_logs(steps, rate, earlier)
-    running_bits = running * LOG2_E
-    across = jnp.transpose(running_bits)
-    scores = score_matrix(queries, keys_t, earlier)
-    arrived = jnp.exp(running)
-    leaving = jnp.exp(jnp.minimum(total - running, 0.0))
-    decay = jnp.exp(total)
-    for pair in range(chunk.pairs):
-        lanes = pl.ds(pair * LANES, LANES)
-        values = chunk.values(pair)
-        scaled = values * spread(steps, pair, head_size)
-        result = within_pair(pair, split(scaled), running_bits, across, scores, head_size)
-        memory = memory_ref[:, lanes]
-        result = result + carried(queries, memory) * spread(arrived, pair, head_size)
-        emit(pair, result, values)
-        weighted = scaled * spread(leaving, pair, head_size)
-        memory_ref[:, lanes] = advance(memory, keys_t, weighted, spread(decay, pair, head_size))
-
-
 def carried(queries, memory):
     queries_high, queries_low = queries
     memory_high, memory_low = split(memory)
@@ -709,21 +698,35 @@
 
 
 def output_kernel(
-    head_size, values_ref, keys_ref, steps_ref, queries_ref, rate_ref, entering_ref, skip_ref, out_ref, memory_ref
+    head_size,
+    values_ref,
+    keys_ref,
+    steps_ref,
+    queries_ref,
+    kept_ref,
+    before_ref,
+    rate_ref,
+    entering_ref,
+    skip_ref,
+    out_ref,
 ):
     chunk = Chunk(0, values_ref, keys_ref, steps_ref, None)
-
-    @pl.when(pl.program_id(0) == 0)
-    def _():
-        memory_ref[...] = entering_ref[...]
-
-    def emit(pair, result, values):
+    queries = split(chunk.queries(queries_ref))
+    steps, earlier = chunk.steps(), chunk.earlier()
+    running, _ = running_logs(steps, widen(rate_ref[...], 1)[0:1], earlier)
+    running_bits = running * LOG2_E
+    across = jnp.transpose(running_bits)
+    scores = score_matrix(queries, split(jnp.transpose(chunk.keys())), earlier)
+    arrived, decayed = jnp.exp(running), jnp.exp(before_ref[0, 0:1])
+    for pair in range(chunk.pairs):
         lanes = pl.ds(pair * LANES, LANES)
+        values = chunk.values(pair)
+        scaled = split(values * spread(steps, pair, head_size))
+        result = within_pair(pair, scaled, running_bits, across, scores, head_size)
+        memory = kept_ref[0, :, lanes] + entering_ref[:, lanes] * spread(decayed, pair, head_size)
+        result = result + carried(queries, memory) * spread(arrived, pair, head_size)
         result = result + values * skip_ref[:, lanes]
         out_ref[:, :, lanes] = result.reshape(1, chunk.size, LANES)
-
-    queries = split(chunk.queries(queries_ref))
-    output_chunk(chunk, queries, widen(rate_ref[...], 1)[0:1], memory_ref, head_size, emit)
 
 
 def whole(shape):
@@ -736,7 +739,7 @@
     )
 
 
-def row_output(values, keys, rate, entering, skip, inner, size, head_size):
+def row_output(values, keys, kept, before, rate, entering, skip, inner, size, head_size):
     count = values.shape[1] // size
 
     def spec(lane_count, lane_block):
@@ -750,16 +753,17 @@
             spec(LANES, 0),
             spec(LANES, 2),
             spec(LANES, 1),
+            pl.BlockSpec((1, LANES, inner), lambda j: (j, 0, 0)),
+            pl.BlockSpec((1, 8, LANES), lambda j: (j, 0, 0)),
             whole(rate.shape),
             whole((LANES, inner)),
             whole((1, inner)),
         ],
         out_specs=spec(inner, 0),
         out_shape=jax.ShapeDtypeStruct(values.shape, F32),
-        scratch_shapes=[pltpu.VMEM((LANES, inner), F32)],
         cost_estimate=estimate(count * size, inner, 30, 32 << 20),
         compiler_params=params(),
-    )(values, keys, keys, keys, rate, entering, skip)
+    )(values, keys, keys, keys, kept, before, rate, entering, skip)
 
 
 def states_kernel(
@@ -1112,7 +1116,7 @@
 
     skips = jnp.repeat(skip[0] + skip[1], head_size)[None]
 
-    values, keys, columns, memory, total, gate_weight = project(
+    values, keys, columns, memory, total, gate_weight, kept, before = project(
         flattened,
         state_weight,
         step_weight,
@@ -1130,7 +1134,7 @@
     )
     returned = lax.all_to_all(backward, "spatial", 0, 0, tiled=True)
     forward = row_output(
-        values[None], keys[None], decay_rate, entering, skips, inner, size, head_size
+        values[None], keys[None], kept, before, decay_rate, entering, skips, inner, size, head_size
     )
     gate_weight, forward = lax.optimization_barrier((gate_weight, forward))
     gate_rows = gate_rows_of(flattened, gate_weight, xz_weight.shape[0])

time: 197 us -> 195 us (0.990)
  Pallas kernels: 188 us -> 185 us
    pallas_call x1, Pallas kernels: 21.7 us -> 18.7 us  [row_output(): pl.pallas_call(functools.partial(output_kernel, head_size), grid=(count,)...]
  transfers between devices with their start and end apart: 1 -> 1, of which waited for: 0 -> 0; matrix products, arithmetic and copies ran while one was open for 1% -> 1% of each run, Pallas kernels for 19% -> 18%
where the time goes in v8:
time: 195 us
  Pallas kernels  185 us (95%)
  starting transfers between devices  4.9 us (3%)
  local copies, waits for them, and re-layouts  4.44 us (2%)
    pallas_call x1, Pallas kernels, project(): pl.pallas_call(functools.partial(project_kernel, (row_part, col_total, in...  92.5 us
    pallas_call x1, Pallas kernels, column_output(): pl.pallas_call(functools.partial(states_kernel, geometry), in_specs=[vmem...  47.5 us
    pallas_call x1, Pallas kernels, row_output(): pl.pallas_call(functools.partial(output_kernel, head_size), grid=(count,)...  18.7 us
    pallas_call x1, Pallas kernels, gate_rows_of(): pl.pallas_call(functools.partial(gate_kernel, depth), grid=(2,), in_specs...  15.6 us
    pallas_call x1, Pallas kernels, finish(): pl.pallas_call(functools.partial(finish_kernel, head_size, groups, row_pa...  10.8 us
    all_to_all x1, starting transfers between devices, local(): returned = lax.all_to_all(backward, 'spatial', 0, 0, tiled=True)  4.9 us
  transfers between devices with their start and end apart: 1, of which 0 were waited for; matrix products, arithmetic and copies ran while one was open for 1% of the time, Pallas kernels for 18%

profile of v8, /device:TPU:2, one launch (start us, length us, event | category | flops | bytes accessed | tf_op | source)
XLA Modules:
  0.0 194.5 jit_solution(16663016605016779985)
XLA Ops:
  0.0 1.4 copy.9.step_weight_ref
  1.4 92.5 %shard_map.82 = (f32[960,1536]{1,0:T(8,128)}, f32[960,384]{1,0:T(8,128)}, bf16[4,256,1920]{2,1,0:T(8,128)(2,1)}, f32[128,1536]{1,0:T(8,128)}, f32[8,128]{1,0:T(8...) custom-call(bf16[960,3072]{1,0:T(8,128)(2,1)} %bitcast.8, ...), custom_call_target="tpu_custom_call" | custom-call | tf_op jit(solution)/shard_map/pallas_call | solution.py:588
  93.9 47.5 %shard_map.83 = (f32[128,1536]{1,0:T(8,128)}, bf16[4,256,1536]{2,1,0:T(8,128)(2,1)}) custom-call(bf16[4,256,1920]{2,1,0:T(8,128)(2,1)} %get-tuple-element.22.columns_ref, f32[2,24]{1,0:T(2,128)} %rate_ref.5, f32[128,1536]{1,0:T(8,128)} %get-tuple-element.23.forward_ref, f32[8,128]{1,0:T(8,128)} %get-tuple-element.24.forward_total_ref), custom_call_target="tpu_custom_call" | custom-call | tf_op jit(solution)/shard_map/pallas_call | solution.py:1025
  141.4 0.0 copy-start.2
  141.4 4.9 %all-to-all-start = ((bf16[4,256,1536]{2,1,0:T(8,128)(2,1)}), bf16[4,256,1536]{2,1,0:T(8,128)(2,1)S(1)}, u32[]{:S(2)}, u32[]{:S(2)}) async-start(bf16[4,256,1536]{2,1,0:T(8,128)(2,1)} %get-tuple-element.27), calls=%async_computation | async-start | bytes 6291456 | tf_op jit(solution)/shard_map/all_to_all | solution.py:1135
  146.3 0.0 copy-done.2
  146.3 0.1 broadcast_in_dim.18
  146.4 0.7 broadcast_in_dim_reshape.3.skip_ref
  147.1 0.0 copy-start.1
  147.1 18.7 %shard_map.84 = f32[1,960,1536]{2,1,0:T(8,128)} custom-call(f32[1,960,1536]{2,1,0:T(8,128)} %bitcast.12, f32[1,960,384]{2,1,0:T(8,128)} %bitcast.13, f32[1,960,384]{2,1,0:T(8,128)} %bitcast.14, f32[1,960,384]{2,1,0:T(8,128)} %bitcast.15, f32[5,128,1536]{2,1,0:T(8,128)} %get-tuple-element.20.kept_ref, f32[5,8,128]{2,1,0:T(8,128)} %get-tuple-element.21.before_ref, ...), custom_call_target="tpu_custom_call" | custom-call | flops 16986931200 | bytes 33554432 | tf_op jit(solution)/shard_map/pallas_call | solution.py:748
  165.8 0.0 copy-done.1
  165.8 0.6 broadcast_in_dim.19.gain_ref
  166.4 15.6 %shard_map.85.gate_ref = f32[960,1536]{1,0:T(8,128)} custom-call(bf16[960,3072]{1,0:T(8,128)(2,1)} %bitcast.9, bf16[4,3072,384]{2,1,0:T(8,128)(2,1)} %get-tuple-element.28.weight_ref), custom_call_target="tpu_custom_call" | custom-call | flops 9059696640 | bytes 20971520 | tf_op jit(solution)/shard_map/pallas_call | solution.py:153
  182.0 0.0 all-to-all-done.backward_ref
  182.0 0.0 copy-start
  182.0 1.6 copy-done
  183.7 10.8 %shard_map.86 = bf16[960,1536]{1,0:T(8,128)(2,1)} custom-call(f32[960,1536]{1,0:T(8,128)} %bitcast.10, bf16[4,256,1536]{2,1,0:T(8,128)(2,1)} %copy-done, f32[960,1536]{1,0:T(8,128)} %shard_map.85.gate_ref, f32[1,1536]{1,0:T(1,128)} %broadcast_in_dim.19.gain_ref), custom_call_target="tpu_custom_call" | custom-call | tf_op jit(solution)/shard_map/pallas_call | solution.py:1096
  (1 shorter events, 0.0 us)
Async XLA Ops:
  141.4 4.9 %copy-start.2 = (f32[2,24]{1,0:T(2,128)S(1)}, f32[2,24]{1,0:T(2,128)}, u32[]{:S(2)}) copy-start(f32[2,24]{1,0:T(2,128)} %param.14) | copy-start | bytes 580
  141.4 40.6 %all-to-all-start = ((bf16[4,256,1536]{2,1,0:T(8,128)(2,1)}), bf16[4,256,1536]{2,1,0:T(8,128)(2,1)S(1)}, u32[]{:S(2)}, u32[]{:S(2)}) async-start(bf16[4,256,1536]{2,1,0:T(8,128)(2,1)} %get-tuple-element.27), calls=%async_computation | async-start | bytes 6291456 | tf_op jit(solution)/shard_map/all_to_all | solution.py:1135
  147.1 18.7 %copy-start.1 = (f32[1536]{0:T(1024)S(1)}, f32[1536]{0:T(1024)}, u32[]{:S(2)}) copy-start(f32[1536]{0:T(1024)} %param.15) | copy-start | bytes 18436
  182.0 1.7 copy-start
